TPU v7x, 32 devices: a whole 2x2x4 slice. The times are simulated.
32 devices in a mesh: row: 8 (over y, x, core), col: 4 (over z).
Axes of the slice: x: 2, y: 2, z: 4, core: 2. Of those that a mesh axis runs over, the one named last changes fastest.
Arguments:
- tile_blocks: bfloat16 [768, 128, 128], P(('row', 'col')), may hold values from -0.21875 to 0.21875
- tile_rows: int32 [768], P(('row', 'col')), may hold values from 0 to 255, as said below
- tile_cols: int32 [768], P(('row', 'col')), may hold values from 0 to 255, as said below
- trial_vectors: bfloat16 [4, 32768], P(None, ('col', 'row')), may hold values from -6 to 6
- basis_old: float32 [44, 32768], P(None, ('col', 'row'))
- image_old: float32 [44, 32768], P(None, ('col', 'row'))
Outputs:
- projected: float32 [48, 48], replicated
- basis_new: float32 [48, 32768], P(None, ('col', 'row'))
- image_new: float32 [48, 32768], P(None, ('col', 'row'))
Inputs may be any that keep to these rules, and one draw needn't show every extreme that they name: `tile_rows`: the 24 tiles of each device with index r on row have block rows b for which (b // 8) % 8 equals r. `tile_cols`: the 24 tiles of each device with index c on col have block columns from c * 64 to (c + 1) * 64 - 1.
All inputs are finite; a program needn't handle non-finite values.
Results may differ from a plain program's by a relative error of at most 0.0003.
Values may be sent and summed in bfloat16 or wider, within the bound.
No kernel may reach another device: no remote copies, remote signals or barrier semaphores. Data moves between devices by JAX's collectives and lax.ppermute only.
A program may use at most 64 MiB of HBM per device.

v0:
```python
import jax
import jax.numpy as jnp
from jax import lax
from jax.sharding import PartitionSpec as P


def rows_product(left, right):
    return lax.dot_general(left, right, (((1,), (1,)), ((), ())), precision=lax.Precision.HIGHEST)


def place_blocks(local_index, block_count, products):
    onehot = (local_index[None, :] == jnp.arange(block_count, dtype=jnp.int32)[:, None]).astype(
        jnp.float32
    )
    flat = products.reshape(products.shape[0], -1)
    placed = jnp.dot(onehot, flat, precision=lax.Precision.HIGHEST)
    return placed.reshape(block_count, products.shape[1], products.shape[2])


def local(tile_blocks, tile_rows, tile_cols, trial_vectors, basis_old, image_old):
    tile_size = tile_blocks.shape[1]
    piece_width = trial_vectors.shape[1]
    vec_count = trial_vectors.shape[0]
    blocks_dev = piece_width // tile_size
    n_row = lax.axis_size("row")
    n_col = lax.axis_size("col")
    row_blocks = blocks_dev * n_col
    col_blocks = blocks_dev * n_row
    col_index = lax.axis_index("col")
    all_rows = float(piece_width * n_row * n_col)
    col_vectors = lax.all_gather(trial_vectors, "row", axis=1, tiled=True)
    row_vectors = lax.all_gather(trial_vectors, "col", axis=1, tiled=True)
    local_rows = tile_rows // blocks_dev // n_row * blocks_dev + tile_rows % blocks_dev
    local_cols = tile_cols - col_index * col_blocks
    picked_cols = jnp.take(
        col_vectors.reshape(vec_count, col_blocks, tile_size), local_cols, axis=1
    )
    forward = jnp.einsum(
        "ktb,tab->tka", picked_cols, tile_blocks, preferred_element_type=jnp.float32
    )
    picked_rows = jnp.take(
        row_vectors.reshape(vec_count, row_blocks, tile_size), local_rows, axis=1
    )
    backward = jnp.einsum(
        "kta,tab->tkb", picked_rows, tile_blocks, preferred_element_type=jnp.float32
    )
    row_partial = place_blocks(local_rows, row_blocks, forward)
    col_partial = place_blocks(local_cols, col_blocks, backward)
    col_share = lax.psum_scatter(col_partial, "row", scatter_dimension=0, tiled=True)
    row_total = lax.psum(row_partial, "col")
    own_rows = lax.dynamic_slice_in_dim(row_total, col_index * blocks_dev, blocks_dev, 0)
    new_image = (own_rows + col_share).transpose(1, 0, 2).reshape(vec_count, piece_width)
    trial_wide = trial_vectors.astype(jnp.float32)
    basis_all = jnp.concatenate([basis_old, trial_wide], axis=0)
    images_all = jnp.concatenate([image_old, new_image], axis=0)
    correlation, coupling = lax.psum(
        (rows_product(basis_all, basis_all), rows_product(basis_all, images_all)), ("row", "col")
    )
    correlation = correlation / all_rows
    coupling = coupling / all_rows
    factor = jnp.linalg.cholesky(correlation)

    def solve_lower(matrix):
        return lax.linalg.triangular_solve(factor, matrix, left_side=True, lower=True)

    half_done = solve_lower(coupling)
    projected = solve_lower(half_done.T).T
    return (projected, solve_lower(basis_all), solve_lower(images_all))


def solution(mesh):
    in_specs = (
        P(("row", "col"), None, None),
        P(("row", "col")),
        P(("row", "col")),
        P(None, ("col", "row")),
        P(None, ("col", "row")),
        P(None, ("col", "row")),
    )
    out_specs = (P(), P(None, ("col", "row")), P(None, ("col", "row")))
    return jax.shard_map(local, mesh=mesh, in_specs=in_specs, out_specs=out_specs, check_vma=False)
```

profile of v0, /device:TPU:0, one launch (start us, length us, event | category | flops | bytes accessed | tf_op | source)
XLA Modules:
  0.0 132.5 jit_solution(612166987977802005)
XLA Ops:
  8.1 0.7 copy-done.4
  8.8 0.6 copy-done.5
  9.5 10.7 %all_gather.6 = bf16[4,8192]{1,0:T(4,128)(2,1)S(1)} all-gather(bf16[4,1024]{1,0:T(4,128)(2,1)S(1)} %copy-done.3), channel_id=1, replica_groups=mesh['row'=8,'col'=4] {'row'}, dimensions={1}, use_global_device_ids=true | all-gather | bytes 73728 | tf_op jit(solution)/shard_map/all_gather | solution.py:31
  20.2 0.6 gather_fusion
  20.8 0.5 fusion.13
  21.3 0.9 fusion.7
  22.3 13.4 %all_gather.7 = bf16[4,4096]{1,0:T(4,128)(2,1)S(1)} all-gather(bf16[4,1024]{1,0:T(4,128)(2,1)S(1)} %copy-done.3), channel_id=1, replica_groups=mesh['row'=8,'col'=4] {'col'}, dimensions={1}, use_global_device_ids=true | all-gather | bytes 40960 | tf_op jit(solution)/shard_map/all_gather | solution.py:32
  35.7 0.6 gather_fusion.1
  36.3 0.4 fusion.11
  36.7 1.0 fusion.4
  37.7 0.3 fusion.3
  38.0 18.7 %all-reduce.3.cloned.1.call-done = f32[32,4,128]{2,0,1:T(8,128)} async-done(((f32[32,4,128]{2,0,1:T(8,128)}), f32[32,4,128]{2,0,1:T(8,128)}) %all-reduce.3.cloned.1.call-update) | async-done | bytes 65552 | tf_op jit(solution)/shard_map/psum | solution.py:50
  56.8 14.5 %reduce-scatter.2.cloned.1.call-done = f32[8,4,128]{2,0,1:T(8,128)} async-done(((f32[64,4,128]{2,0,1:T(8,128)}), f32[8,4,128]{2,0,1:T(8,128)}) %reduce-scatter.2.cloned.1.call-update) | async-done | bytes 16400 | tf_op jit(solution)/shard_map/reduce_scatter | solution.py:49
  71.2 0.7 add_bitcast_fusion
  72.0 0.3 fusion.1
  72.3 40.0 %all-reduce = (f32[48,48]{0,1:T(8,128)S(1)}, f32[48,48]{0,1:T(8,128)S(1)}) all-reduce(f32[48,48]{0,1:T(8,128)S(1)} %fusion.3, f32[48,48]{0,1:T(8,128)S(1)} %fusion.1), channel_id=1, replica_groups=mesh['row'=8,'col'=4] {'row','col'}, use_global_device_ids=true, to_apply=%region_0.1 | all-reduce | flops 4608 | bytes 36864 | tf_op jit(solution)/shard_map/psum | solution.py:56
  112.4 4.4 %cholesky.18 = f32[48,48]{1,0:T(8,128)S(1)} custom-call(f32[48,48]{1,0:T(8,128)S(1)} %fusion.19), custom_call_target="Cholesky" | custom-call | tf_op jit(solution)/shard_map/jit(cholesky)/cholesky | solution.py:61
  116.8 0.6 compare_reduce_fusion
  117.5 0.7 fusion.10
  118.1 3.7 %custom-call.12 = f32[1,48,48]{1,2,0:T(8,128)S(1)} custom-call(f32[1,48,48]{2,1,0:T(8,128)S(1)} %fusion.10), custom_call_target="InvertDiagBlocksLowerTriangular" | custom-call | tf_op jit(solution)/shard_map/triangular_solve/custom-call.0 | solution.py:64
  121.8 1.1 fusion.2
  122.8 1.0 fusion
  124.1 0.2 convolution_bitcast_fusion
  124.3 0.7 copy.16
  (27 shorter events, 0.5 us)
Async XLA Ops:
  8.0 12.8 %copy-start = (bf16[24,128,128]{2,1,0:T(8,128)(2,1)S(1)}, bf16[24,128,128]{2,1,0:T(8,128)(2,1)}, u32[]{:S(2)}) copy-start(bf16[24,128,128]{2,1,0:T(8,128)(2,1)} %param.10) | copy-start | bytes 2359300
  8.0 48.8 %all-reduce.3.cloned.1.call-start = ((), (), s32[]{:S(2)}) async-start(), calls=%async_computation.1 | async-start | bytes 131072 | tf_op jit(solution)/shard_map/psum | solution.py:50
  8.1 0.7 copy-start.4
  8.1 1.4 %copy-start.3 = (bf16[4,1024]{1,0:T(4,128)(2,1)S(1)}, bf16[4,1024]{1,0:T(4,128)(2,1)}, u32[]{:S(2)}) copy-start(bf16[4,1024]{1,0:T(4,128)(2,1)} %param.13) | copy-start | bytes 24580
  8.8 0.7 copy-start.5
  22.3 49.0 %reduce-scatter.2.cloned.1.call-start = ((), (), s32[]{:S(2)}) async-start(), calls=%async_computation.2 | async-start | bytes 147456 | tf_op jit(solution)/shard_map/reduce_scatter | solution.py:49
  36.7 1.1 copy-start.1
  37.7 34.3 %copy-start.2 = (f32[44,1024]{1,0:T(8,128)S(1)}, f32[44,1024]{1,0:T(8,128)}, u32[]{:S(2)}) copy-start(f32[44,1024]{1,0:T(8,128)} %param.15) | copy-start | bytes 540676
Sparse Core Ops, SparseCore 0:
  22.4 34.3 all-reduce.2
Sparse Core Ops, SparseCore 1:
  37.8 33.4 reduce-scatter.1
where the time goes:
time: 133 us; the launch traced here: 132 us
  blocking collectives  64 us (48%)
  waiting for transfers between devices  33.2 us (25%)
  between operations  15.7 us (12%)
  other arithmetic  10.2 us (8%)
  matrix products  5.97 us (4%)
  local copies, waits for them, and re-layouts  3.32 us (2%)
    psum x1, blocking collectives, local(): lax.psum((rows_product(basis_all, basis_all), rows_product(basis_all, ima...  40 us
    psum x1, waiting for transfers between devices, local(): row_total = lax.psum(row_partial, 'col')  18.7 us
    reduce_scatter x1, waiting for transfers between devices, local(): lax.psum_scatter(col_partial, 'row', scatter_dimension=0, tiled=True)  14.5 us
    all_gather x1, blocking collectives, local(): row_vectors = lax.all_gather(trial_vectors, 'col', axis=1, tiled=True)  13.4 us
    all_gather x1, blocking collectives, local(): col_vectors = lax.all_gather(trial_vectors, 'row', axis=1, tiled=True)  10.7 us
    another operation x3, other arithmetic, local(): factor = jnp.linalg.cholesky(correlation)  5.05 us
    another operation x2, other arithmetic, solve_lower(): lax.linalg.triangular_solve(factor, matrix, left_side=True, lower=True)  4.32 us
  transfers between devices with their start and end apart: 2, of which 2 were waited for; matrix products, arithmetic and copies ran while one was open for 2% of the time, Pallas kernels for 0%

commit v1 on v0

v1 whole, which is shorter than its diff:
```python
import functools

import jax
import jax.numpy as jnp
from jax import lax
from jax.experimental import pallas as pl
from jax.experimental.pallas import tpu as pltpu
from jax.sharding import PartitionSpec as P

HIGHEST = lax.Precision.HIGHEST
LANES = 128
VMEM_LIMIT = 32 * 1024 * 1024


def contract_last(left, right):
    return lax.dot_general(
        left,
        right,
        (((1,), (1,)), ((), ())),
        precision=HIGHEST,
        preferred_element_type=jnp.float32,
    )


def multiply(left, right):
    return jnp.dot(left, right, precision=HIGHEST, preferred_element_type=jnp.float32)


def side_by_side(blocks_ref):
    return jnp.concatenate([blocks_ref[b] for b in range(blocks_ref.shape[0])], axis=1)


def gram_kernel(scale, trial_ref, basis_ref, image_ref, wide_ref, gram_ref):
    trial = trial_ref[...].astype(jnp.float32)
    for b in range(wide_ref.shape[0]):
        wide_ref[b] = trial[:, b * LANES : (b + 1) * LANES]
    basis_all = jnp.concatenate([basis_ref[...], trial], axis=0)
    correlation = contract_last(basis_all, basis_all)
    coupling = contract_last(basis_all, image_ref[...])
    count = correlation.shape[0]
    unused = jnp.zeros((count, LANES - count - coupling.shape[1]), jnp.float32)
    gram = jnp.concatenate([correlation, coupling, unused], axis=1) * scale
    vecs = gram_ref.shape[1]
    for i in range(gram_ref.shape[0]):
        gram_ref[i] = gram[i * vecs : (i + 1) * vecs]


def tiles_kernel(index_ref, tiles_ref, col_vecs_ref, row_vecs_ref, row_sums_ref, col_sums_ref):
    row_sums_ref[...] = jnp.zeros_like(row_sums_ref)
    col_sums_ref[...] = jnp.zeros_like(col_sums_ref)
    for t in range(tiles_ref.shape[0]):
        tile = tiles_ref[t]
        by_cols = col_vecs_ref[index_ref[0, t]].astype(jnp.bfloat16)
        by_rows = row_vecs_ref[index_ref[1, t]].astype(jnp.bfloat16)
        forward = lax.dot_general(
            by_cols, tile, (((1,), (1,)), ((), ())), preferred_element_type=jnp.float32
        )
        backward = jnp.dot(by_rows, tile, preferred_element_type=jnp.float32)
        to_row, to_col = index_ref[2, t], index_ref[3, t]
        row_sums_ref[to_row] = row_sums_ref[to_row] + forward
        col_sums_ref[to_col] = col_sums_ref[to_col] + backward


def factor_kernel(count, gram_ref, inverse_ref, start_ref):
    gram = jnp.concatenate([gram_ref[i] for i in range(gram_ref.shape[0])], axis=0)
    row_id = lax.broadcasted_iota(jnp.int32, (count, LANES), 0)
    lane_id = lax.broadcasted_iota(jnp.int32, (count, LANES), 1)
    identity = jnp.where(lane_id == row_id + count, 1.0, 0.0)
    work = jnp.where(lane_id < count, gram, identity)
    diagonal = jnp.ones((count, 1), jnp.float32)
    for j in range(count):
        pivot_row = work[j : j + 1, :]
        pivot = work[j : j + 1, j : j + 1]
        column = work[:, j : j + 1]
        below = row_id[:, :1] > j
        ratio = jnp.where(below, column / pivot, 0.0)
        diagonal = jnp.where(row_id[:, :1] == j, pivot, diagonal)
        work = work - ratio * pivot_row
    inverse = work[:, count : 2 * count] * lax.rsqrt(diagonal)
    old = count - gram_ref.shape[1]
    coupling = gram[:, count : count + old]
    inverse_ref[...] = inverse
    start_ref[...] = contract_last(multiply(inverse, coupling), inverse[:, :old])


def image_kernel(
    scale, inverse_ref, wide_ref, basis_ref, image_ref, rows_ref, cols_ref, basis_new_ref, image_new_ref, part_ref
):
    inverse = inverse_ref[...]
    basis_new = multiply(inverse, jnp.concatenate([basis_ref[...], side_by_side(wide_ref)], axis=0))
    basis_new_ref[...] = basis_new
    summed = [rows_ref[b] + cols_ref[b] for b in range(rows_ref.shape[0])]
    image = jnp.concatenate(summed, axis=1)
    vecs, count = image.shape[0], inverse.shape[0]
    part = contract_last(image, basis_new) * scale
    part = jnp.concatenate([part, jnp.zeros((vecs, LANES - count), jnp.float32)], axis=1)
    part_ref[...] = jnp.broadcast_to(part[None], part_ref.shape)
    image_new_ref[...] = multiply(inverse, jnp.concatenate([image_ref[...], image], axis=0))


def project_kernel(inverse_ref, start_ref, parts_ref, projected_ref):
    total = jnp.sum(parts_ref[...], axis=0)
    vecs = total.shape[0]
    count = inverse_ref.shape[0]
    last = inverse_ref[...][:, count - vecs :]
    new = lax.dot_general(
        total[:, :count],
        last,
        (((0,), (1,)), ((), ())),
        precision=HIGHEST,
        preferred_element_type=jnp.float32,
    )
    projected_ref[...] = start_ref[...] + new


def call(kernel, outs, *args, smem=(), flops=0):
    in_specs = [
        pl.BlockSpec(memory_space=pltpu.SMEM if i in smem else pltpu.VMEM) for i in range(len(args))
    ]
    many = isinstance(outs, (list, tuple))
    return pl.pallas_call(
        kernel,
        out_shape=[jax.ShapeDtypeStruct(o, jnp.float32) for o in outs],
        in_specs=in_specs,
        out_specs=[pl.BlockSpec(memory_space=pltpu.VMEM)] * len(outs),
        compiler_params=pltpu.CompilerParams(vmem_limit_bytes=VMEM_LIMIT),
        cost_estimate=pl.CostEstimate(flops=flops, bytes_accessed=0, transcendentals=0),
    )(*args)


def bits_of(size):
    return [1 << j for j in range(size.bit_length() - 1)]


def swap(array, axis, mask):
    size = lax.axis_size(axis)
    return lax.ppermute(array, axis, [(i, i ^ mask) for i in range(size)])


def place(apart, bits):
    return sum(((apart // m) % 2) * (1 << j) for j, m in enumerate(bits))


def local(tile_blocks, tile_rows, tile_cols, trial_vectors, basis_old, image_old):
    tile_size = tile_blocks.shape[1]
    vecs, width = trial_vectors.shape
    old = basis_old.shape[0]
    count = old + vecs
    blocks = width // tile_size
    n_row, n_col = lax.axis_size("row"), lax.axis_size("col")
    row, col = lax.axis_index("row"), lax.axis_index("col")
    scale = 1.0 / float(width * n_row * n_col)
    row_bits, col_bits = bits_of(n_row), bits_of(n_col)

    gather_row = row_bits[1:] + row_bits[:1]
    gather_col = col_bits
    scatter_row = row_bits
    scatter_col = col_bits
    row_piece = tile_rows // blocks // n_row
    row_inner = tile_rows % blocks
    local_col = tile_cols - col * (blocks * n_row)
    col_piece, col_inner = local_col // blocks, local_col % blocks
    row_apart = row_piece ^ col
    col_apart = col_piece ^ row
    index = jnp.stack(
        [
            place(col_apart, gather_row) * blocks + col_inner,
            place(row_apart, gather_col) * blocks + row_inner,
            place(row_apart, scatter_col[::-1]) * blocks + row_inner,
            place(col_apart, scatter_row[::-1]) * blocks + col_inner,
        ]
    )

    wide, gram = call(
        functools.partial(gram_kernel, scale),
        [(blocks, vecs, tile_size), (count // vecs, vecs, LANES)],
        trial_vectors,
        basis_old,
        image_old,
    )
    col_vecs = wide
    for m in gather_row:
        col_vecs = jnp.concatenate([col_vecs, swap(col_vecs, "row", m)], axis=0)
    row_vecs = wide
    for m in gather_col:
        size = row_vecs.shape[0]
        got = swap(jnp.concatenate([row_vecs, gram], axis=0), "col", m)
        row_vecs = jnp.concatenate([row_vecs, got[:size]], axis=0)
        gram = gram + got[size:]

    row_sums, col_sums = call(
        tiles_kernel,
        [(blocks * n_col, vecs, tile_size), (blocks * n_row, vecs, tile_size)],
        index,
        tile_blocks,
        col_vecs,
        row_vecs,
        smem=(0,),
    )
    for m in scatter_row:
        half = col_sums.shape[0] // 2
        got = swap(jnp.concatenate([col_sums[half:], gram], axis=0), "row", m)
        col_sums = col_sums[:half] + got[:half]
        gram = gram + got[half:]
    for m in scatter_col:
        half = row_sums.shape[0] // 2
        row_sums = row_sums[:half] + swap(row_sums[half:], "col", m)

    inverse, start = call(
        functools.partial(factor_kernel, count), [(count, count), (count, count)], gram
    )
    basis_new, image_new, part = call(
        functools.partial(image_kernel, scale),
        [(count, width), (count, width), (n_row * n_col, vecs, LANES)],
        inverse,
        wide,
        basis_old,
        image_old,
        row_sums,
        col_sums,
    )
    parts = lax.all_to_all(part, ("row", "col"), split_axis=0, concat_axis=0, tiled=True)
    (projected,) = call(project_kernel, [(count, count)], inverse, start, parts)
    return projected, basis_new, image_new


def solution(mesh):
    in_specs = (
        P(("row", "col"), None, None),
        P(("row", "col")),
        P(("row", "col")),
        P(None, ("col", "row")),
        P(None, ("col", "row")),
        P(None, ("col", "row")),
    )
    out_specs = (P(), P(None, ("col", "row")), P(None, ("col", "row")))
    return jax.shard_map(local, mesh=mesh, in_specs=in_specs, out_specs=out_specs, check_vma=False)
```

time: 133 us -> 48.5 us (0.36)
  blocking collectives: 64 us -> 10.4 us
  waiting for transfers between devices: 33.2 us -> 10.7 us
  between operations: 15.7 us -> 0.86 us
  starting transfers between devices: 0.08 us -> 12.7 us
  Pallas kernels: 0 us -> 8.61 us
  other arithmetic: 10.2 us -> 2.32 us
  matrix products: 5.97 us -> 0 us
    psum x1 -> x0, blocking collectives: 40 us -> none  [local(): lax.psum((rows_product(basis_all, basis_all), rows_product(basis_all, ima...]
    all_gather x2 -> x0, blocking collectives: 24 us -> none  [the longest x1 13.4 us: local(): row_vectors = lax.all_gather(trial_vectors, 'col', axis=1, tiled=True)]
    psum x1 -> x0, waiting for transfers between devices: 18.7 us -> none  [local(): row_total = lax.psum(row_partial, 'col')]
    reduce_scatter x1 -> x0, waiting for transfers between devices: 14.5 us -> none  [local(): lax.psum_scatter(col_partial, 'row', scatter_dimension=0, tiled=True)]
    ppermute x0 -> x10, starting transfers between devices: none -> 12.7 us  [swap(): return lax.ppermute(array, axis, [(i, i ^ mask) for i in range(size)])]
    ppermute x0 -> x10, waiting for transfers between devices: none -> 10.7 us  [swap(): return lax.ppermute(array, axis, [(i, i ^ mask) for i in range(size)])]
    all_to_all x0 -> x1, blocking collectives: none -> 10.4 us  [local(): lax.all_to_all(part, ('row', 'col'), split_axis=0, concat_axis=0, tiled=T...]
    pallas_call x0 -> x5, Pallas kernels: none -> 8.61 us  [call(): pl.pallas_call(kernel, out_shape=[jax.ShapeDtypeStruct(o, jnp.float32) fo...]
  transfers between devices with their start and end apart: 2 -> 10, of which waited for: 2 -> 6; matrix products, arithmetic and copies ran while one was open for 2% -> 5% of each run, Pallas kernels for 0% -> 0%
where the time goes in v1:
time: 48.5 us; the launch traced here: 48.3 us
  starting transfers between devices  12.7 us (26%)
  waiting for transfers between devices  10.7 us (22%)
  blocking collectives  10.4 us (21%)
  Pallas kernels  8.61 us (18%)
  local copies, waits for them, and re-layouts  2.6 us (5%)
  other arithmetic  2.32 us (5%)
  between operations  0.86 us (2%)
    ppermute x10, starting transfers between devices, swap(): return lax.ppermute(array, axis, [(i, i ^ mask) for i in range(size)])  12.7 us
    ppermute x10, waiting for transfers between devices, swap(): return lax.ppermute(array, axis, [(i, i ^ mask) for i in range(size)])  10.7 us
    all_to_all x1, blocking collectives, local(): lax.all_to_all(part, ('row', 'col'), split_axis=0, concat_axis=0, tiled=T...  10.4 us
    pallas_call x5, Pallas kernels, call(): pl.pallas_call(kernel, out_shape=[jax.ShapeDtypeStruct(o, jnp.float32) fo...  8.61 us
    unnamed x12, local copies, waits for them, and re-layouts  2.56 us
    another operation x4, other arithmetic, local(): jnp.stack([place(col_apart, gather_row) * blocks + col_inner, place(row_a...  1.4 us
  transfers between devices with their start and end apart: 10, of which 6 were waited for; matrix products, arithmetic and copies ran while one was open for 5% of the time, Pallas kernels for 0%

profile of v1, /device:TPU:0, one launch (start us, length us, event | category | flops | bytes accessed | tf_op | source)
XLA Modules:
  0.0 48.3 jit_solution(16161761166485547878)
XLA Ops:
  0.6 0.9 %copy-done = f32[44,1024]{1,0:T(8,128)S(1)} copy-done((f32[44,1024]{1,0:T(8,128)S(1)}, f32[44,1024]{1,0:T(8,128)}, u32[]{:S(2)}) %copy-start) | copy-done | bytes 180248
  1.6 0.9 %copy-done.2 = f32[44,1024]{1,0:T(8,128)S(1)} copy-done((f32[44,1024]{1,0:T(8,128)S(1)}, f32[44,1024]{1,0:T(8,128)}, u32[]{:S(2)}) %copy-start.2) | copy-done | bytes 180248
  2.5 0.7 %copy-done.5 = bf16[4,1024]{1,0:T(4,128)(2,1)S(1)} copy-done((bf16[4,1024]{1,0:T(4,128)(2,1)S(1)}, bf16[4,1024]{1,0:T(4,128)(2,1)}, u32[]{:S(2)}) %copy-start.5) | copy-done | bytes 8216
  3.7 3.0 %collective-permute-start.2 = (f32[8,4,128]{2,1,0:T(4,128)S(1)}, f32[8,4,128]{2,1,0:T(4,128)S(1)}, u32[]{:S(2)}, u32[]{:S(2)}) collective-permute-start(f32[8,4,128]{2,1,0:T(4,128)S(1)} %get-tuple-element.13.wide_ref), channel_id=1, source_target_pairs={{0,8},{4,12},{8,0},{12,4},{16,24},{20,28},{24,16},{28,20},{1,9},{5... | collective-permute-start | bytes 49160 | tf_op jit(solution)/shard_map/ppermute | solution.py:137
  6.7 1.6 %collective-permute-start = (f32[20,4,128]{2,1,0:T(4,128)S(1)}, f32[20,4,128]{2,1,0:T(4,128)S(1)}, u32[]{:S(2)}, u32[]{:S(2)}) collective-permute-start(f32[20,4,128]{2,1,0:T(4,128)S(1)} %pad_maximum_fusion.6), channel_id=1, source_target_pairs={{0,1},{1,0},{2,3},{3,2},{4,5},{5,4},{6,7},{7,6},{8,9},{9,8},{10,11... | collective-permute-start | bytes 122888 | tf_op jit(solution)/shard_map/ppermute | solution.py:137
  8.4 0.7 %add_bitcast_fusion.2 = (s32[1,24]{1,0:T(1,128)S(1)}, s32[24]{0:T(128)S(1)}, s32[24]{0:T(128)S(1)}) fusion(s32[24]{0:T(128)} %param.7, s32[]{:T(128)S(6)} %axis_index.22), kind=kLoop, calls=%fused_computation.64 | loop fusion | flops 1656 | bytes 388 | tf_op jit(solution)/shard_map/stack | solution.py:165
  9.1 0.7 %fusion.7 = (s32[24]{0:T(128)S(1)}, s32[24]{0:T(128)S(1)}) fusion(s32[]{:T(128)S(6)} %axis_index.25, s32[24]{0:T(128)} %param.8, s32[]{:T(128)S(6)} %mul.31), kind=kLoop, calls=%fused_computation.67 | loop fusion | flops 408 | bytes 296 | tf_op jit(solution)/shard_map/xor | solution.py:164
  9.8 0.7 %add_bitcast_fusion = (s32[1,24]{1,0:T(1,128)S(1)}, s32[1,24]{1,0:T(1,128)S(1)}) fusion(s32[24]{0:T(128)S(1)} %get-tuple-element.24, s32[24]{0:T(128)S(1)} %get-tuple-element.23, s32[24]{0:T(128)S(1)} %get-tuple-element.22, s32[24]{0:T(128)S(1)} %get-tuple-element.29, s32[24]{0:T(128)} %param.7, s32[24]{0:T(128)S(1)} %get-tuple-element.26, ...), kind=kLoop, calls=%fused_computation.62 | loop fusion | flops 720 | bytes 864 | tf_op jit(solution)/shard_map/stack | solution.py:165
  10.5 1.6 %collective-permute-start.3 = (f32[16,4,128]{2,1,0:T(4,128)S(1)}, f32[16,4,128]{2,1,0:T(4,128)S(1)}, u32[]{:S(2)}, u32[]{:S(2)}) collective-permute-start(f32[16,4,128]{2,1,0:T(4,128)S(1)} %pad_maximum_fusion.8), channel_id=1, source_target_pairs={{0,16},{4,20},{8,24},{12,28},{16,0},{20,4},{24,8},{28,12},{1,17},{... | collective-permute-start | bytes 98312 | tf_op jit(solution)/shard_map/ppermute | solution.py:137
  12.1 2.7 %collective-permute-start.1 = (f32[28,4,128]{2,1,0:T(4,128)S(1)}, f32[28,4,128]{2,1,0:T(4,128)S(1)}, u32[]{:S(2)}, u32[]{:S(2)}) collective-permute-start(f32[28,4,128]{2,1,0:T(4,128)S(1)} %pad_maximum_fusion.4), channel_id=1, source_target_pairs={{0,2},{1,3},{2,0},{3,1},{4,6},{5,7},{6,4},{7,5},{8,10},{9,11},{10,... | collective-permute-start | bytes 172040 | tf_op jit(solution)/shard_map/ppermute | solution.py:137
  14.8 3.0 %collective-permute-done.1 = f32[28,4,128]{2,1,0:T(4,128)S(1)} collective-permute-done((f32[28,4,128]{2,1,0:T(4,128)S(1)}, f32[28,4,128]{2,1,0:T(4,128)S(1)}, u32[]{:S(2)}, u32[]{:S(2)}) %collective-permute-start.1) | collective-permute-done | bytes 57376 | tf_op jit(solution)/shard_map/ppermute | solution.py:137
  17.9 1.2 %collective-permute-done.4 = f32[32,4,128]{2,1,0:T(4,128)S(1)} collective-permute-done((f32[32,4,128]{2,1,0:T(4,128)S(1)}, f32[32,4,128]{2,1,0:T(4,128)S(1)}, u32[]{:S(2)}, u32[]{:S(2)}) %collective-permute-start.4) | collective-permute-done | bytes 65568 | tf_op jit(solution)/shard_map/ppermute | solution.py:137
  19.2 1.3 %shard_map.86 = (f32[32,4,128]{2,1,0:T(4,128)S(1)}, f32[64,4,128]{2,1,0:T(4,128)S(1)}) custom-call(s32[4,24]{1,0:T(4,128)S(1)} %pad_add_fusion.index_ref, bf16[24,128,128]{2,1,0:T(8,128)(2,1)S(1)} %copy-done.4, f32[64,4,128]{2,1,0:T(4,128)S(1)} %pad_maximum_fusion.col_vecs_ref, f32[32,4,128]{2,1,0:T(4,128)S(1)} %get-tuple-element.30.row_vecs_ref), custom_call_target="tpu_custom_call" | custom-call | tf_op jit(solution)/shard_map/pallas_call | solution.py:121
  20.8 1.1 %collective-permute-done.5 = f32[44,4,128]{2,1,0:T(4,128)S(1)} collective-permute-done((f32[44,4,128]{2,1,0:T(4,128)S(1)}, f32[44,4,128]{2,1,0:T(4,128)S(1)}, u32[]{:S(2)}, u32[]{:S(2)}) %collective-permute-start.5) | collective-permute-done | bytes 90144 | tf_op jit(solution)/shard_map/ppermute | solution.py:137
  21.9 0.7 %collective-permute-start.6 = (f32[28,4,128]{2,1,0:T(4,128)S(1)}, f32[28,4,128]{2,1,0:T(4,128)S(1)}, u32[]{:S(2)}, u32[]{:S(2)}) collective-permute-start(f32[28,4,128]{2,1,0:T(4,128)S(1)} %pad_maximum_fusion.5), channel_id=1, source_target_pairs={{0,8},{4,12},{8,0},{12,4},{16,24},{20,28},{24,16},{28,20},{1,9},{5... | collective-permute-start | bytes 172040 | tf_op jit(solution)/shard_map/ppermute | solution.py:137
  22.7 2.0 %collective-permute-done.8 = f32[16,4,128]{2,1,0:T(4,128)S(1)} collective-permute-done((f32[16,4,128]{2,1,0:T(4,128)S(1)}, f32[16,4,128]{2,1,0:T(4,128)S(1)}, u32[]{:S(2)}, u32[]{:S(2)}) %collective-permute-start.8) | collective-permute-done | bytes 32800 | tf_op jit(solution)/shard_map/ppermute | solution.py:137
  24.7 2.1 %collective-permute-start.9 = (f32[8,4,128]{2,1,0:T(4,128)S(1)}, f32[8,4,128]{2,1,0:T(4,128)S(1)}, u32[]{:S(2)}, u32[]{:S(2)}) collective-permute-start(f32[8,4,128]{2,1,0:T(4,128)S(1)} %slice.93), channel_id=1, source_target_pairs={{0,2},{1,3},{2,0},{3,1},{4,6},{5,7},{6,4},{7,5},{8,10},{9,11},{10,... | collective-permute-start | bytes 49160 | tf_op jit(solution)/shard_map/ppermute | solution.py:137
  26.9 0.7 %collective-permute-start.7 = (f32[20,4,128]{2,1,0:T(4,128)S(1)}, f32[20,4,128]{2,1,0:T(4,128)S(1)}, u32[]{:S(2)}, u32[]{:S(2)}) collective-permute-start(f32[20,4,128]{2,1,0:T(4,128)S(1)} %pad_maximum_fusion.7), channel_id=1, source_target_pairs={{0,16},{4,20},{8,24},{12,28},{16,0},{20,4},{24,8},{28,12},{1,17},{... | collective-permute-start | bytes 122888 | tf_op jit(solution)/shard_map/ppermute | solution.py:137
  27.6 1.8 %collective-permute-done.9 = f32[8,4,128]{2,1,0:T(4,128)S(1)} collective-permute-done((f32[8,4,128]{2,1,0:T(4,128)S(1)}, f32[8,4,128]{2,1,0:T(4,128)S(1)}, u32[]{:S(2)}, u32[]{:S(2)}) %collective-permute-start.9) | collective-permute-done | bytes 16416 | tf_op jit(solution)/shard_map/ppermute | solution.py:137
  29.4 1.6 %collective-permute-done.7 = f32[20,4,128]{2,1,0:T(4,128)S(1)} collective-permute-done((f32[20,4,128]{2,1,0:T(4,128)S(1)}, f32[20,4,128]{2,1,0:T(4,128)S(1)}, u32[]{:S(2)}, u32[]{:S(2)}) %collective-permute-start.7) | collective-permute-done | bytes 40992 | tf_op jit(solution)/shard_map/ppermute | solution.py:137
  31.0 4.6 %shard_map.87 = (f32[48,48]{1,0:T(8,128)S(1)}, f32[48,48]{1,0:T(8,128)S(1)}) custom-call(f32[12,4,128]{2,1,0:T(4,128)S(1)} %slice_add_fusion.3.gram_ref), custom_call_target="tpu_custom_call" | custom-call | tf_op jit(solution)/shard_map/pallas_call | solution.py:121
  35.7 1.3 %shard_map.88 = (f32[48,1024]{1,0:T(8,128)}, f32[48,1024]{1,0:T(8,128)}, f32[32,4,128]{2,1,0:T(4,128)S(1)}) custom-call(f32[48,48]{1,0:T(8,128)S(1)} %get-tuple-element.15.inverse_ref, f32[8,4,128]{2,1,0:T(4,128)S(1)} %get-tuple-element.13.wide_ref, f32[44,1024]{1,0:T(8,128)S(1)} %copy-done.1, f32[44,1024]{1,0:T(8,128)S(1)} %copy-done.3, ...), custom_call_target="tpu_custom_call" | custom-call | tf_op jit(solution)/shard_map/pallas_call | solution.py:121
  37.0 10.4 %all_to_all.5.parts_ref = f32[32,4,128]{2,1,0:T(4,128)S(1)} all-to-all(f32[32,4,128]{2,1,0:T(4,128)S(1)} %get-tuple-element.18), channel_id=1, replica_groups=mesh['row'=8,'col'=4] {'row','col'}, dimensions={0} | all-to-all | bytes 131072 | tf_op jit(solution)/shard_map/all_to_all | solution.py:222
  47.4 0.9 %shard_map.89 = f32[48,48]{1,0:T(8,128)} custom-call(f32[48,48]{1,0:T(8,128)S(1)} %get-tuple-element.15.inverse_ref, f32[48,48]{1,0:T(8,128)S(1)} %get-tuple-element.16.start_ref, f32[32,4,128]{2,1,0:T(4,128)S(1)} %all_to_all.5.parts_ref), custom_call_target="tpu_custom_call" | custom-call | tf_op jit(solution)/shard_map/pallas_call | solution.py:121
  (44 shorter events, 1.2 us)
Async XLA Ops:
  0.6 0.9 %copy-start = (f32[44,1024]{1,0:T(8,128)S(1)}, f32[44,1024]{1,0:T(8,128)}, u32[]{:S(2)}) copy-start(f32[44,1024]{1,0:T(8,128)} %basis_ref.3) | copy-start | bytes 540676
  1.6 0.9 %copy-start.2 = (f32[44,1024]{1,0:T(8,128)S(1)}, f32[44,1024]{1,0:T(8,128)}, u32[]{:S(2)}) copy-start(f32[44,1024]{1,0:T(8,128)} %image_ref.3) | copy-start | bytes 540676
  2.5 0.7 %copy-start.5 = (bf16[4,1024]{1,0:T(4,128)(2,1)S(1)}, bf16[4,1024]{1,0:T(4,128)(2,1)}, u32[]{:S(2)}) copy-start(bf16[4,1024]{1,0:T(4,128)(2,1)} %trial_ref.1) | copy-start | bytes 24580
  3.2 16.0 %copy-start.4 = (bf16[24,128,128]{2,1,0:T(8,128)(2,1)S(1)}, bf16[24,128,128]{2,1,0:T(8,128)(2,1)}, u32[]{:S(2)}) copy-start(bf16[24,128,128]{2,1,0:T(8,128)(2,1)} %tiles_ref.1) | copy-start | bytes 2359300
  3.7 6.7 %collective-permute-start.2 = (f32[8,4,128]{2,1,0:T(4,128)S(1)}, f32[8,4,128]{2,1,0:T(4,128)S(1)}, u32[]{:S(2)}, u32[]{:S(2)}) collective-permute-start(f32[8,4,128]{2,1,0:T(4,128)S(1)} %get-tuple-element.13.wide_ref), channel_id=1, source_target_pairs={{0,8},{4,12},{8,0},{12,4},{16,24},{20,28},{24,16},{28,20},{1,9},{5... | collective-permute-start | bytes 49160 | tf_op jit(solution)/shard_map/ppermute | solution.py:137
  6.7 5.3 %collective-permute-start = (f32[20,4,128]{2,1,0:T(4,128)S(1)}, f32[20,4,128]{2,1,0:T(4,128)S(1)}, u32[]{:S(2)}, u32[]{:S(2)}) collective-permute-start(f32[20,4,128]{2,1,0:T(4,128)S(1)} %pad_maximum_fusion.6), channel_id=1, source_target_pairs={{0,1},{1,0},{2,3},{3,2},{4,5},{5,4},{6,7},{7,6},{8,9},{9,8},{10,11... | collective-permute-start | bytes 122888 | tf_op jit(solution)/shard_map/ppermute | solution.py:137
  10.5 7.3 %collective-permute-start.3 = (f32[16,4,128]{2,1,0:T(4,128)S(1)}, f32[16,4,128]{2,1,0:T(4,128)S(1)}, u32[]{:S(2)}, u32[]{:S(2)}) collective-permute-start(f32[16,4,128]{2,1,0:T(4,128)S(1)} %pad_maximum_fusion.8), channel_id=1, source_target_pairs={{0,16},{4,20},{8,24},{12,28},{16,0},{20,4},{24,8},{28,12},{1,17},{... | collective-permute-start | bytes 98312 | tf_op jit(solution)/shard_map/ppermute | solution.py:137
  12.1 5.6 %collective-permute-start.1 = (f32[28,4,128]{2,1,0:T(4,128)S(1)}, f32[28,4,128]{2,1,0:T(4,128)S(1)}, u32[]{:S(2)}, u32[]{:S(2)}) collective-permute-start(f32[28,4,128]{2,1,0:T(4,128)S(1)} %pad_maximum_fusion.4), channel_id=1, source_target_pairs={{0,2},{1,3},{2,0},{3,1},{4,6},{5,7},{6,4},{7,5},{8,10},{9,11},{10,... | collective-permute-start | bytes 172040 | tf_op jit(solution)/shard_map/ppermute | solution.py:137
  17.8 1.3 %collective-permute-start.4 = (f32[32,4,128]{2,1,0:T(4,128)S(1)}, f32[32,4,128]{2,1,0:T(4,128)S(1)}, u32[]{:S(2)}, u32[]{:S(2)}) collective-permute-start(f32[32,4,128]{2,1,0:T(4,128)S(1)} %get-tuple-element.31), channel_id=1, source_target_pairs={{0,4},{4,0},{8,12},{12,8},{16,20},{20,16},{24,28},{28,24},{1,5},{5... | collective-permute-start | bytes 196616 | tf_op jit(solution)/shard_map/ppermute | solution.py:137
  20.5 1.4 %collective-permute-start.5 = (f32[44,4,128]{2,1,0:T(4,128)S(1)}, f32[44,4,128]{2,1,0:T(4,128)S(1)}, u32[]{:S(2)}, u32[]{:S(2)}) collective-permute-start(f32[44,4,128]{2,1,0:T(4,128)S(1)} %pad_maximum_fusion.1), channel_id=1, source_target_pairs={{0,4},{4,0},{8,12},{12,8},{16,20},{20,16},{24,28},{28,24},{1,5},{5... | collective-permute-start | bytes 270344 | tf_op jit(solution)/shard_map/ppermute | solution.py:137
  20.7 3.9 %collective-permute-start.8 = (f32[16,4,128]{2,1,0:T(4,128)S(1)}, f32[16,4,128]{2,1,0:T(4,128)S(1)}, u32[]{:S(2)}, u32[]{:S(2)}) collective-permute-start(f32[16,4,128]{2,1,0:T(4,128)S(1)} %slice.75), channel_id=1, source_target_pairs={{0,1},{1,0},{2,3},{3,2},{4,5},{5,4},{6,7},{7,6},{8,9},{9,8},{10,11... | collective-permute-start | bytes 98312 | tf_op jit(solution)/shard_map/ppermute | solution.py:137
  21.9 4.9 %collective-permute-start.6 = (f32[28,4,128]{2,1,0:T(4,128)S(1)}, f32[28,4,128]{2,1,0:T(4,128)S(1)}, u32[]{:S(2)}, u32[]{:S(2)}) collective-permute-start(f32[28,4,128]{2,1,0:T(4,128)S(1)} %pad_maximum_fusion.5), channel_id=1, source_target_pairs={{0,8},{4,12},{8,0},{12,4},{16,24},{20,28},{24,16},{28,20},{1,9},{5... | collective-permute-start | bytes 172040 | tf_op jit(solution)/shard_map/ppermute | solution.py:137
  24.7 4.7 %collective-permute-start.9 = (f32[8,4,128]{2,1,0:T(4,128)S(1)}, f32[8,4,128]{2,1,0:T(4,128)S(1)}, u32[]{:S(2)}, u32[]{:S(2)}) collective-permute-start(f32[8,4,128]{2,1,0:T(4,128)S(1)} %slice.93), channel_id=1, source_target_pairs={{0,2},{1,3},{2,0},{3,1},{4,6},{5,7},{6,4},{7,5},{8,10},{9,11},{10,... | collective-permute-start | bytes 49160 | tf_op jit(solution)/shard_map/ppermute | solution.py:137
  26.8 8.8 %copy-start.3 = (f32[44,1024]{1,0:T(8,128)S(1)}, f32[44,1024]{1,0:T(8,128)}, u32[]{:S(2)}) copy-start(f32[44,1024]{1,0:T(8,128)} %image_ref.3) | copy-start | bytes 540676
  26.9 8.8 %copy-start.1 = (f32[44,1024]{1,0:T(8,128)S(1)}, f32[44,1024]{1,0:T(8,128)}, u32[]{:S(2)}) copy-start(f32[44,1024]{1,0:T(8,128)} %basis_ref.3) | copy-start | bytes 540676
  26.9 4.1 %collective-permute-start.7 = (f32[20,4,128]{2,1,0:T(4,128)S(1)}, f32[20,4,128]{2,1,0:T(4,128)S(1)}, u32[]{:S(2)}, u32[]{:S(2)}) collective-permute-start(f32[20,4,128]{2,1,0:T(4,128)S(1)} %pad_maximum_fusion.7), channel_id=1, source_target_pairs={{0,16},{4,20},{8,24},{12,28},{16,0},{20,4},{24,8},{28,12},{1,17},{... | collective-permute-start | bytes 122888 | tf_op jit(solution)/shard_map/ppermute | solution.py:137

commit v2 on v1

v2 whole, which is shorter than its diff:
```python
import functools

import jax
import jax.numpy as jnp
from jax import lax
from jax.experimental import pallas as pl
from jax.experimental.pallas import tpu as pltpu
from jax.sharding import PartitionSpec as P

HIGHEST = lax.Precision.HIGHEST
LANES = 128
SUBLANES = 8
PANEL = 16
VMEM_LIMIT = 32 * 1024 * 1024


def contract_last(left, right):
    return lax.dot_general(
        left,
        right,
        (((1,), (1,)), ((), ())),
        precision=HIGHEST,
        preferred_element_type=jnp.float32,
    )


def multiply(left, right):
    return jnp.dot(left, right, precision=HIGHEST, preferred_element_type=jnp.float32)


def side_by_side(blocks_ref):
    return jnp.concatenate([blocks_ref[b] for b in range(blocks_ref.shape[0])], axis=1)


def load_kernel(
    trial_hbm, basis_hbm, image_hbm, rows_hbm, cols_hbm,
    wide_ref, basis_ref, image_ref, rows_ref, cols_ref, trial_vmem, basis_vmem, sems,
):
    copies = [
        pltpu.make_async_copy(source, target, sems.at[i])
        for i, (source, target) in enumerate(
            [
                (trial_hbm, trial_vmem),
                (basis_hbm, basis_vmem),
                (image_hbm, image_ref),
                (rows_hbm, rows_ref),
                (cols_hbm, cols_ref),
            ]
        )
    ]
    for copy in copies:
        copy.start()
    copies[0].wait()
    trial = trial_vmem[...].astype(jnp.float32)
    for b in range(wide_ref.shape[0]):
        wide_ref[b] = trial[:, b * LANES : (b + 1) * LANES]
    copies[1].wait()
    basis_ref[...] = jnp.concatenate([basis_vmem[...], trial], axis=0)
    for copy in copies[2:]:
        copy.wait()


def gram_kernel(scale, wide_ref, basis_ref, image_ref, sent_ref):
    blocks, vecs = wide_ref.shape[:2]
    basis_all = basis_ref[...]
    correlation = contract_last(basis_all, basis_all)
    coupling = contract_last(basis_all, image_ref[...])
    count = correlation.shape[0]
    unused = jnp.zeros((count, LANES - count - coupling.shape[1]), jnp.float32)
    gram = jnp.concatenate([correlation, coupling, unused], axis=1) * scale
    sent_ref[:blocks] = wide_ref[...]
    for i in range(sent_ref.shape[0] - blocks):
        sent_ref[blocks + i] = gram[i * vecs : (i + 1) * vecs]


def split(index, size):
    return index >> (size.bit_length() - 1), index & (size - 1)


def place(apart, bits):
    if bits == bits_of(1 << len(bits)):
        return apart
    return sum(((apart >> (m.bit_length() - 1)) & 1) << j for j, m in enumerate(bits))


def tiles_kernel(
    contract, by_rows, by_cols, n_row, blocks, position_ref, rows_ref, cols_ref, tiles_ref, vecs_ref, sums_ref
):
    sums_ref[...] = jnp.zeros_like(sums_ref)
    row, col = position_ref[0], position_ref[1]
    for t in range(tiles_ref.shape[0]):
        row_piece, row_inner = split(rows_ref[t], blocks)
        col_piece, col_inner = split(cols_ref[t] - col * (blocks * n_row), blocks)
        at_row = place(split(row_piece, n_row)[0] ^ col, by_rows) * blocks + row_inner
        at_col = place(col_piece ^ row, by_cols) * blocks + col_inner
        source, target = (at_col, at_row) if contract else (at_row, at_col)
        product = lax.dot_general(
            vecs_ref[source].astype(jnp.bfloat16),
            tiles_ref[t],
            (((1,), (contract,)), ((), ())),
            preferred_element_type=jnp.float32,
        )
        sums_ref[target] = sums_ref[target] + product


def factor_kernel(count, gram_ref, inverse_ref):
    gram = jnp.concatenate([gram_ref[i] for i in range(gram_ref.shape[0])], axis=0)
    row_id = lax.broadcasted_iota(jnp.int32, (count, LANES), 0)
    lane_id = lax.broadcasted_iota(jnp.int32, (count, LANES), 1)
    identity = jnp.where(lane_id == row_id + count, 1.0, 0.0)
    work = jnp.where(lane_id < count, gram, identity)
    tiles = count // SUBLANES
    work = [work[SUBLANES * g : SUBLANES * (g + 1)] for g in range(tiles)]
    sublane = lax.broadcasted_iota(jnp.int32, (SUBLANES, LANES), 0)
    diagonal = [jnp.ones((SUBLANES, LANES), jnp.float32)] * tiles

    def spread(tile, i):
        return jnp.broadcast_to(tile[i : i + 1, :], (SUBLANES, LANES))

    for start in range(0, count, PANEL):
        stop = min(start + PANEL, count)
        first = start // SUBLANES
        columns = {
            j: {
                g: jnp.broadcast_to(work[g][:, j : j + 1], (SUBLANES, LANES))
                for g in range(first, tiles)
            }
            for j in range(start, stop)
        }
        for j in range(start, stop):
            i, own = j % SUBLANES, j // SUBLANES
            pivot = spread(columns[j][own], i)
            diagonal[own] = jnp.where(sublane == i, pivot, diagonal[own])
            reciprocal = 1.0 / pivot
            row = spread(work[own], i)
            entries = {k: spread(columns[k][own], i) for k in range(j + 1, stop)}
            for g in range(own, tiles):
                ratio = columns[j][g] * reciprocal
                if g == own:
                    ratio = jnp.where(sublane > i, ratio, 0.0)
                work[g] = work[g] - ratio * row
                for k in range(j + 1, stop):
                    columns[k][g] = columns[k][g] - ratio * entries[k]
    for g in range(tiles):
        scaled = work[g] * lax.rsqrt(diagonal[g])
        inverse_ref[SUBLANES * g : SUBLANES * (g + 1), :] = scaled[:, count : 2 * count]


def basis_kernel(inverse_ref, gram_ref, basis_ref, image_ref, basis_new_ref, image_start_ref, start_ref):
    inverse = inverse_ref[...]
    count, old = inverse.shape[0], image_ref.shape[0]
    basis_new_ref[...] = multiply(inverse, basis_ref[...])
    image_start_ref[...] = multiply(inverse[:, :old], image_ref[...])
    gram = jnp.concatenate([gram_ref[i] for i in range(gram_ref.shape[0])], axis=0)
    coupling = gram[:, count : count + old]
    start_ref[...] = contract_last(multiply(inverse, coupling), inverse[:, :old])


def image_kernel(scale, basis_new_ref, rows_ref, cols_ref, image_ref, part_ref):
    summed = [rows_ref[b] + cols_ref[b] for b in range(rows_ref.shape[0])]
    image = jnp.concatenate(summed, axis=1)
    image_ref[...] = image
    vecs, count = image.shape[0], basis_new_ref.shape[0]
    part = contract_last(image, basis_new_ref[...]) * scale
    part = jnp.concatenate([part, jnp.zeros((vecs, LANES - count), jnp.float32)], axis=1)
    part_ref[...] = jnp.broadcast_to(part[None], part_ref.shape)


def finish_kernel(
    inverse_ref, basis_new_ref, image_start_ref, image_ref, start_ref, parts_ref,
    projected_hbm, basis_new_hbm, image_new_hbm, projected_vmem, image_new_vmem, sems,
):
    basis_copy = pltpu.make_async_copy(basis_new_ref, basis_new_hbm, sems.at[0])
    basis_copy.start()
    vecs = image_ref.shape[0]
    count = inverse_ref.shape[0]
    last = inverse_ref[...][:, count - vecs :]
    image_new_vmem[...] = image_start_ref[...] + multiply(last, image_ref[...])
    image_copy = pltpu.make_async_copy(image_new_vmem, image_new_hbm, sems.at[1])
    image_copy.start()
    total = jnp.sum(parts_ref[...], axis=0)
    new = lax.dot_general(
        total[:, :count],
        last,
        (((0,), (1,)), ((), ())),
        precision=HIGHEST,
        preferred_element_type=jnp.float32,
    )
    projected_vmem[...] = start_ref[...] + new
    projected_copy = pltpu.make_async_copy(projected_vmem, projected_hbm, sems.at[2])
    projected_copy.start()
    basis_copy.wait()
    image_copy.wait()
    projected_copy.wait()


def call(kernel, outs, *args, smem=0, from_hbm=False, to_hbm=False, scratch=(), flops=0):
    operand = pl.BlockSpec(memory_space=pltpu.HBM if from_hbm else pltpu.VMEM)
    result = pl.BlockSpec(memory_space=pltpu.HBM if to_hbm else pltpu.VMEM)
    scalars = pl.BlockSpec(memory_space=pltpu.SMEM)
    if from_hbm:
        args = [pltpu.with_memory_space_constraint(arg, pltpu.HBM) for arg in args]
    outs = [o if hasattr(o, "dtype") else jax.ShapeDtypeStruct(o, jnp.float32) for o in outs]
    return pl.pallas_call(
        kernel,
        out_shape=outs,
        in_specs=[scalars] * smem + [operand] * (len(args) - smem),
        out_specs=[result] * len(outs),
        scratch_shapes=scratch,
        compiler_params=pltpu.CompilerParams(vmem_limit_bytes=VMEM_LIMIT),
        cost_estimate=pl.CostEstimate(flops=flops, bytes_accessed=0, transcendentals=0),
    )(*args)


def bits_of(size):
    return [1 << j for j in range(size.bit_length() - 1)]


def swap(array, axis, mask):
    size = lax.axis_size(axis)
    return lax.ppermute(array, axis, [(i, i ^ mask) for i in range(size)])


def local(tile_blocks, tile_rows, tile_cols, trial_vectors, basis_old, image_old):
    tile_size = tile_blocks.shape[1]
    vecs, width = trial_vectors.shape
    old = basis_old.shape[0]
    count = old + vecs
    blocks = width // tile_size
    n_row, n_col = lax.axis_size("row"), lax.axis_size("col")
    row, col = lax.axis_index("row"), lax.axis_index("col")
    scale = 1.0 / float(width * n_row * n_col)
    row_bits, col_bits = bits_of(n_row), bits_of(n_col)
    gather_row = row_bits[1:] + row_bits[:1]
    gather_col = col_bits
    scatter_row = row_bits
    scatter_col = col_bits
    grams = count // vecs
    position = jnp.stack([row, col])

    places = jax.ShapeDtypeStruct(tile_rows.shape, tile_rows.dtype)
    wide, basis_all, image_kept, rows_kept, cols_kept = call(
        load_kernel,
        [(blocks, vecs, tile_size), (count, width), (old, width), places, places],
        trial_vectors,
        basis_old,
        image_old,
        tile_rows,
        tile_cols,
        from_hbm=True,
        scratch=[
            pltpu.VMEM((vecs, width), trial_vectors.dtype),
            pltpu.VMEM((old, width), jnp.float32),
            pltpu.SemaphoreType.DMA((5,)),
        ],
    )
    col_vecs = wide
    for m in gather_row:
        col_vecs = jnp.concatenate([col_vecs, swap(col_vecs, "row", m)], axis=0)
    (sent,) = call(
        functools.partial(gram_kernel, scale),
        [(blocks + grams, vecs, LANES)],
        wide,
        basis_all,
        image_kept,
    )
    for m in gather_col:
        size = sent.shape[0] - grams
        got = swap(sent, "col", m)
        gram = sent[size:] + got[size:]
        sent = jnp.concatenate([sent[:size], got[:size], gram], axis=0)

    (col_sums,) = call(
        functools.partial(tiles_kernel, 0, gather_col, scatter_row[::-1], n_row, blocks),
        [(blocks * n_row, vecs, tile_size)],
        position,
        rows_kept,
        cols_kept,
        tile_blocks,
        sent,
        smem=3,
    )
    (row_sums,) = call(
        functools.partial(tiles_kernel, 1, scatter_col[::-1], gather_row, n_row, blocks),
        [(blocks * n_col, vecs, tile_size)],
        position,
        rows_kept,
        cols_kept,
        tile_blocks,
        col_vecs,
        smem=3,
    )
    for m in scatter_row:
        half = col_sums.shape[0] // 2
        got = swap(jnp.concatenate([col_sums[half:], gram], axis=0), "row", m)
        col_sums = col_sums[:half] + got[:half]
        gram = gram + got[half:]
    for m in scatter_col:
        half = row_sums.shape[0] // 2
        row_sums = row_sums[:half] + swap(row_sums[half:], "col", m)

    (inverse,) = call(functools.partial(factor_kernel, count), [(count, count)], gram)
    basis_new, image_start, start = call(
        basis_kernel,
        [(count, width), (count, width), (count, count)],
        inverse,
        gram,
        basis_all,
        image_kept,
    )
    image, part = call(
        functools.partial(image_kernel, scale),
        [(vecs, width), (n_row * n_col, vecs, LANES)],
        basis_new,
        row_sums,
        col_sums,
    )
    parts = lax.all_to_all(part, ("row", "col"), split_axis=0, concat_axis=0, tiled=True)
    return call(
        finish_kernel,
        [(count, count), (count, width), (count, width)],
        inverse,
        basis_new,
        image_start,
        image,
        start,
        parts,
        to_hbm=True,
        scratch=[
            pltpu.VMEM((count, count), jnp.float32),
            pltpu.VMEM((count, width), jnp.float32),
            pltpu.SemaphoreType.DMA((3,)),
        ],
    )


def solution(mesh):
    in_specs = (
        P(("row", "col"), None, None),
        P(("row", "col")),
        P(("row", "col")),
        P(None, ("col", "row")),
        P(None, ("col", "row")),
        P(None, ("col", "row")),
    )
    out_specs = (P(), P(None, ("col", "row")), P(None, ("col", "row")))
    return jax.shard_map(local, mesh=mesh, in_specs=in_specs, out_specs=out_specs, check_vma=False)
```

time: 48.5 us -> 41.9 us (0.86)
  waiting for transfers between devices: 10.7 us -> 7.07 us
  starting transfers between devices: 12.7 us -> 15.9 us
  local copies, waits for them, and re-layouts: 2.6 us -> 0.03 us
  other arithmetic: 2.32 us -> 0.33 us
  Pallas kernels: 8.61 us -> 6.7 us
    ppermute x10, waiting for transfers between devices: 10.7 us -> 7.07 us  [swap(): return lax.ppermute(array, axis, [(i, i ^ mask) for i in range(size)])]
    ppermute x10, starting transfers between devices: 12.7 us -> 15.9 us  [swap(): return lax.ppermute(array, axis, [(i, i ^ mask) for i in range(size)])]
    unnamed x12 -> x2, local copies, waits for them, and re-layouts: 2.56 us -> 0.01 us
    pallas_call x5 -> x8, Pallas kernels: 8.61 us -> 6.7 us  [call(): pl.pallas_call(kernel, out_shape=outs, in_specs=[scalars] * smem + [opera...]
    another operation x4 -> x1, other arithmetic: 1.4 us -> 0.07 us  [local(): position = jnp.stack([row, col])]
    xor x1 -> x0, other arithmetic: 0.67 us -> none  [local(): col_apart = col_piece ^ row]
  transfers between devices with their start and end apart: 10 -> 10, of which waited for: 6 -> 5; matrix products, arithmetic and copies ran while one was open for 5% -> 1% of each run, Pallas kernels for 0% -> 6%
where the time goes in v2:
time: 41.9 us; the launch traced here: 41.7 us
  starting transfers between devices  15.9 us (38%)
  blocking collectives  10.8 us (26%)
  waiting for transfers between devices  7.07 us (17%)
  Pallas kernels  6.7 us (16%)
  between operations  0.85 us (2%)
    ppermute x10, starting transfers between devices, swap(): return lax.ppermute(array, axis, [(i, i ^ mask) for i in range(size)])  15.9 us
    all_to_all x1, blocking collectives, local(): lax.all_to_all(part, ('row', 'col'), split_axis=0, concat_axis=0, tiled=T...  10.8 us
    ppermute x10, waiting for transfers between devices, swap(): return lax.ppermute(array, axis, [(i, i ^ mask) for i in range(size)])  7.07 us
    pallas_call x8, Pallas kernels, call(): pl.pallas_call(kernel, out_shape=outs, in_specs=[scalars] * smem + [opera...  6.7 us
  transfers between devices with their start and end apart: 10, of which 5 were waited for; matrix products, arithmetic and copies ran while one was open for 1% of the time, Pallas kernels for 6%

profile of v2, /device:TPU:0, one launch (start us, length us, event | category | flops | bytes accessed | tf_op | source)
XLA Modules:
  0.0 41.7 jit_solution(15789125995171260765)
XLA Ops:
  0.6 1.2 %shard_map.85 = (f32[8,4,128]{2,1,0:T(4,128)S(1)}, f32[48,1024]{1,0:T(8,128)S(1)}, f32[44,1024]{1,0:T(8,128)S(1)}, s32[24]{0:T(128)S(1)}, s32[24]{0:T(128)S(1)}) custom-call(bf16[4,1024]{1,0:T(4,128)(2,1)} %trial_hbm.1, f32[44,1024]{1,0:T(8,128)} %basis_hbm.1, f32[44,1024]{1,0:T(8,128)} %image_hbm.1, s32[24]{0:T(128)} %rows_hbm.1, s32[24]{0:T(128)} %cols_hbm.1), custom_call_target="tpu_custom_call" | custom-call | tf_op jit(solution)/shard_map/pallas_call | solution.py:204
  1.8 3.0 %collective-permute-start.5 = (f32[8,4,128]{2,1,0:T(4,128)S(1)}, f32[8,4,128]{2,1,0:T(4,128)S(1)}, u32[]{:S(2)}, u32[]{:S(2)}) collective-permute-start(f32[8,4,128]{2,1,0:T(4,128)S(1)} %get-tuple-element.13.wide_ref), channel_id=1, source_target_pairs={{0,8},{4,12},{8,0},{12,4},{16,24},{20,28},{24,16},{28,20},{1,9},{5... | collective-permute-start | bytes 49160 | tf_op jit(solution)/shard_map/ppermute | solution.py:221
  4.8 0.5 %shard_map.86 = f32[20,4,128]{2,1,0:T(4,128)S(1)} custom-call(f32[8,4,128]{2,1,0:T(4,128)S(1)} %get-tuple-element.13.wide_ref, f32[48,1024]{1,0:T(8,128)S(1)} %get-tuple-element.14.basis_ref, f32[44,1024]{1,0:T(8,128)S(1)} %get-tuple-element.15.image_ref), custom_call_target="tpu_custom_call" | custom-call | tf_op jit(solution)/shard_map/pallas_call | solution.py:204
  5.3 1.6 %collective-permute-start = (f32[20,4,128]{2,1,0:T(4,128)S(1)}, f32[20,4,128]{2,1,0:T(4,128)S(1)}, u32[]{:S(2)}, u32[]{:S(2)}) collective-permute-start(f32[20,4,128]{2,1,0:T(4,128)S(1)} %shard_map.86), channel_id=1, source_target_pairs={{0,1},{1,0},{2,3},{3,2},{4,5},{5,4},{6,7},{7,6},{8,9},{9,8},{10,11... | collective-permute-start | bytes 122888 | tf_op jit(solution)/shard_map/ppermute | solution.py:221
  7.0 0.1 pad_add_fusion.position_ref
  7.1 1.6 %collective-permute-start.6 = (f32[16,4,128]{2,1,0:T(4,128)S(1)}, f32[16,4,128]{2,1,0:T(4,128)S(1)}, u32[]{:S(2)}, u32[]{:S(2)}) collective-permute-start(f32[16,4,128]{2,1,0:T(4,128)S(1)} %pad_maximum_fusion.7), channel_id=1, source_target_pairs={{0,16},{4,20},{8,24},{12,28},{16,0},{20,4},{24,8},{28,12},{1,17},{... | collective-permute-start | bytes 98312 | tf_op jit(solution)/shard_map/ppermute | solution.py:221
  8.7 0.7 %collective-permute-done = f32[20,4,128]{2,1,0:T(4,128)S(1)} collective-permute-done((f32[20,4,128]{2,1,0:T(4,128)S(1)}, f32[20,4,128]{2,1,0:T(4,128)S(1)}, u32[]{:S(2)}, u32[]{:S(2)}) %collective-permute-start) | collective-permute-done | bytes 40992 | tf_op jit(solution)/shard_map/ppermute | solution.py:221
  9.5 2.7 %collective-permute-start.1 = (f32[28,4,128]{2,1,0:T(4,128)S(1)}, f32[28,4,128]{2,1,0:T(4,128)S(1)}, u32[]{:S(2)}, u32[]{:S(2)}) collective-permute-start(f32[28,4,128]{2,1,0:T(4,128)S(1)} %pad_maximum_fusion.4), channel_id=1, source_target_pairs={{0,2},{1,3},{2,0},{3,1},{4,6},{5,7},{6,4},{7,5},{8,10},{9,11},{10,... | collective-permute-start | bytes 172040 | tf_op jit(solution)/shard_map/ppermute | solution.py:221
  12.1 0.1 collective-permute-start.7
  12.2 2.4 %collective-permute-done.1 = f32[28,4,128]{2,1,0:T(4,128)S(1)} collective-permute-done((f32[28,4,128]{2,1,0:T(4,128)S(1)}, f32[28,4,128]{2,1,0:T(4,128)S(1)}, u32[]{:S(2)}, u32[]{:S(2)}) %collective-permute-start.1) | collective-permute-done | bytes 57376 | tf_op jit(solution)/shard_map/ppermute | solution.py:221
  14.7 0.9 %shard_map.87 = f32[64,4,128]{2,1,0:T(4,128)S(1)} custom-call(s32[2]{0:T(128)S(1)} %pad_add_fusion.position_ref, s32[24]{0:T(128)S(1)} %get-tuple-element.16.rows_ref, s32[24]{0:T(128)S(1)} %get-tuple-element.17.cols_ref, bf16[24,128,128]{2,1,0:T(8,128)(2,1)S(1)} %copy-done, f32[44,4,128]{2,1,0:T(4,128)S(1)} %pad_maximum_fusion.2.vecs_ref), custom_call_target="tpu_custom_call" | custom-call | tf_op jit(solution)/shard_map/pallas_call | solution.py:204
  15.7 1.1 %shard_map.90 = f32[32,4,128]{2,1,0:T(4,128)S(1)} custom-call(s32[2]{0:T(128)S(1)} %pad_add_fusion.position_ref, s32[24]{0:T(128)S(1)} %get-tuple-element.16.rows_ref, s32[24]{0:T(128)S(1)} %get-tuple-element.17.cols_ref, bf16[24,128,128]{2,1,0:T(8,128)(2,1)S(1)} %copy-done, f32[64,4,128]{2,1,0:T(4,128)S(1)} %pad_maximum_fusion.vecs_ref), custom_call_target="tpu_custom_call" | custom-call | tf_op jit(solution)/shard_map/pallas_call | solution.py:204
  16.8 1.6 %collective-permute-start.8 = (f32[16,4,128]{2,1,0:T(4,128)S(1)}, f32[16,4,128]{2,1,0:T(4,128)S(1)}, u32[]{:S(2)}, u32[]{:S(2)}) collective-permute-start(f32[16,4,128]{2,1,0:T(4,128)S(1)} %slice.107), channel_id=1, source_target_pairs={{0,1},{1,0},{2,3},{3,2},{4,5},{5,4},{6,7},{7,6},{8,9},{9,8},{10,11... | collective-permute-start | bytes 98312 | tf_op jit(solution)/shard_map/ppermute | solution.py:221
  18.5 0.8 %collective-permute-start.3 = (f32[28,4,128]{2,1,0:T(4,128)S(1)}, f32[28,4,128]{2,1,0:T(4,128)S(1)}, u32[]{:S(2)}, u32[]{:S(2)}) collective-permute-start(f32[28,4,128]{2,1,0:T(4,128)S(1)} %pad_maximum_fusion.5), channel_id=1, source_target_pairs={{0,8},{4,12},{8,0},{12,4},{16,24},{20,28},{24,16},{28,20},{1,9},{5... | collective-permute-start | bytes 172040 | tf_op jit(solution)/shard_map/ppermute | solution.py:221
  19.3 1.4 %collective-permute-done.8 = f32[16,4,128]{2,1,0:T(4,128)S(1)} collective-permute-done((f32[16,4,128]{2,1,0:T(4,128)S(1)}, f32[16,4,128]{2,1,0:T(4,128)S(1)}, u32[]{:S(2)}, u32[]{:S(2)}) %collective-permute-start.8) | collective-permute-done | bytes 32800 | tf_op jit(solution)/shard_map/ppermute | solution.py:221
  20.8 2.9 %collective-permute-start.9 = (f32[8,4,128]{2,1,0:T(4,128)S(1)}, f32[8,4,128]{2,1,0:T(4,128)S(1)}, u32[]{:S(2)}, u32[]{:S(2)}) collective-permute-start(f32[8,4,128]{2,1,0:T(4,128)S(1)} %slice.109), channel_id=1, source_target_pairs={{0,2},{1,3},{2,0},{3,1},{4,6},{5,7},{6,4},{7,5},{8,10},{9,11},{10,... | collective-permute-start | bytes 49160 | tf_op jit(solution)/shard_map/ppermute | solution.py:221
  23.7 1.6 %collective-permute-start.4 = (f32[20,4,128]{2,1,0:T(4,128)S(1)}, f32[20,4,128]{2,1,0:T(4,128)S(1)}, u32[]{:S(2)}, u32[]{:S(2)}) collective-permute-start(f32[20,4,128]{2,1,0:T(4,128)S(1)} %pad_maximum_fusion.6), channel_id=1, source_target_pairs={{0,16},{4,20},{8,24},{12,28},{16,0},{20,4},{24,8},{28,12},{1,17},{... | collective-permute-start | bytes 122888 | tf_op jit(solution)/shard_map/ppermute | solution.py:221
  25.3 0.2 collective-permute-done.9
  25.5 2.3 %collective-permute-done.4 = f32[20,4,128]{2,1,0:T(4,128)S(1)} collective-permute-done((f32[20,4,128]{2,1,0:T(4,128)S(1)}, f32[20,4,128]{2,1,0:T(4,128)S(1)}, u32[]{:S(2)}, u32[]{:S(2)}) %collective-permute-start.4) | collective-permute-done | bytes 40992 | tf_op jit(solution)/shard_map/ppermute | solution.py:221
  27.8 1.1 %shard_map.88.inverse_ref = f32[48,48]{1,0:T(8,128)S(1)} custom-call(f32[12,4,128]{2,1,0:T(4,128)S(1)} %slice_add_fusion.3.gram_ref), custom_call_target="tpu_custom_call" | custom-call | tf_op jit(solution)/shard_map/pallas_call | solution.py:204
  28.8 0.7 %shard_map.89 = (f32[48,1024]{1,0:T(8,128)S(1)}, f32[48,1024]{1,0:T(8,128)S(1)}, f32[48,48]{1,0:T(8,128)S(1)}) custom-call(f32[48,48]{1,0:T(8,128)S(1)} %shard_map.88.inverse_ref, f32[12,4,128]{2,1,0:T(4,128)S(1)} %slice_add_fusion.3.gram_ref, f32[48,1024]{1,0:T(8,128)S(1)} %get-tuple-element.14.basis_ref, f32[44,1024]{1,0:T(8,128)S(1)} %get-tuple-element.15.image_ref), custom_call_target="tpu_custom_call" | custom-call | tf_op jit(solution)/shard_map/pallas_call | solution.py:204
  29.5 0.3 shard_map.91
  29.8 10.8 %all_to_all.5.parts_ref = f32[32,4,128]{2,1,0:T(4,128)S(1)} all-to-all(f32[32,4,128]{2,1,0:T(4,128)S(1)} %get-tuple-element.22), channel_id=1, replica_groups=mesh['row'=8,'col'=4] {'row','col'}, dimensions={0} | all-to-all | bytes 131072 | tf_op jit(solution)/shard_map/all_to_all | solution.py:318
  40.6 1.1 %shard_map.92 = (f32[48,48]{1,0:T(8,128)}, f32[48,1024]{1,0:T(8,128)}, f32[48,1024]{1,0:T(8,128)}) custom-call(f32[48,48]{1,0:T(8,128)S(1)} %shard_map.88.inverse_ref, f32[48,1024]{1,0:T(8,128)S(1)} %get-tuple-element.18.basis_new_ref, f32[48,1024]{1,0:T(8,128)S(1)} %get-tuple-element.19.image_start_ref, f32[4,1024]{1,0:T(4,128)S(1)} %get-tuple-element.20.image_ref, ...), custom_call_target="tpu_custom_call" | custom-call | tf_op jit(solution)/shard_map/pallas_call | solution.py:204
  (34 shorter events, 0.4 us)
Async XLA Ops:
  0.6 14.0 %copy-start = (bf16[24,128,128]{2,1,0:T(8,128)(2,1)S(1)}, bf16[24,128,128]{2,1,0:T(8,128)(2,1)}, u32[]{:S(2)}) copy-start(bf16[24,128,128]{2,1,0:T(8,128)(2,1)} %tiles_ref.3) | copy-start | bytes 2359300
  1.8 5.3 %collective-permute-start.5 = (f32[8,4,128]{2,1,0:T(4,128)S(1)}, f32[8,4,128]{2,1,0:T(4,128)S(1)}, u32[]{:S(2)}, u32[]{:S(2)}) collective-permute-start(f32[8,4,128]{2,1,0:T(4,128)S(1)} %get-tuple-element.13.wide_ref), channel_id=1, source_target_pairs={{0,8},{4,12},{8,0},{12,4},{16,24},{20,28},{24,16},{28,20},{1,9},{5... | collective-permute-start | bytes 49160 | tf_op jit(solution)/shard_map/ppermute | solution.py:221
  5.3 4.1 %collective-permute-start = (f32[20,4,128]{2,1,0:T(4,128)S(1)}, f32[20,4,128]{2,1,0:T(4,128)S(1)}, u32[]{:S(2)}, u32[]{:S(2)}) collective-permute-start(f32[20,4,128]{2,1,0:T(4,128)S(1)} %shard_map.86), channel_id=1, source_target_pairs={{0,1},{1,0},{2,3},{3,2},{4,5},{5,4},{6,7},{7,6},{8,9},{9,8},{10,11... | collective-permute-start | bytes 122888 | tf_op jit(solution)/shard_map/ppermute | solution.py:221
  7.1 5.0 %collective-permute-start.6 = (f32[16,4,128]{2,1,0:T(4,128)S(1)}, f32[16,4,128]{2,1,0:T(4,128)S(1)}, u32[]{:S(2)}, u32[]{:S(2)}) collective-permute-start(f32[16,4,128]{2,1,0:T(4,128)S(1)} %pad_maximum_fusion.7), channel_id=1, source_target_pairs={{0,16},{4,20},{8,24},{12,28},{16,0},{20,4},{24,8},{28,12},{1,17},{... | collective-permute-start | bytes 98312 | tf_op jit(solution)/shard_map/ppermute | solution.py:221
  9.5 5.1 %collective-permute-start.1 = (f32[28,4,128]{2,1,0:T(4,128)S(1)}, f32[28,4,128]{2,1,0:T(4,128)S(1)}, u32[]{:S(2)}, u32[]{:S(2)}) collective-permute-start(f32[28,4,128]{2,1,0:T(4,128)S(1)} %pad_maximum_fusion.4), channel_id=1, source_target_pairs={{0,2},{1,3},{2,0},{3,1},{4,6},{5,7},{6,4},{7,5},{8,10},{9,11},{10,... | collective-permute-start | bytes 172040 | tf_op jit(solution)/shard_map/ppermute | solution.py:221
  12.1 3.5 %collective-permute-start.7 = (f32[32,4,128]{2,1,0:T(4,128)S(1)}, f32[32,4,128]{2,1,0:T(4,128)S(1)}, u32[]{:S(2)}, u32[]{:S(2)}) collective-permute-start(f32[32,4,128]{2,1,0:T(4,128)S(1)} %pad_maximum_fusion.3), channel_id=1, source_target_pairs={{0,4},{4,0},{8,12},{12,8},{16,20},{20,16},{24,28},{28,24},{1,5},{5... | collective-permute-start | bytes 196616 | tf_op jit(solution)/shard_map/ppermute | solution.py:221
  15.6 2.8 %collective-permute-start.2 = (f32[44,4,128]{2,1,0:T(4,128)S(1)}, f32[44,4,128]{2,1,0:T(4,128)S(1)}, u32[]{:S(2)}, u32[]{:S(2)}) collective-permute-start(f32[44,4,128]{2,1,0:T(4,128)S(1)} %pad_maximum_fusion.1), channel_id=1, source_target_pairs={{0,4},{4,0},{8,12},{12,8},{16,20},{20,16},{24,28},{28,24},{1,5},{5... | collective-permute-start | bytes 270344 | tf_op jit(solution)/shard_map/ppermute | solution.py:221
  16.8 4.0 %collective-permute-start.8 = (f32[16,4,128]{2,1,0:T(4,128)S(1)}, f32[16,4,128]{2,1,0:T(4,128)S(1)}, u32[]{:S(2)}, u32[]{:S(2)}) collective-permute-start(f32[16,4,128]{2,1,0:T(4,128)S(1)} %slice.107), channel_id=1, source_target_pairs={{0,1},{1,0},{2,3},{3,2},{4,5},{5,4},{6,7},{7,6},{8,9},{9,8},{10,11... | collective-permute-start | bytes 98312 | tf_op jit(solution)/shard_map/ppermute | solution.py:221
  18.5 5.1 %collective-permute-start.3 = (f32[28,4,128]{2,1,0:T(4,128)S(1)}, f32[28,4,128]{2,1,0:T(4,128)S(1)}, u32[]{:S(2)}, u32[]{:S(2)}) collective-permute-start(f32[28,4,128]{2,1,0:T(4,128)S(1)} %pad_maximum_fusion.5), channel_id=1, source_target_pairs={{0,8},{4,12},{8,0},{12,4},{16,24},{20,28},{24,16},{28,20},{1,9},{5... | collective-permute-start | bytes 172040 | tf_op jit(solution)/shard_map/ppermute | solution.py:221
  20.8 4.7 %collective-permute-start.9 = (f32[8,4,128]{2,1,0:T(4,128)S(1)}, f32[8,4,128]{2,1,0:T(4,128)S(1)}, u32[]{:S(2)}, u32[]{:S(2)}) collective-permute-start(f32[8,4,128]{2,1,0:T(4,128)S(1)} %slice.109), channel_id=1, source_target_pairs={{0,2},{1,3},{2,0},{3,1},{4,6},{5,7},{6,4},{7,5},{8,10},{9,11},{10,... | collective-permute-start | bytes 49160 | tf_op jit(solution)/shard_map/ppermute | solution.py:221
  23.7 4.1 %collective-permute-start.4 = (f32[20,4,128]{2,1,0:T(4,128)S(1)}, f32[20,4,128]{2,1,0:T(4,128)S(1)}, u32[]{:S(2)}, u32[]{:S(2)}) collective-permute-start(f32[20,4,128]{2,1,0:T(4,128)S(1)} %pad_maximum_fusion.6), channel_id=1, source_target_pairs={{0,16},{4,20},{8,24},{12,28},{16,0},{20,4},{24,8},{28,12},{1,17},{... | collective-permute-start | bytes 122888 | tf_op jit(solution)/shard_map/ppermute | solution.py:221

commit v3 on v2

--- a/solution.py
+++ b/solution.py
@@ -11,6 +11,8 @@
 LANES = 128
 SUBLANES = 8
 PANEL = 16
+FLOPS_PER_US = 1.1e9
+BYTES_PER_US = 3.6e6
 VMEM_LIMIT = 32 * 1024 * 1024
 
 
@@ -26,6 +28,12 @@
 
 def multiply(left, right):
     return jnp.dot(left, right, precision=HIGHEST, preferred_element_type=jnp.float32)
+
+
+def pairwise(terms):
+    while len(terms) > 1:
+        terms = [sum(terms[i + 1 : i + 2], terms[i]) for i in range(0, len(terms), 2)]
+    return terms[0]
 
 
 def side_by_side(blocks_ref):
@@ -83,9 +91,8 @@
     return sum(((apart >> (m.bit_length() - 1)) & 1) << j for j, m in enumerate(bits))
 
 
-def tiles_kernel(
-    contract, by_rows, by_cols, n_row, blocks, position_ref, rows_ref, cols_ref, tiles_ref, vecs_ref, sums_ref
-):
+def tiles_product(contract, by_rows, by_cols, n_row, blocks, scalars, tiles_ref, vecs_ref, sums_ref):
+    position_ref, rows_ref, cols_ref = scalars
     sums_ref[...] = jnp.zeros_like(sums_ref)
     row, col = position_ref[0], position_ref[1]
     for t in range(tiles_ref.shape[0]):
@@ -103,8 +110,44 @@
         sums_ref[target] = sums_ref[target] + product
 
 
-def factor_kernel(count, gram_ref, inverse_ref):
-    gram = jnp.concatenate([gram_ref[i] for i in range(gram_ref.shape[0])], axis=0)
+def backward_kernel(by_rows, by_cols, n_row, blocks, n_got, _, *refs):
+    scalars, tiles_ref, own_ref = refs[:3], refs[3], refs[4]
+    got_refs = refs[5 : 5 + n_got]
+    kept_ref, sent_ref, vecs_ref, sums_ref = refs[5 + n_got :]
+    for p, ref in enumerate([own_ref, *got_refs]):
+        vecs_ref[p * blocks : (p + 1) * blocks] = ref[:blocks]
+    tiles_product(0, by_rows, by_cols, n_row, blocks, scalars, tiles_ref, vecs_ref, sums_ref)
+    half = kept_ref.shape[0]
+    kept_ref[...] = sums_ref[:half]
+    sent_ref[:half] = sums_ref[half:]
+    sent_ref[half:] = pairwise([ref[blocks:] for ref in (own_ref, *got_refs)])
+
+
+def forward_kernel(by_rows, by_cols, n_row, blocks, n_got, *refs):
+    scalars, tiles_ref = refs[:3], refs[3]
+    got_refs = refs[4 : 4 + n_got]
+    *piece_refs, vecs_ref, sums_ref = refs[4 + n_got :]
+    at = 0
+    for ref in got_refs:
+        vecs_ref[at : at + ref.shape[0]] = ref[...]
+        at += ref.shape[0]
+    tiles_product(1, by_rows, by_cols, n_row, blocks, scalars, tiles_ref, vecs_ref, sums_ref)
+    for p, ref in enumerate(piece_refs):
+        ref[...] = sums_ref[p * blocks : (p + 1) * blocks]
+
+
+def fold_kernel(_, kept_ref, sent_ref, got_ref, kept_next_ref, sent_next_ref):
+    size, half = kept_ref.shape[0], kept_next_ref.shape[0]
+    kept_next_ref[...] = kept_ref[:half] + got_ref[:half]
+    sent_next_ref[:half] = kept_ref[half:] + got_ref[half:size]
+    sent_next_ref[half:] = sent_ref[size:] + got_ref[size:]
+
+
+def factor_kernel(count, blocks, *refs):
+    sent_ref, got_ref, inverse_ref, gram_ref = refs[-4:]
+    summed = sent_ref[blocks:] + got_ref[blocks:]
+    gram = jnp.concatenate([summed[i] for i in range(summed.shape[0])], axis=0)
+    gram_ref[...] = gram
     row_id = lax.broadcasted_iota(jnp.int32, (count, LANES), 0)
     lane_id = lax.broadcasted_iota(jnp.int32, (count, LANES), 1)
     identity = jnp.where(lane_id == row_id + count, 1.0, 0.0)
@@ -151,14 +194,15 @@
     count, old = inverse.shape[0], image_ref.shape[0]
     basis_new_ref[...] = multiply(inverse, basis_ref[...])
     image_start_ref[...] = multiply(inverse[:, :old], image_ref[...])
-    gram = jnp.concatenate([gram_ref[i] for i in range(gram_ref.shape[0])], axis=0)
-    coupling = gram[:, count : count + old]
+    coupling = gram_ref[:, count : count + old]
     start_ref[...] = contract_last(multiply(inverse, coupling), inverse[:, :old])
 
 
-def image_kernel(scale, basis_new_ref, rows_ref, cols_ref, image_ref, part_ref):
-    summed = [rows_ref[b] + cols_ref[b] for b in range(rows_ref.shape[0])]
-    image = jnp.concatenate(summed, axis=1)
+def image_kernel(scale, basis_new_ref, *refs):
+    *sums_refs, image_ref, part_ref = refs
+    blocks = sums_refs[0].shape[0]
+    summed = pairwise([ref[:blocks] for ref in sums_refs])
+    image = jnp.concatenate([summed[b] for b in range(summed.shape[0])], axis=1)
     image_ref[...] = image
     vecs, count = image.shape[0], basis_new_ref.shape[0]
     part = contract_last(image, basis_new_ref[...]) * scale
@@ -194,7 +238,7 @@
     projected_copy.wait()
 
 
-def call(kernel, outs, *args, smem=0, from_hbm=False, to_hbm=False, scratch=(), flops=0):
+def call(kernel, outs, *args, time=0.0, after=0, smem=0, from_hbm=False, to_hbm=False, scratch=()):
     operand = pl.BlockSpec(memory_space=pltpu.HBM if from_hbm else pltpu.VMEM)
     result = pl.BlockSpec(memory_space=pltpu.HBM if to_hbm else pltpu.VMEM)
     scalars = pl.BlockSpec(memory_space=pltpu.SMEM)
@@ -204,11 +248,13 @@
     return pl.pallas_call(
         kernel,
         out_shape=outs,
-        in_specs=[scalars] * smem + [operand] * (len(args) - smem),
+        in_specs=[operand] * after + [scalars] * smem + [operand] * (len(args) - smem - after),
         out_specs=[result] * len(outs),
         scratch_shapes=scratch,
         compiler_params=pltpu.CompilerParams(vmem_limit_bytes=VMEM_LIMIT),
-        cost_estimate=pl.CostEstimate(flops=flops, bytes_accessed=0, transcendentals=0),
+        cost_estimate=pl.CostEstimate(
+            flops=int(time * FLOPS_PER_US), bytes_accessed=int(time * BYTES_PER_US), transcendentals=0
+        ),
     )(*args)
 
 
@@ -232,9 +278,7 @@
     scale = 1.0 / float(width * n_row * n_col)
     row_bits, col_bits = bits_of(n_row), bits_of(n_col)
     gather_row = row_bits[1:] + row_bits[:1]
-    gather_col = col_bits
     scatter_row = row_bits
-    scatter_col = col_bits
     grams = count // vecs
     position = jnp.stack([row, col])
 
@@ -247,6 +291,7 @@
         image_old,
         tile_rows,
         tile_cols,
+        time=0.0,
         from_hbm=True,
         scratch=[
             pltpu.VMEM((vecs, width), trial_vectors.dtype),
@@ -254,52 +299,75 @@
             pltpu.SemaphoreType.DMA((5,)),
         ],
     )
-    col_vecs = wide
+    col_got, payloads = [wide], []
     for m in gather_row:
-        col_vecs = jnp.concatenate([col_vecs, swap(col_vecs, "row", m)], axis=0)
-    (sent,) = call(
+        payloads.append(jnp.concatenate(col_got, axis=0))
+        col_got.append(swap(payloads[-1], "row", m))
+    (own,) = call(
         functools.partial(gram_kernel, scale),
         [(blocks + grams, vecs, LANES)],
         wide,
         basis_all,
         image_kept,
     )
-    for m in gather_col:
-        size = sent.shape[0] - grams
-        got = swap(sent, "col", m)
-        gram = sent[size:] + got[size:]
-        sent = jnp.concatenate([sent[:size], got[:size], gram], axis=0)
-
-    (col_sums,) = call(
-        functools.partial(tiles_kernel, 0, gather_col, scatter_row[::-1], n_row, blocks),
-        [(blocks * n_row, vecs, tile_size)],
+    row_got = [swap(own, "col", m) for m in range(1, n_col)]
+
+    half = blocks * n_row // 2
+    kept, sent = call(
+        functools.partial(
+            backward_kernel, col_bits, scatter_row[::-1], n_row, blocks, len(row_got)
+        ),
+        [(half, vecs, tile_size), (half + grams, vecs, tile_size)],
+        payloads[1],
         position,
         rows_kept,
         cols_kept,
         tile_blocks,
-        sent,
+        own,
+        *row_got,
+        after=1,
         smem=3,
-    )
-    (row_sums,) = call(
-        functools.partial(tiles_kernel, 1, scatter_col[::-1], gather_row, n_row, blocks),
-        [(blocks * n_col, vecs, tile_size)],
+        scratch=[
+            pltpu.VMEM((blocks * n_col, vecs, tile_size), jnp.float32),
+            pltpu.VMEM((blocks * n_row, vecs, tile_size), jnp.float32),
+        ],
+    )
+    forward = call(
+        functools.partial(forward_kernel, col_bits, gather_row, n_row, blocks, len(col_got)),
+        [(blocks, vecs, tile_size)] * n_col,
         position,
         rows_kept,
         cols_kept,
         tile_blocks,
-        col_vecs,
+        *col_got,
         smem=3,
-    )
-    for m in scatter_row:
-        half = col_sums.shape[0] // 2
-        got = swap(jnp.concatenate([col_sums[half:], gram], axis=0), "row", m)
-        col_sums = col_sums[:half] + got[:half]
-        gram = gram + got[half:]
-    for m in scatter_col:
-        half = row_sums.shape[0] // 2
-        row_sums = row_sums[:half] + swap(row_sums[half:], "col", m)
-
-    (inverse,) = call(functools.partial(factor_kernel, count), [(count, count)], gram)
+        scratch=[
+            pltpu.VMEM((blocks * n_row, vecs, tile_size), jnp.float32),
+            pltpu.VMEM((blocks * n_col, vecs, tile_size), jnp.float32),
+        ],
+    )
+    row_parts = [forward[0]] + [swap(part, "col", m) for m, part in enumerate(forward) if m]
+    for m in scatter_row[:-1]:
+        half //= 2
+        kept, sent = call(
+            fold_kernel,
+            [(half, vecs, tile_size), (half + grams, vecs, tile_size)],
+            forward[0] if m == scatter_row[-2] else wide,
+            kept,
+            sent,
+            swap(sent, "row", m),
+        )
+    got = swap(sent, "row", scatter_row[-1])
+    col_parts = [kept, got]
+
+    inverse, gram = call(
+        functools.partial(factor_kernel, count, blocks),
+        [(count, count), (count, LANES)],
+        row_parts[-1],
+        sent,
+        got,
+        time=1.1,
+    )
     basis_new, image_start, start = call(
         basis_kernel,
         [(count, width), (count, width), (count, count)],
@@ -307,13 +375,15 @@
         gram,
         basis_all,
         image_kept,
+        time=0.7,
     )
     image, part = call(
         functools.partial(image_kernel, scale),
         [(vecs, width), (n_row * n_col, vecs, LANES)],
         basis_new,
-        row_sums,
-        col_sums,
+        *row_parts,
+        *col_parts,
+        time=0.0,
     )
     parts = lax.all_to_all(part, ("row", "col"), split_axis=0, concat_axis=0, tiled=True)
     return call(

time: 41.9 us -> 40.3 us (0.962)
  blocking collectives: 10.8 us -> 9.42 us
    all_to_all x1, blocking collectives: 10.8 us -> 9.42 us  [local(): lax.all_to_all(part, ('row', 'col'), split_axis=0, concat_axis=0, tiled=T...]
    ppermute x10 -> x12, starting transfers between devices: 15.9 us -> 16.2 us  [swap(): return lax.ppermute(array, axis, [(i, i ^ mask) for i in range(size)])]
    ppermute x10 -> x12, waiting for transfers between devices: 7.07 us -> 6.88 us  [swap(): return lax.ppermute(array, axis, [(i, i ^ mask) for i in range(size)])]
    pallas_call x8 -> x10, Pallas kernels: 6.7 us -> 6.77 us  [call(): pl.pallas_call(kernel, out_shape=outs, in_specs=[operand] * after + [scal...]
  transfers between devices with their start and end apart: 10 -> 12, of which waited for: 5 -> 5; matrix products, arithmetic and copies ran while one was open for 1% -> 0% of each run, Pallas kernels for 6% -> 11%
where the time goes in v3:
time: 40.3 us; the launch traced here: 40.1 us
  starting transfers between devices  16.2 us (40%)
  blocking collectives  9.42 us (23%)
  waiting for transfers between devices  6.88 us (17%)
  Pallas kernels  6.77 us (17%)
  between operations  0.73 us (2%)
    ppermute x12, starting transfers between devices, swap(): return lax.ppermute(array, axis, [(i, i ^ mask) for i in range(size)])  16.2 us
    all_to_all x1, blocking collectives, local(): lax.all_to_all(part, ('row', 'col'), split_axis=0, concat_axis=0, tiled=T...  9.42 us
    ppermute x12, waiting for transfers between devices, swap(): return lax.ppermute(array, axis, [(i, i ^ mask) for i in range(size)])  6.88 us
    pallas_call x10, Pallas kernels, call(): pl.pallas_call(kernel, out_shape=outs, in_specs=[operand] * after + [scal...  6.77 us
  transfers between devices with their start and end apart: 12, of which 5 were waited for; matrix products, arithmetic and copies ran while one was open for 0% of the time, Pallas kernels for 11%

profile of v3, /device:TPU:0, one launch (start us, length us, event | category | flops | bytes accessed | tf_op | source)
XLA Modules:
  0.0 40.1 jit_solution(14682202432678056509)
XLA Ops:
  0.6 1.2 %shard_map.85 = (f32[8,4,128]{2,1,0:T(4,128)S(1)}, f32[48,1024]{1,0:T(8,128)S(1)}, f32[44,1024]{1,0:T(8,128)S(1)}, s32[24]{0:T(128)S(1)}, s32[24]{0:T(128)S(1)}) custom-call(bf16[4,1024]{1,0:T(4,128)(2,1)} %trial_hbm.1, f32[44,1024]{1,0:T(8,128)} %basis_hbm.1, f32[44,1024]{1,0:T(8,128)} %image_hbm.1, s32[24]{0:T(128)} %rows_hbm.1, s32[24]{0:T(128)} %cols_hbm.1), custom_call_target="tpu_custom_call" | custom-call | tf_op jit(solution)/shard_map/pallas_call | solution.py:248
  1.8 3.0 %collective-permute-start = (f32[8,4,128]{2,1,0:T(4,128)S(1)}, f32[8,4,128]{2,1,0:T(4,128)S(1)}, u32[]{:S(2)}, u32[]{:S(2)}) collective-permute-start(f32[8,4,128]{2,1,0:T(4,128)S(1)} %get-tuple-element.27.refs_4_.wide_ref._), channel_id=1, source_target_pairs={{0,8},{4,12},{8,0},{12,4},{16,24},{20,28},{24,16},{28,20},{1,9},{5... | collective-permute-start | bytes 49160 | tf_op jit(solution)/shard_map/ppermute | solution.py:267
  4.8 0.5 %shard_map.87.refs_4_ = f32[20,4,128]{2,1,0:T(4,128)S(1)} custom-call(f32[8,4,128]{2,1,0:T(4,128)S(1)} %get-tuple-element.27.refs_4_.wide_ref._, f32[48,1024]{1,0:T(8,128)S(1)} %get-tuple-element.30.basis_ref, f32[44,1024]{1,0:T(8,128)S(1)} %get-tuple-element.31.image_ref), custom_call_target="tpu_custom_call" | custom-call | tf_op jit(solution)/shard_map/pallas_call | solution.py:248
  5.3 3.7 %collective-permute-start.6 = (f32[20,4,128]{2,1,0:T(4,128)S(1)}, f32[20,4,128]{2,1,0:T(4,128)S(1)}, u32[]{:S(2)}, u32[]{:S(2)}) collective-permute-start(f32[20,4,128]{2,1,0:T(4,128)S(1)} %shard_map.87.refs_4_), channel_id=1, source_target_pairs={{0,3},{1,2},{2,1},{3,0},{4,7},{5,6},{6,5},{7,4},{8,11},{9,10},{10,... | collective-permute-start | bytes 122888 | tf_op jit(solution)/shard_map/ppermute | solution.py:267
  9.0 0.8 %collective-permute-start.4 = (f32[20,4,128]{2,1,0:T(4,128)S(1)}, f32[20,4,128]{2,1,0:T(4,128)S(1)}, u32[]{:S(2)}, u32[]{:S(2)}) collective-permute-start(f32[20,4,128]{2,1,0:T(4,128)S(1)} %shard_map.87.refs_4_), channel_id=1, source_target_pairs={{0,1},{1,0},{2,3},{3,2},{4,5},{5,4},{6,7},{7,6},{8,9},{9,8},{10,11... | collective-permute-start | bytes 122888 | tf_op jit(solution)/shard_map/ppermute | solution.py:267
  9.8 1.6 %collective-permute-start.1 = (f32[16,4,128]{2,1,0:T(4,128)S(1)}, f32[16,4,128]{2,1,0:T(4,128)S(1)}, u32[]{:S(2)}, u32[]{:S(2)}) collective-permute-start(f32[16,4,128]{2,1,0:T(4,128)S(1)} %constant_dynamic-update-slice_fusion._), channel_id=1, source_target_pairs={{0,16},{4,20},{8,24},{12,28},{16,0},{20,4},{24,8},{28,12},{1,17},{... | collective-permute-start | bytes 98312 | tf_op jit(solution)/shard_map/ppermute | solution.py:267
  11.5 0.2 collective-permute-done.6.refs_7_
  11.6 2.3 %collective-permute-done.5.refs_6_ = f32[20,4,128]{2,1,0:T(4,128)S(1)} collective-permute-done((f32[20,4,128]{2,1,0:T(4,128)S(1)}, f32[20,4,128]{2,1,0:T(4,128)S(1)}, u32[]{:S(2)}, u32[]{:S(2)}) %collective-permute-start.5) | collective-permute-done | bytes 40992 | tf_op jit(solution)/shard_map/ppermute | solution.py:267
  13.9 0.9 %shard_map.88 = (f32[32,4,128]{2,1,0:T(4,128)S(1)}, f32[44,4,128]{2,1,0:T(4,128)S(1)}) custom-call(f32[16,4,128]{2,1,0:T(4,128)S(1)} %constant_dynamic-update-slice_fusion._, s32[2]{0:T(128)S(1)} %pad_add_fusion.refs_0_, s32[24]{0:T(128)S(1)} %get-tuple-element.25.refs_1_, s32[24]{0:T(128)S(1)} %get-tuple-element.26.refs_2_, ...), custom_call_target="tpu_custom_call" | custom-call | tf_op jit(solution)/shard_map/pallas_call | solution.py:248
  14.9 0.6 %collective-permute-start.2 = (f32[32,4,128]{2,1,0:T(4,128)S(1)}, f32[32,4,128]{2,1,0:T(4,128)S(1)}, u32[]{:S(2)}, u32[]{:S(2)}) collective-permute-start(f32[32,4,128]{2,1,0:T(4,128)S(1)} %pad_maximum_fusion), channel_id=1, source_target_pairs={{0,4},{4,0},{8,12},{12,8},{16,20},{20,16},{24,28},{28,24},{1,5},{5... | collective-permute-start | bytes 196616 | tf_op jit(solution)/shard_map/ppermute | solution.py:267
  15.5 0.7 %collective-permute-done.7.got_ref = f32[44,4,128]{2,1,0:T(4,128)S(1)} collective-permute-done((f32[44,4,128]{2,1,0:T(4,128)S(1)}, f32[44,4,128]{2,1,0:T(4,128)S(1)}, u32[]{:S(2)}, u32[]{:S(2)}) %collective-permute-start.7) | collective-permute-done | bytes 90144 | tf_op jit(solution)/shard_map/ppermute | solution.py:267
  16.2 0.6 %collective-permute-start.8 = (f32[28,4,128]{2,1,0:T(4,128)S(1)}, f32[28,4,128]{2,1,0:T(4,128)S(1)}, u32[]{:S(2)}, u32[]{:S(2)}) collective-permute-start(f32[28,4,128]{2,1,0:T(4,128)S(1)} %get-tuple-element.35.sent_ref), channel_id=1, source_target_pairs={{0,8},{4,12},{8,0},{12,4},{16,24},{20,28},{24,16},{28,20},{1,9},{5... | collective-permute-start | bytes 172040 | tf_op jit(solution)/shard_map/ppermute | solution.py:267
  16.8 1.1 %shard_map.86 = (f32[8,4,128]{2,1,0:T(4,128)S(1)}, f32[8,4,128]{2,1,0:T(4,128)S(1)}, f32[8,4,128]{2,1,0:T(4,128)S(1)}, f32[8,4,128]{2,1,0:T(4,128)S(1)}) custom-call(s32[2]{0:T(128)S(1)} %pad_add_fusion.refs_0_, s32[24]{0:T(128)S(1)} %get-tuple-element.25.refs_1_, s32[24]{0:T(128)S(1)} %get-tuple-element.26.refs_2_, bf16[24,128,128]{2,1,0:T(8,128)(2,1)S(1)} %copy-done, ...), custom_call_target="tpu_custom_call" | custom-call | tf_op jit(solution)/shard_map/pallas_call | solution.py:248
  17.9 2.6 %collective-permute-done.8.got_ref = f32[28,4,128]{2,1,0:T(4,128)S(1)} collective-permute-done((f32[28,4,128]{2,1,0:T(4,128)S(1)}, f32[28,4,128]{2,1,0:T(4,128)S(1)}, u32[]{:S(2)}, u32[]{:S(2)}) %collective-permute-start.8) | collective-permute-done | bytes 57376 | tf_op jit(solution)/shard_map/ppermute | solution.py:267
  20.5 1.6 %collective-permute-start.9 = (f32[20,4,128]{2,1,0:T(4,128)S(1)}, f32[20,4,128]{2,1,0:T(4,128)S(1)}, u32[]{:S(2)}, u32[]{:S(2)}) collective-permute-start(f32[20,4,128]{2,1,0:T(4,128)S(1)} %get-tuple-element.36.refs_1_), channel_id=1, source_target_pairs={{0,16},{4,20},{8,24},{12,28},{16,0},{20,4},{24,8},{28,12},{1,17},{... | collective-permute-start | bytes 122888 | tf_op jit(solution)/shard_map/ppermute | solution.py:267
  22.0 1.5 %collective-permute-start.3 = (f32[8,4,128]{2,1,0:T(4,128)S(1)}, f32[8,4,128]{2,1,0:T(4,128)S(1)}, u32[]{:S(2)}, u32[]{:S(2)}) collective-permute-start(f32[8,4,128]{2,1,0:T(4,128)S(1)} %get-tuple-element.28), channel_id=1, source_target_pairs={{0,3},{1,2},{2,1},{3,0},{4,7},{5,6},{6,5},{7,4},{8,11},{9,10},{10,... | collective-permute-start | bytes 49160 | tf_op jit(solution)/shard_map/ppermute | solution.py:267
  23.5 1.1 %collective-permute-start.10 = (f32[8,4,128]{2,1,0:T(4,128)S(1)}, f32[8,4,128]{2,1,0:T(4,128)S(1)}, u32[]{:S(2)}, u32[]{:S(2)}) collective-permute-start(f32[8,4,128]{2,1,0:T(4,128)S(1)} %get-tuple-element.41), channel_id=1, source_target_pairs={{0,1},{1,0},{2,3},{3,2},{4,5},{5,4},{6,7},{7,6},{8,9},{9,8},{10,11... | collective-permute-start | bytes 49160 | tf_op jit(solution)/shard_map/ppermute | solution.py:267
  24.6 1.8 %collective-permute-start.11 = (f32[8,4,128]{2,1,0:T(4,128)S(1)}, f32[8,4,128]{2,1,0:T(4,128)S(1)}, u32[]{:S(2)}, u32[]{:S(2)}) collective-permute-start(f32[8,4,128]{2,1,0:T(4,128)S(1)} %get-tuple-element.42), channel_id=1, source_target_pairs={{0,2},{1,3},{2,0},{3,1},{4,6},{5,7},{6,4},{7,5},{8,10},{9,11},{10,... | collective-permute-start | bytes 49160 | tf_op jit(solution)/shard_map/ppermute | solution.py:267
  26.4 1.1 %collective-permute-done.3.refs_0_.refs_3_ = f32[8,4,128]{2,1,0:T(4,128)S(1)} collective-permute-done((f32[8,4,128]{2,1,0:T(4,128)S(1)}, f32[8,4,128]{2,1,0:T(4,128)S(1)}, u32[]{:S(2)}, u32[]{:S(2)}) %collective-permute-start.3) | collective-permute-done | bytes 16416 | tf_op jit(solution)/shard_map/ppermute | solution.py:267
  27.6 1.1 %shard_map.91 = (f32[48,48]{1,0:T(8,128)S(1)}, f32[48,128]{1,0:T(8,128)S(1)}) custom-call(f32[8,4,128]{2,1,0:T(4,128)S(1)} %collective-permute-done.3.refs_0_.refs_3_, f32[20,4,128]{2,1,0:T(4,128)S(1)} %get-tuple-element.36.refs_1_, f32[20,4,128]{2,1,0:T(4,128)S(1)} %collective-permute-done.9.refs_2_.refs_5_), custom_call_target="tpu_custom_call" | custom-call | flops 1210000000 | bytes 3960000 | tf_op jit(solution)/shard_map/pallas_call | solution.py:248
  28.6 0.6 %shard_map.92 = (f32[48,1024]{1,0:T(8,128)S(1)}, f32[48,1024]{1,0:T(8,128)S(1)}, f32[48,48]{1,0:T(8,128)S(1)}) custom-call(f32[48,48]{1,0:T(8,128)S(1)} %get-tuple-element.37.inverse_ref, f32[48,128]{1,0:T(8,128)S(1)} %get-tuple-element.38.gram_ref, f32[48,1024]{1,0:T(8,128)S(1)} %get-tuple-element.30.basis_ref, f32[44,1024]{1,0:T(8,128)S(1)} %get-tuple-element.31.image_ref), custom_call_target="tpu_custom_call" | custom-call | flops 770000000 | bytes 2520000 | tf_op jit(solution)/shard_map/pallas_call | solution.py:248
  29.3 0.3 shard_map.93
  29.6 9.4 %all_to_all.5.parts_ref = f32[32,4,128]{2,1,0:T(4,128)S(1)} all-to-all(f32[32,4,128]{2,1,0:T(4,128)S(1)} %get-tuple-element.46), channel_id=1, replica_groups=mesh['row'=8,'col'=4] {'row','col'}, dimensions={0} | all-to-all | bytes 131072 | tf_op jit(solution)/shard_map/all_to_all | solution.py:388
  39.0 1.1 %shard_map.94 = (f32[48,48]{1,0:T(8,128)}, f32[48,1024]{1,0:T(8,128)}, f32[48,1024]{1,0:T(8,128)}) custom-call(f32[48,48]{1,0:T(8,128)S(1)} %get-tuple-element.37.inverse_ref, f32[48,1024]{1,0:T(8,128)S(1)} %get-tuple-element.39.basis_new_ref, f32[48,1024]{1,0:T(8,128)S(1)} %get-tuple-element.40.image_start_ref, f32[4,1024]{1,0:T(4,128)S(1)} %get-tuple-element.44.image_ref, ...), custom_call_target="tpu_custom_call" | custom-call | tf_op jit(solution)/shard_map/pallas_call | solution.py:248
  (17 shorter events, 0.3 us)
Async XLA Ops:
  0.6 13.3 %copy-start = (bf16[24,128,128]{2,1,0:T(8,128)(2,1)S(1)}, bf16[24,128,128]{2,1,0:T(8,128)(2,1)}, u32[]{:S(2)}) copy-start(bf16[24,128,128]{2,1,0:T(8,128)(2,1)} %refs_3_.3) | copy-start | bytes 2359300
  1.8 8.0 %collective-permute-start = (f32[8,4,128]{2,1,0:T(4,128)S(1)}, f32[8,4,128]{2,1,0:T(4,128)S(1)}, u32[]{:S(2)}, u32[]{:S(2)}) collective-permute-start(f32[8,4,128]{2,1,0:T(4,128)S(1)} %get-tuple-element.27.refs_4_.wide_ref._), channel_id=1, source_target_pairs={{0,8},{4,12},{8,0},{12,4},{16,24},{20,28},{24,16},{28,20},{1,9},{5... | collective-permute-start | bytes 49160 | tf_op jit(solution)/shard_map/ppermute | solution.py:267
  5.3 6.3 %collective-permute-start.6 = (f32[20,4,128]{2,1,0:T(4,128)S(1)}, f32[20,4,128]{2,1,0:T(4,128)S(1)}, u32[]{:S(2)}, u32[]{:S(2)}) collective-permute-start(f32[20,4,128]{2,1,0:T(4,128)S(1)} %shard_map.87.refs_4_), channel_id=1, source_target_pairs={{0,3},{1,2},{2,1},{3,0},{4,7},{5,6},{6,5},{7,4},{8,11},{9,10},{10,... | collective-permute-start | bytes 122888 | tf_op jit(solution)/shard_map/ppermute | solution.py:267
  9.0 4.9 %collective-permute-start.5 = (f32[20,4,128]{2,1,0:T(4,128)S(1)}, f32[20,4,128]{2,1,0:T(4,128)S(1)}, u32[]{:S(2)}, u32[]{:S(2)}) collective-permute-start(f32[20,4,128]{2,1,0:T(4,128)S(1)} %shard_map.87.refs_4_), channel_id=1, source_target_pairs={{0,2},{1,3},{2,0},{3,1},{4,6},{5,7},{6,4},{7,5},{8,10},{9,11},{10,... | collective-permute-start | bytes 122888 | tf_op jit(solution)/shard_map/ppermute | solution.py:267
  9.0 4.9 %collective-permute-start.4 = (f32[20,4,128]{2,1,0:T(4,128)S(1)}, f32[20,4,128]{2,1,0:T(4,128)S(1)}, u32[]{:S(2)}, u32[]{:S(2)}) collective-permute-start(f32[20,4,128]{2,1,0:T(4,128)S(1)} %shard_map.87.refs_4_), channel_id=1, source_target_pairs={{0,1},{1,0},{2,3},{3,2},{4,5},{5,4},{6,7},{7,6},{8,9},{9,8},{10,11... | collective-permute-start | bytes 122888 | tf_op jit(solution)/shard_map/ppermute | solution.py:267
  9.8 5.1 %collective-permute-start.1 = (f32[16,4,128]{2,1,0:T(4,128)S(1)}, f32[16,4,128]{2,1,0:T(4,128)S(1)}, u32[]{:S(2)}, u32[]{:S(2)}) collective-permute-start(f32[16,4,128]{2,1,0:T(4,128)S(1)} %constant_dynamic-update-slice_fusion._), channel_id=1, source_target_pairs={{0,16},{4,20},{8,24},{12,28},{16,0},{20,4},{24,8},{28,12},{1,17},{... | collective-permute-start | bytes 98312 | tf_op jit(solution)/shard_map/ppermute | solution.py:267
  14.8 1.4 %collective-permute-start.7 = (f32[44,4,128]{2,1,0:T(4,128)S(1)}, f32[44,4,128]{2,1,0:T(4,128)S(1)}, u32[]{:S(2)}, u32[]{:S(2)}) collective-permute-start(f32[44,4,128]{2,1,0:T(4,128)S(1)} %get-tuple-element.33.sent_ref), channel_id=1, source_target_pairs={{0,4},{4,0},{8,12},{12,8},{16,20},{20,16},{24,28},{28,24},{1,5},{5... | collective-permute-start | bytes 270344 | tf_op jit(solution)/shard_map/ppermute | solution.py:267
  14.9 1.9 %collective-permute-start.2 = (f32[32,4,128]{2,1,0:T(4,128)S(1)}, f32[32,4,128]{2,1,0:T(4,128)S(1)}, u32[]{:S(2)}, u32[]{:S(2)}) collective-permute-start(f32[32,4,128]{2,1,0:T(4,128)S(1)} %pad_maximum_fusion), channel_id=1, source_target_pairs={{0,4},{4,0},{8,12},{12,8},{16,20},{20,16},{24,28},{28,24},{1,5},{5... | collective-permute-start | bytes 196616 | tf_op jit(solution)/shard_map/ppermute | solution.py:267
  16.2 4.2 %collective-permute-start.8 = (f32[28,4,128]{2,1,0:T(4,128)S(1)}, f32[28,4,128]{2,1,0:T(4,128)S(1)}, u32[]{:S(2)}, u32[]{:S(2)}) collective-permute-start(f32[28,4,128]{2,1,0:T(4,128)S(1)} %get-tuple-element.35.sent_ref), channel_id=1, source_target_pairs={{0,8},{4,12},{8,0},{12,4},{16,24},{20,28},{24,16},{28,20},{1,9},{5... | collective-permute-start | bytes 172040 | tf_op jit(solution)/shard_map/ppermute | solution.py:267
  20.5 7.1 %collective-permute-start.9 = (f32[20,4,128]{2,1,0:T(4,128)S(1)}, f32[20,4,128]{2,1,0:T(4,128)S(1)}, u32[]{:S(2)}, u32[]{:S(2)}) collective-permute-start(f32[20,4,128]{2,1,0:T(4,128)S(1)} %get-tuple-element.36.refs_1_), channel_id=1, source_target_pairs={{0,16},{4,20},{8,24},{12,28},{16,0},{20,4},{24,8},{28,12},{1,17},{... | collective-permute-start | bytes 122888 | tf_op jit(solution)/shard_map/ppermute | solution.py:267
  22.0 5.5 %collective-permute-start.3 = (f32[8,4,128]{2,1,0:T(4,128)S(1)}, f32[8,4,128]{2,1,0:T(4,128)S(1)}, u32[]{:S(2)}, u32[]{:S(2)}) collective-permute-start(f32[8,4,128]{2,1,0:T(4,128)S(1)} %get-tuple-element.28), channel_id=1, source_target_pairs={{0,3},{1,2},{2,1},{3,0},{4,7},{5,6},{6,5},{7,4},{8,11},{9,10},{10,... | collective-permute-start | bytes 49160 | tf_op jit(solution)/shard_map/ppermute | solution.py:267
  23.5 5.8 %collective-permute-start.10 = (f32[8,4,128]{2,1,0:T(4,128)S(1)}, f32[8,4,128]{2,1,0:T(4,128)S(1)}, u32[]{:S(2)}, u32[]{:S(2)}) collective-permute-start(f32[8,4,128]{2,1,0:T(4,128)S(1)} %get-tuple-element.41), channel_id=1, source_target_pairs={{0,1},{1,0},{2,3},{3,2},{4,5},{5,4},{6,7},{7,6},{8,9},{9,8},{10,11... | collective-permute-start | bytes 49160 | tf_op jit(solution)/shard_map/ppermute | solution.py:267
  24.6 4.7 %collective-permute-start.11 = (f32[8,4,128]{2,1,0:T(4,128)S(1)}, f32[8,4,128]{2,1,0:T(4,128)S(1)}, u32[]{:S(2)}, u32[]{:S(2)}) collective-permute-start(f32[8,4,128]{2,1,0:T(4,128)S(1)} %get-tuple-element.42), channel_id=1, source_target_pairs={{0,2},{1,3},{2,0},{3,1},{4,6},{5,7},{6,4},{7,5},{8,10},{9,11},{10,... | collective-permute-start | bytes 49160 | tf_op jit(solution)/shard_map/ppermute | solution.py:267

commit v4 on v3

--- a/solution.py
+++ b/solution.py
@@ -11,23 +11,47 @@
 LANES = 128
 SUBLANES = 8
 PANEL = 16
+GROUP = 2
 FLOPS_PER_US = 1.1e9
 BYTES_PER_US = 3.6e6
 VMEM_LIMIT = 32 * 1024 * 1024
 
 
+def three_parts(wide):
+    high = wide.astype(jnp.bfloat16)
+    rest = wide - high.astype(jnp.float32)
+    middle = rest.astype(jnp.bfloat16)
+    return high, middle, (rest - middle.astype(jnp.float32)).astype(jnp.bfloat16)
+
+
+def product(left, right, contract):
+    rows = left.shape[0]
+    padding = -rows % 16
+    if padding:
+        left = jnp.concatenate([left, jnp.zeros((padding, left.shape[1]), left.dtype)], axis=0)
+    size = rows + padding
+    high, middle, low = three_parts(left)
+    stacked = jnp.concatenate([high, middle, low], axis=0)
+    sums = [
+        lax.dot_general(
+            stacked[: size * (3 - i)],
+            part,
+            (((1,), (contract,)), ((), ())),
+            preferred_element_type=jnp.float32,
+        )
+        for i, part in enumerate(three_parts(right))
+    ]
+    small = (sums[0][2 * size : 2 * size + rows] + sums[1][size : size + rows]) + sums[2][:rows]
+    middle = sums[0][size : size + rows] + sums[1][:rows]
+    return sums[0][:rows] + (middle + small)
+
+
 def contract_last(left, right):
-    return lax.dot_general(
-        left,
-        right,
-        (((1,), (1,)), ((), ())),
-        precision=HIGHEST,
-        preferred_element_type=jnp.float32,
-    )
+    return product(left, right, 1)
 
 
 def multiply(left, right):
-    return jnp.dot(left, right, precision=HIGHEST, preferred_element_type=jnp.float32)
+    return product(left, right, 0)
 
 
 def pairwise(terms):
@@ -71,11 +95,10 @@
 def gram_kernel(scale, wide_ref, basis_ref, image_ref, sent_ref):
     blocks, vecs = wide_ref.shape[:2]
     basis_all = basis_ref[...]
-    correlation = contract_last(basis_all, basis_all)
-    coupling = contract_last(basis_all, image_ref[...])
-    count = correlation.shape[0]
-    unused = jnp.zeros((count, LANES - count - coupling.shape[1]), jnp.float32)
-    gram = jnp.concatenate([correlation, coupling, unused], axis=1) * scale
+    images = image_ref[...]
+    unused = LANES - basis_all.shape[0] - images.shape[0]
+    filler = jnp.zeros((unused, images.shape[1]), jnp.float32)
+    gram = contract_last(basis_all, jnp.concatenate([basis_all, images, filler], axis=0)) * scale
     sent_ref[:blocks] = wide_ref[...]
     for i in range(sent_ref.shape[0] - blocks):
         sent_ref[blocks + i] = gram[i * vecs : (i + 1) * vecs]
@@ -92,28 +115,36 @@
 
 
 def tiles_product(contract, by_rows, by_cols, n_row, blocks, scalars, tiles_ref, vecs_ref, sums_ref):
-    position_ref, rows_ref, cols_ref = scalars
+    rows_ref, cols_ref = scalars
     sums_ref[...] = jnp.zeros_like(sums_ref)
-    row, col = position_ref[0], position_ref[1]
+    row, col = lax.axis_index("row"), lax.axis_index("col")
+    places = []
     for t in range(tiles_ref.shape[0]):
         row_piece, row_inner = split(rows_ref[t], blocks)
         col_piece, col_inner = split(cols_ref[t] - col * (blocks * n_row), blocks)
         at_row = place(split(row_piece, n_row)[0] ^ col, by_rows) * blocks + row_inner
         at_col = place(col_piece ^ row, by_cols) * blocks + col_inner
-        source, target = (at_col, at_row) if contract else (at_row, at_col)
-        product = lax.dot_general(
-            vecs_ref[source].astype(jnp.bfloat16),
-            tiles_ref[t],
+        places.append((at_col, at_row) if contract else (at_row, at_col))
+    vecs, size = vecs_ref.shape[1:]
+    for t in range(0, len(places), GROUP):
+        group = range(t, min(t + GROUP, len(places)))
+        picked = jnp.concatenate([vecs_ref[places[u][0]] for u in group], axis=0)
+        products = lax.dot_general(
+            picked.astype(jnp.bfloat16),
+            jnp.concatenate([tiles_ref[u] for u in group], axis=1 - contract),
             (((1,), (contract,)), ((), ())),
             preferred_element_type=jnp.float32,
         )
-        sums_ref[target] = sums_ref[target] + product
-
-
-def backward_kernel(by_rows, by_cols, n_row, blocks, n_got, _, *refs):
-    scalars, tiles_ref, own_ref = refs[:3], refs[3], refs[4]
-    got_refs = refs[5 : 5 + n_got]
-    kept_ref, sent_ref, vecs_ref, sums_ref = refs[5 + n_got :]
+        for i, u in enumerate(group):
+            target = places[u][1]
+            own = products[i * vecs : (i + 1) * vecs, i * size : (i + 1) * size]
+            sums_ref[target] = sums_ref[target] + own
+
+
+def backward_kernel(by_rows, by_cols, n_row, blocks, n_got, *refs):
+    scalars, tiles_ref, own_ref = refs[:2], refs[2], refs[3]
+    got_refs = refs[4 : 4 + n_got]
+    kept_ref, sent_ref, vecs_ref, sums_ref = refs[4 + n_got :]
     for p, ref in enumerate([own_ref, *got_refs]):
         vecs_ref[p * blocks : (p + 1) * blocks] = ref[:blocks]
     tiles_product(0, by_rows, by_cols, n_row, blocks, scalars, tiles_ref, vecs_ref, sums_ref)
@@ -124,27 +155,29 @@
 
 
 def forward_kernel(by_rows, by_cols, n_row, blocks, n_got, *refs):
-    scalars, tiles_ref = refs[:3], refs[3]
-    got_refs = refs[4 : 4 + n_got]
-    *piece_refs, vecs_ref, sums_ref = refs[4 + n_got :]
+    scalars, tiles_ref = refs[:2], refs[2]
+    got_refs = refs[3 : 3 + n_got]
+    *piece_refs, vecs_ref, sums_ref = refs[3 + n_got :]
     at = 0
     for ref in got_refs:
         vecs_ref[at : at + ref.shape[0]] = ref[...]
         at += ref.shape[0]
     tiles_product(1, by_rows, by_cols, n_row, blocks, scalars, tiles_ref, vecs_ref, sums_ref)
-    for p, ref in enumerate(piece_refs):
-        ref[...] = sums_ref[p * blocks : (p + 1) * blocks]
-
-
-def fold_kernel(_, kept_ref, sent_ref, got_ref, kept_next_ref, sent_next_ref):
+    at = 0
+    for ref in piece_refs:
+        ref[...] = sums_ref[at : at + ref.shape[0]]
+        at += ref.shape[0]
+
+
+def fold_kernel(kept_ref, sent_ref, got_ref, kept_next_ref, sent_next_ref):
     size, half = kept_ref.shape[0], kept_next_ref.shape[0]
     kept_next_ref[...] = kept_ref[:half] + got_ref[:half]
     sent_next_ref[:half] = kept_ref[half:] + got_ref[half:size]
-    sent_next_ref[half:] = sent_ref[size:] + got_ref[size:]
-
-
-def factor_kernel(count, blocks, *refs):
-    sent_ref, got_ref, inverse_ref, gram_ref = refs[-4:]
+    if sent_next_ref.shape[0] > half:
+        sent_next_ref[half:] = sent_ref[size:] + got_ref[size:]
+
+
+def factor_kernel(count, blocks, sent_ref, got_ref, inverse_ref, gram_ref):
     summed = sent_ref[blocks:] + got_ref[blocks:]
     gram = jnp.concatenate([summed[i] for i in range(summed.shape[0])], axis=0)
     gram_ref[...] = gram
@@ -219,7 +252,10 @@
     vecs = image_ref.shape[0]
     count = inverse_ref.shape[0]
     last = inverse_ref[...][:, count - vecs :]
-    image_new_vmem[...] = image_start_ref[...] + multiply(last, image_ref[...])
+    image_new = image_start_ref[...]
+    for k in range(vecs):
+        image_new = image_new + last[:, k : k + 1] * image_ref[k : k + 1, :]
+    image_new_vmem[...] = image_new
     image_copy = pltpu.make_async_copy(image_new_vmem, image_new_hbm, sems.at[1])
     image_copy.start()
     total = jnp.sum(parts_ref[...], axis=0)
@@ -238,24 +274,31 @@
     projected_copy.wait()
 
 
-def call(kernel, outs, *args, time=0.0, after=0, smem=0, from_hbm=False, to_hbm=False, scratch=()):
+def call(kernel, outs, *args, after=(), time=0.0, smem=0, from_hbm=False, to_hbm=False, scratch=()):
     operand = pl.BlockSpec(memory_space=pltpu.HBM if from_hbm else pltpu.VMEM)
     result = pl.BlockSpec(memory_space=pltpu.HBM if to_hbm else pltpu.VMEM)
     scalars = pl.BlockSpec(memory_space=pltpu.SMEM)
     if from_hbm:
         args = [pltpu.with_memory_space_constraint(arg, pltpu.HBM) for arg in args]
+    result_specs = [scalars if hasattr(o, "dtype") else result for o in outs]
     outs = [o if hasattr(o, "dtype") else jax.ShapeDtypeStruct(o, jnp.float32) for o in outs]
+    n_after = len(after)
+
+    def body(*refs):
+        kernel(*refs[n_after:])
+
     return pl.pallas_call(
-        kernel,
+        body,
         out_shape=outs,
-        in_specs=[operand] * after + [scalars] * smem + [operand] * (len(args) - smem - after),
-        out_specs=[result] * len(outs),
+        in_specs=[operand] * n_after + [scalars] * smem + [operand] * (len(args) - smem),
+        out_specs=result_specs,
         scratch_shapes=scratch,
         compiler_params=pltpu.CompilerParams(vmem_limit_bytes=VMEM_LIMIT),
         cost_estimate=pl.CostEstimate(
             flops=int(time * FLOPS_PER_US), bytes_accessed=int(time * BYTES_PER_US), transcendentals=0
         ),
-    )(*args)
+        name=(kernel.func if hasattr(kernel, "func") else kernel).__name__[:-7],
+    )(*after, *args)
 
 
 def bits_of(size):
@@ -274,24 +317,23 @@
     count = old + vecs
     blocks = width // tile_size
     n_row, n_col = lax.axis_size("row"), lax.axis_size("col")
-    row, col = lax.axis_index("row"), lax.axis_index("col")
     scale = 1.0 / float(width * n_row * n_col)
     row_bits, col_bits = bits_of(n_row), bits_of(n_col)
     gather_row = row_bits[1:] + row_bits[:1]
-    scatter_row = row_bits
+    scatter_row, scatter_col = row_bits, col_bits
     grams = count // vecs
-    position = jnp.stack([row, col])
-
-    places = jax.ShapeDtypeStruct(tile_rows.shape, tile_rows.dtype)
+    tile = (vecs, tile_size)
+
+    places = pltpu.SMEM(tile_rows.shape, tile_rows.dtype)
     wide, basis_all, image_kept, rows_kept, cols_kept = call(
         load_kernel,
-        [(blocks, vecs, tile_size), (count, width), (old, width), places, places],
+        [(blocks, *tile), (count, width), (old, width), places, places],
         trial_vectors,
         basis_old,
         image_old,
         tile_rows,
         tile_cols,
-        time=0.0,
+        time=1.0,
         from_hbm=True,
         scratch=[
             pltpu.VMEM((vecs, width), trial_vectors.dtype),
@@ -299,73 +341,83 @@
             pltpu.SemaphoreType.DMA((5,)),
         ],
     )
-    col_got, payloads = [wide], []
-    for m in gather_row:
-        payloads.append(jnp.concatenate(col_got, axis=0))
-        col_got.append(swap(payloads[-1], "row", m))
     (own,) = call(
         functools.partial(gram_kernel, scale),
-        [(blocks + grams, vecs, LANES)],
+        [(blocks + grams, *tile)],
         wide,
         basis_all,
         image_kept,
+        time=0.5,
     )
     row_got = [swap(own, "col", m) for m in range(1, n_col)]
-
-    half = blocks * n_row // 2
-    kept, sent = call(
+    col_got = [wide]
+    for m in gather_row:
+        col_got.append(swap(jnp.concatenate(col_got, axis=0), "row", m))
+
+    half_row, half_col = blocks * n_row // 2, blocks * n_col // 2
+    col_kept, col_sent = call(
         functools.partial(
             backward_kernel, col_bits, scatter_row[::-1], n_row, blocks, len(row_got)
         ),
-        [(half, vecs, tile_size), (half + grams, vecs, tile_size)],
-        payloads[1],
-        position,
+        [(half_row, *tile), (half_row + grams, *tile)],
         rows_kept,
         cols_kept,
         tile_blocks,
         own,
         *row_got,
-        after=1,
-        smem=3,
+        time=1.0,
+        smem=2,
         scratch=[
-            pltpu.VMEM((blocks * n_col, vecs, tile_size), jnp.float32),
-            pltpu.VMEM((blocks * n_row, vecs, tile_size), jnp.float32),
+            pltpu.VMEM((2 * half_col, *tile), jnp.float32),
+            pltpu.VMEM((2 * half_row, *tile), jnp.float32),
         ],
     )
-    forward = call(
-        functools.partial(forward_kernel, col_bits, gather_row, n_row, blocks, len(col_got)),
-        [(blocks, vecs, tile_size)] * n_col,
-        position,
+    row_kept, row_sent = call(
+        functools.partial(
+            forward_kernel, scatter_col[::-1], gather_row, n_row, blocks, len(col_got)
+        ),
+        [(half_col, *tile)] * 2,
         rows_kept,
         cols_kept,
         tile_blocks,
         *col_got,
-        smem=3,
+        time=1.0,
+        smem=2,
         scratch=[
-            pltpu.VMEM((blocks * n_row, vecs, tile_size), jnp.float32),
-            pltpu.VMEM((blocks * n_col, vecs, tile_size), jnp.float32),
+            pltpu.VMEM((2 * half_row, *tile), jnp.float32),
+            pltpu.VMEM((2 * half_col, *tile), jnp.float32),
         ],
     )
-    row_parts = [forward[0]] + [swap(part, "col", m) for m, part in enumerate(forward) if m]
-    for m in scatter_row[:-1]:
-        half //= 2
-        kept, sent = call(
+    forward_done = row_kept
+    for i, m in enumerate(scatter_row[:-1]):
+        half_row //= 2
+        col_kept, col_sent = call(
             fold_kernel,
-            [(half, vecs, tile_size), (half + grams, vecs, tile_size)],
-            forward[0] if m == scatter_row[-2] else wide,
-            kept,
-            sent,
-            swap(sent, "row", m),
+            [(half_row, *tile), (half_row + grams, *tile)],
+            col_kept,
+            col_sent,
+            swap(col_sent, "row", m),
+            after=[forward_done] if i == n_row.bit_length() - 3 else [],
+            time=0.1,
         )
-    got = swap(sent, "row", scatter_row[-1])
-    col_parts = [kept, got]
+    col_parts = [col_kept, swap(col_sent, "row", scatter_row[-1])]
+    for m in scatter_col[:-1]:
+        half_col //= 2
+        row_kept, row_sent = call(
+            fold_kernel,
+            [(half_col, *tile)] * 2,
+            row_kept,
+            row_sent,
+            swap(row_sent, "col", m),
+            time=0.1,
+        )
+    row_parts = [row_kept, swap(row_sent, "col", scatter_col[-1])]
 
     inverse, gram = call(
         functools.partial(factor_kernel, count, blocks),
         [(count, count), (count, LANES)],
-        row_parts[-1],
-        sent,
-        got,
+        col_sent,
+        col_parts[1],
         time=1.1,
     )
     basis_new, image_start, start = call(
@@ -375,7 +427,6 @@
         gram,
         basis_all,
         image_kept,
-        time=0.7,
     )
     image, part = call(
         functools.partial(image_kernel, scale),
@@ -383,7 +434,6 @@
         basis_new,
         *row_parts,
         *col_parts,
-        time=0.0,
     )
     parts = lax.all_to_all(part, ("row", "col"), split_axis=0, concat_axis=0, tiled=True)
     return call(

time: 40.3 us -> 37.9 us (0.940)
  starting transfers between devices: 16.2 us -> 14.2 us
  Pallas kernels: 6.77 us -> 4.96 us
  blocking collectives: 9.42 us -> 10.6 us
    ppermute x12 -> x11, starting transfers between devices: 16.2 us -> 14.2 us  [swap(): return lax.ppermute(array, axis, [(i, i ^ mask) for i in range(size)])]
    pallas_call x10 -> x11, Pallas kernels: 6.77 us -> 4.96 us  [call(): pl.pallas_call(body, out_shape=outs, in_specs=[operand] * n_after + [scal...]
    all_to_all x1, blocking collectives: 9.42 us -> 10.6 us  [local(): lax.all_to_all(part, ('row', 'col'), split_axis=0, concat_axis=0, tiled=T...]
    ppermute x12 -> x11, waiting for transfers between devices: 6.88 us -> 7.18 us  [swap(): return lax.ppermute(array, axis, [(i, i ^ mask) for i in range(size)])]
  transfers between devices with their start and end apart: 12 -> 11, of which waited for: 5 -> 6; matrix products, arithmetic and copies ran while one was open for 0% -> 0% of each run, Pallas kernels for 11% -> 7%
where the time goes in v4:
time: 37.9 us; the launch traced here: 37.7 us
  starting transfers between devices  14.2 us (37%)
  blocking collectives  10.6 us (28%)
  waiting for transfers between devices  7.18 us (19%)
  Pallas kernels  4.96 us (13%)
  between operations  0.72 us (2%)
    ppermute x11, starting transfers between devices, swap(): return lax.ppermute(array, axis, [(i, i ^ mask) for i in range(size)])  14.2 us
    all_to_all x1, blocking collectives, local(): lax.all_to_all(part, ('row', 'col'), split_axis=0, concat_axis=0, tiled=T...  10.6 us
    ppermute x11, waiting for transfers between devices, swap(): return lax.ppermute(array, axis, [(i, i ^ mask) for i in range(size)])  7.18 us
    pallas_call x11, Pallas kernels, call(): pl.pallas_call(body, out_shape=outs, in_specs=[operand] * n_after + [scal...  4.96 us
  transfers between devices with their start and end apart: 11, of which 6 were waited for; matrix products, arithmetic and copies ran while one was open for 0% of the time, Pallas kernels for 7%

profile of v4, /device:TPU:0, one launch (start us, length us, event | category | flops | bytes accessed | tf_op | source)
XLA Modules:
  0.0 37.7 jit_solution(4681120087414922412)
XLA Ops:
  0.6 1.1 %load.1 = (f32[8,4,128]{2,1,0:T(4,128)S(1)}, f32[48,1024]{1,0:T(8,128)S(1)}, f32[44,1024]{1,0:T(8,128)S(1)}, s32[24]{0:T(128)S(4)}, s32[24]{0:T(128)S(4)}) custom-call(bf16[4,1024]{1,0:T(4,128)(2,1)} %refs_0_.1, f32[44,1024]{1,0:T(8,128)} %refs_1_.1, f32[44,1024]{1,0:T(8,128)} %refs_2_.3, s32[24]{0:T(128)} %refs_3_.1, s32[24]{0:T(128)} %refs_4_.1), custom_call_target="tpu_custom_call" | custom-call | flops 1100000000 | bytes 3600000 | tf_op jit(solution)/shard_map/load/pallas_call | solution.py:290
  1.7 3.0 %collective-permute-start = (f32[8,4,128]{2,1,0:T(4,128)S(1)}, f32[8,4,128]{2,1,0:T(4,128)S(1)}, u32[]{:S(2)}, u32[]{:S(2)}) collective-permute-start(f32[8,4,128]{2,1,0:T(4,128)S(1)} %get-tuple-element.27.refs_3_.refs_0_), channel_id=1, source_target_pairs={{0,8},{4,12},{8,0},{12,4},{16,24},{20,28},{24,16},{28,20},{1,9},{5... | collective-permute-start | bytes 49160 | tf_op jit(solution)/shard_map/ppermute | solution.py:310
  4.7 0.4 gram.1.refs_3_
  5.1 3.7 %collective-permute-start.5 = (f32[20,4,128]{2,1,0:T(4,128)S(1)}, f32[20,4,128]{2,1,0:T(4,128)S(1)}, u32[]{:S(2)}, u32[]{:S(2)}) collective-permute-start(f32[20,4,128]{2,1,0:T(4,128)S(1)} %gram.1.refs_3_), channel_id=1, source_target_pairs={{0,3},{1,2},{2,1},{3,0},{4,7},{5,6},{6,5},{7,4},{8,11},{9,10},{10,... | collective-permute-start | bytes 122888 | tf_op jit(solution)/shard_map/ppermute | solution.py:310
  8.8 0.8 %collective-permute-start.3 = (f32[20,4,128]{2,1,0:T(4,128)S(1)}, f32[20,4,128]{2,1,0:T(4,128)S(1)}, u32[]{:S(2)}, u32[]{:S(2)}) collective-permute-start(f32[20,4,128]{2,1,0:T(4,128)S(1)} %gram.1.refs_3_), channel_id=1, source_target_pairs={{0,1},{1,0},{2,3},{3,2},{4,5},{5,4},{6,7},{7,6},{8,9},{9,8},{10,11... | collective-permute-start | bytes 122888 | tf_op jit(solution)/shard_map/ppermute | solution.py:310
  9.6 1.6 %collective-permute-start.1 = (f32[16,4,128]{2,1,0:T(4,128)S(1)}, f32[16,4,128]{2,1,0:T(4,128)S(1)}, u32[]{:S(2)}, u32[]{:S(2)}) collective-permute-start(f32[16,4,128]{2,1,0:T(4,128)S(1)} %pad_maximum_fusion.1), channel_id=1, source_target_pairs={{0,16},{4,20},{8,24},{12,28},{16,0},{20,4},{24,8},{28,12},{1,17},{... | collective-permute-start | bytes 98312 | tf_op jit(solution)/shard_map/ppermute | solution.py:310
  11.2 0.2 collective-permute-done.5.refs_6_
  11.4 2.3 %collective-permute-done.4.refs_5_ = f32[20,4,128]{2,1,0:T(4,128)S(1)} collective-permute-done((f32[20,4,128]{2,1,0:T(4,128)S(1)}, f32[20,4,128]{2,1,0:T(4,128)S(1)}, u32[]{:S(2)}, u32[]{:S(2)}) %collective-permute-start.4) | collective-permute-done | bytes 40992 | tf_op jit(solution)/shard_map/ppermute | solution.py:310
  13.7 0.3 backward.1
  14.1 0.6 %collective-permute-start.2 = (f32[32,4,128]{2,1,0:T(4,128)S(1)}, f32[32,4,128]{2,1,0:T(4,128)S(1)}, u32[]{:S(2)}, u32[]{:S(2)}) collective-permute-start(f32[32,4,128]{2,1,0:T(4,128)S(1)} %pad_maximum_fusion), channel_id=1, source_target_pairs={{0,4},{4,0},{8,12},{12,8},{16,20},{20,16},{24,28},{28,24},{1,5},{5... | collective-permute-start | bytes 196616 | tf_op jit(solution)/shard_map/ppermute | solution.py:310
  14.6 0.7 %collective-permute-done.6.refs_2_ = f32[44,4,128]{2,1,0:T(4,128)S(1)} collective-permute-done((f32[44,4,128]{2,1,0:T(4,128)S(1)}, f32[44,4,128]{2,1,0:T(4,128)S(1)}, u32[]{:S(2)}, u32[]{:S(2)}) %collective-permute-start.6) | collective-permute-done | bytes 90144 | tf_op jit(solution)/shard_map/ppermute | solution.py:310
  15.4 0.6 %collective-permute-start.7 = (f32[28,4,128]{2,1,0:T(4,128)S(1)}, f32[28,4,128]{2,1,0:T(4,128)S(1)}, u32[]{:S(2)}, u32[]{:S(2)}) collective-permute-start(f32[28,4,128]{2,1,0:T(4,128)S(1)} %get-tuple-element.34.refs_2_), channel_id=1, source_target_pairs={{0,8},{4,12},{8,0},{12,4},{16,24},{20,28},{24,16},{28,20},{1,9},{5... | collective-permute-start | bytes 172040 | tf_op jit(solution)/shard_map/ppermute | solution.py:310
  16.0 0.3 forward.1
  16.3 0.2 collective-permute-start.9
  16.5 3.1 %collective-permute-done.7.refs_3_ = f32[28,4,128]{2,1,0:T(4,128)S(1)} collective-permute-done((f32[28,4,128]{2,1,0:T(4,128)S(1)}, f32[28,4,128]{2,1,0:T(4,128)S(1)}, u32[]{:S(2)}, u32[]{:S(2)}) %collective-permute-start.7) | collective-permute-done | bytes 57376 | tf_op jit(solution)/shard_map/ppermute | solution.py:310
  19.6 1.6 %collective-permute-start.8 = (f32[20,4,128]{2,1,0:T(4,128)S(1)}, f32[20,4,128]{2,1,0:T(4,128)S(1)}, u32[]{:S(2)}, u32[]{:S(2)}) collective-permute-start(f32[20,4,128]{2,1,0:T(4,128)S(1)} %get-tuple-element.35.refs_0_), channel_id=1, source_target_pairs={{0,16},{4,20},{8,24},{12,28},{16,0},{20,4},{24,8},{28,12},{1,17},{... | collective-permute-start | bytes 122888 | tf_op jit(solution)/shard_map/ppermute | solution.py:310
  21.2 2.1 %collective-permute-start.10 = (f32[8,4,128]{2,1,0:T(4,128)S(1)}, f32[8,4,128]{2,1,0:T(4,128)S(1)}, u32[]{:S(2)}, u32[]{:S(2)}) collective-permute-start(f32[8,4,128]{2,1,0:T(4,128)S(1)} %get-tuple-element.42), channel_id=1, source_target_pairs={{0,2},{1,3},{2,0},{3,1},{4,6},{5,7},{6,4},{7,5},{8,10},{9,11},{10,... | collective-permute-start | bytes 49160 | tf_op jit(solution)/shard_map/ppermute | solution.py:310
  23.3 0.4 collective-permute-done.8.refs_1_.refs_4_
  23.7 1.1 %factor.1 = (f32[48,48]{1,0:T(8,128)S(1)}, f32[48,128]{1,0:T(8,128)S(1)}) custom-call(f32[20,4,128]{2,1,0:T(4,128)S(1)} %get-tuple-element.35.refs_0_, f32[20,4,128]{2,1,0:T(4,128)S(1)} %collective-permute-done.8.refs_1_.refs_4_), custom_call_target="tpu_custom_call" | custom-call | flops 1210000000 | bytes 3960000 | tf_op jit(solution)/shard_map/factor/pallas_call | solution.py:290
  24.7 0.6 %basis.1 = (f32[48,1024]{1,0:T(8,128)S(1)}, f32[48,1024]{1,0:T(8,128)S(1)}, f32[48,48]{1,0:T(8,128)S(1)}) custom-call(f32[48,48]{1,0:T(8,128)S(1)} %get-tuple-element.36.refs_0_, f32[48,128]{1,0:T(8,128)S(1)} %get-tuple-element.37.refs_1_, f32[48,1024]{1,0:T(8,128)S(1)} %get-tuple-element.29.refs_1_.refs_2_, f32[44,1024]{1,0:T(8,128)S(1)} %get-tuple-element.30.refs_2_.refs_3_), custom_call_target="tpu_custom_call" | custom-call | tf_op jit(solution)/shard_map/basis/pallas_call | solution.py:290
  25.4 0.5 %collective-permute-done.10.refs_2_ = f32[8,4,128]{2,1,0:T(4,128)S(1)} collective-permute-done((f32[8,4,128]{2,1,0:T(4,128)S(1)}, f32[8,4,128]{2,1,0:T(4,128)S(1)}, u32[]{:S(2)}, u32[]{:S(2)}) %collective-permute-start.10) | collective-permute-done | bytes 16416 | tf_op jit(solution)/shard_map/ppermute | solution.py:310
  25.9 0.2 image.1
  26.2 10.6 %all_to_all.5.refs_5_ = f32[32,4,128]{2,1,0:T(4,128)S(1)} all-to-all(f32[32,4,128]{2,1,0:T(4,128)S(1)} %get-tuple-element.46), channel_id=1, replica_groups=mesh['row'=8,'col'=4] {'row','col'}, dimensions={0} | all-to-all | bytes 131072 | tf_op jit(solution)/shard_map/all_to_all | solution.py:438
  36.8 0.9 %finish.1 = (f32[48,48]{1,0:T(8,128)}, f32[48,1024]{1,0:T(8,128)}, f32[48,1024]{1,0:T(8,128)}) custom-call(f32[48,48]{1,0:T(8,128)S(1)} %get-tuple-element.36.refs_0_, f32[48,1024]{1,0:T(8,128)S(1)} %get-tuple-element.38.refs_0_.refs_1_, f32[48,1024]{1,0:T(8,128)S(1)} %get-tuple-element.39.refs_2_, f32[4,1024]{1,0:T(4,128)S(1)} %get-tuple-element.44.refs_3_, ...), custom_call_target="tpu_custom_call" | custom-call | tf_op jit(solution)/shard_map/finish/pallas_call | solution.py:290
  (14 shorter events, 0.2 us)
Async XLA Ops:
  1.7 7.8 %collective-permute-start = (f32[8,4,128]{2,1,0:T(4,128)S(1)}, f32[8,4,128]{2,1,0:T(4,128)S(1)}, u32[]{:S(2)}, u32[]{:S(2)}) collective-permute-start(f32[8,4,128]{2,1,0:T(4,128)S(1)} %get-tuple-element.27.refs_3_.refs_0_), channel_id=1, source_target_pairs={{0,8},{4,12},{8,0},{12,4},{16,24},{20,28},{24,16},{28,20},{1,9},{5... | collective-permute-start | bytes 49160 | tf_op jit(solution)/shard_map/ppermute | solution.py:310
  4.7 8.9 %copy-start = (bf16[24,128,128]{2,1,0:T(8,128)(2,1)S(1)}, bf16[24,128,128]{2,1,0:T(8,128)(2,1)}, u32[]{:S(2)}) copy-start(bf16[24,128,128]{2,1,0:T(8,128)(2,1)} %refs_2_.5) | copy-start | bytes 2359300
  5.1 6.3 %collective-permute-start.5 = (f32[20,4,128]{2,1,0:T(4,128)S(1)}, f32[20,4,128]{2,1,0:T(4,128)S(1)}, u32[]{:S(2)}, u32[]{:S(2)}) collective-permute-start(f32[20,4,128]{2,1,0:T(4,128)S(1)} %gram.1.refs_3_), channel_id=1, source_target_pairs={{0,3},{1,2},{2,1},{3,0},{4,7},{5,6},{6,5},{7,4},{8,11},{9,10},{10,... | collective-permute-start | bytes 122888 | tf_op jit(solution)/shard_map/ppermute | solution.py:310
  8.8 4.9 %collective-permute-start.4 = (f32[20,4,128]{2,1,0:T(4,128)S(1)}, f32[20,4,128]{2,1,0:T(4,128)S(1)}, u32[]{:S(2)}, u32[]{:S(2)}) collective-permute-start(f32[20,4,128]{2,1,0:T(4,128)S(1)} %gram.1.refs_3_), channel_id=1, source_target_pairs={{0,2},{1,3},{2,0},{3,1},{4,6},{5,7},{6,4},{7,5},{8,10},{9,11},{10,... | collective-permute-start | bytes 122888 | tf_op jit(solution)/shard_map/ppermute | solution.py:310
  8.8 4.9 %collective-permute-start.3 = (f32[20,4,128]{2,1,0:T(4,128)S(1)}, f32[20,4,128]{2,1,0:T(4,128)S(1)}, u32[]{:S(2)}, u32[]{:S(2)}) collective-permute-start(f32[20,4,128]{2,1,0:T(4,128)S(1)} %gram.1.refs_3_), channel_id=1, source_target_pairs={{0,1},{1,0},{2,3},{3,2},{4,5},{5,4},{6,7},{7,6},{8,9},{9,8},{10,11... | collective-permute-start | bytes 122888 | tf_op jit(solution)/shard_map/ppermute | solution.py:310
  9.6 4.5 %collective-permute-start.1 = (f32[16,4,128]{2,1,0:T(4,128)S(1)}, f32[16,4,128]{2,1,0:T(4,128)S(1)}, u32[]{:S(2)}, u32[]{:S(2)}) collective-permute-start(f32[16,4,128]{2,1,0:T(4,128)S(1)} %pad_maximum_fusion.1), channel_id=1, source_target_pairs={{0,16},{4,20},{8,24},{12,28},{16,0},{20,4},{24,8},{28,12},{1,17},{... | collective-permute-start | bytes 98312 | tf_op jit(solution)/shard_map/ppermute | solution.py:310
  14.0 1.4 %collective-permute-start.6 = (f32[44,4,128]{2,1,0:T(4,128)S(1)}, f32[44,4,128]{2,1,0:T(4,128)S(1)}, u32[]{:S(2)}, u32[]{:S(2)}) collective-permute-start(f32[44,4,128]{2,1,0:T(4,128)S(1)} %get-tuple-element.32.refs_1_), channel_id=1, source_target_pairs={{0,4},{4,0},{8,12},{12,8},{16,20},{20,16},{24,28},{28,24},{1,5},{5... | collective-permute-start | bytes 270344 | tf_op jit(solution)/shard_map/ppermute | solution.py:310
  14.1 1.9 %collective-permute-start.2 = (f32[32,4,128]{2,1,0:T(4,128)S(1)}, f32[32,4,128]{2,1,0:T(4,128)S(1)}, u32[]{:S(2)}, u32[]{:S(2)}) collective-permute-start(f32[32,4,128]{2,1,0:T(4,128)S(1)} %pad_maximum_fusion), channel_id=1, source_target_pairs={{0,4},{4,0},{8,12},{12,8},{16,20},{20,16},{24,28},{28,24},{1,5},{5... | collective-permute-start | bytes 196616 | tf_op jit(solution)/shard_map/ppermute | solution.py:310
  15.4 4.2 %collective-permute-start.7 = (f32[28,4,128]{2,1,0:T(4,128)S(1)}, f32[28,4,128]{2,1,0:T(4,128)S(1)}, u32[]{:S(2)}, u32[]{:S(2)}) collective-permute-start(f32[28,4,128]{2,1,0:T(4,128)S(1)} %get-tuple-element.34.refs_2_), channel_id=1, source_target_pairs={{0,8},{4,12},{8,0},{12,4},{16,24},{20,28},{24,16},{28,20},{1,9},{5... | collective-permute-start | bytes 172040 | tf_op jit(solution)/shard_map/ppermute | solution.py:310
  16.3 4.9 %collective-permute-start.9 = (f32[16,4,128]{2,1,0:T(4,128)S(1)}, f32[16,4,128]{2,1,0:T(4,128)S(1)}, u32[]{:S(2)}, u32[]{:S(2)}) collective-permute-start(f32[16,4,128]{2,1,0:T(4,128)S(1)} %get-tuple-element.40.refs_1_), channel_id=1, source_target_pairs={{0,1},{1,0},{2,3},{3,2},{4,5},{5,4},{6,7},{7,6},{8,9},{9,8},{10,11... | collective-permute-start | bytes 98312 | tf_op jit(solution)/shard_map/ppermute | solution.py:310
  19.6 4.1 %collective-permute-start.8 = (f32[20,4,128]{2,1,0:T(4,128)S(1)}, f32[20,4,128]{2,1,0:T(4,128)S(1)}, u32[]{:S(2)}, u32[]{:S(2)}) collective-permute-start(f32[20,4,128]{2,1,0:T(4,128)S(1)} %get-tuple-element.35.refs_0_), channel_id=1, source_target_pairs={{0,16},{4,20},{8,24},{12,28},{16,0},{20,4},{24,8},{28,12},{1,17},{... | collective-permute-start | bytes 122888 | tf_op jit(solution)/shard_map/ppermute | solution.py:310
  21.2 4.7 %collective-permute-start.10 = (f32[8,4,128]{2,1,0:T(4,128)S(1)}, f32[8,4,128]{2,1,0:T(4,128)S(1)}, u32[]{:S(2)}, u32[]{:S(2)}) collective-permute-start(f32[8,4,128]{2,1,0:T(4,128)S(1)} %get-tuple-element.42), channel_id=1, source_target_pairs={{0,2},{1,3},{2,0},{3,1},{4,6},{5,7},{6,4},{7,5},{8,10},{9,11},{10,... | collective-permute-start | bytes 49160 | tf_op jit(solution)/shard_map/ppermute | solution.py:310

commit v5 on v4

--- a/solution.py
+++ b/solution.py
@@ -108,10 +108,16 @@
     return index >> (size.bit_length() - 1), index & (size - 1)
 
 
-def place(apart, bits):
-    if bits == bits_of(1 << len(bits)):
-        return apart
-    return sum(((apart >> (m.bit_length() - 1)) & 1) << j for j, m in enumerate(bits))
+def place(apart, masks):
+    crossed = any(m & (m - 1) for m in masks)
+    at = 0
+    for j, m in enumerate(masks):
+        bit = apart >> (m.bit_length() - 1)
+        if m == 1 and crossed:
+            for k in range(1, len(masks)):
+                bit = bit ^ (apart >> k)
+        at = at + ((bit & 1) << j)
+    return at
 
 
 def tiles_product(contract, by_rows, by_cols, n_row, blocks, scalars, tiles_ref, vecs_ref, sums_ref):
@@ -318,7 +324,7 @@
     blocks = width // tile_size
     n_row, n_col = lax.axis_size("row"), lax.axis_size("col")
     scale = 1.0 / float(width * n_row * n_col)
-    row_bits, col_bits = bits_of(n_row), bits_of(n_col)
+    row_bits, col_bits = [m | 1 for m in bits_of(n_row)], bits_of(n_col)
     gather_row = row_bits[1:] + row_bits[:1]
     scatter_row, scatter_col = row_bits, col_bits
     grams = count // vecs

time: 37.9 us -> 37.2 us (0.982)
  starting transfers between devices: 14.2 us -> 13.6 us
  waiting for transfers between devices: 7.18 us -> 6.74 us
  blocking collectives: 10.6 us -> 11 us
    ppermute x11, starting transfers between devices: 14.2 us -> 13.6 us  [swap(): return lax.ppermute(array, axis, [(i, i ^ mask) for i in range(size)])]
    ppermute x11, waiting for transfers between devices: 7.18 us -> 6.74 us  [swap(): return lax.ppermute(array, axis, [(i, i ^ mask) for i in range(size)])]
where the time goes in v5:
time: 37.2 us; the launch traced here: 37 us
  starting transfers between devices  13.6 us (37%)
  blocking collectives  11 us (30%)
  waiting for transfers between devices  6.74 us (18%)
  Pallas kernels  4.97 us (13%)
  between operations  0.71 us (2%)
    ppermute x11, starting transfers between devices, swap(): return lax.ppermute(array, axis, [(i, i ^ mask) for i in range(size)])  13.6 us
    all_to_all x1, blocking collectives, local(): lax.all_to_all(part, ('row', 'col'), split_axis=0, concat_axis=0, tiled=T...  11 us
    ppermute x11, waiting for transfers between devices, swap(): return lax.ppermute(array, axis, [(i, i ^ mask) for i in range(size)])  6.74 us
    pallas_call x11, Pallas kernels, call(): pl.pallas_call(body, out_shape=outs, in_specs=[operand] * n_after + [scal...  4.97 us
  transfers between devices with their start and end apart: 11, of which 6 were waited for; matrix products, arithmetic and copies ran while one was open for 0% of the time, Pallas kernels for 7%

profile of v5, /device:TPU:0, one launch (start us, length us, event | category | flops | bytes accessed | tf_op | source)
XLA Modules:
  0.0 37.0 jit_solution(464209344273427347)
XLA Ops:
  0.6 1.1 %load.1 = (f32[8,4,128]{2,1,0:T(4,128)S(1)}, f32[48,1024]{1,0:T(8,128)S(1)}, f32[44,1024]{1,0:T(8,128)S(1)}, s32[24]{0:T(128)S(4)}, s32[24]{0:T(128)S(4)}) custom-call(bf16[4,1024]{1,0:T(4,128)(2,1)} %refs_0_.1, f32[44,1024]{1,0:T(8,128)} %refs_1_.1, f32[44,1024]{1,0:T(8,128)} %refs_2_.3, s32[24]{0:T(128)} %refs_3_.1, s32[24]{0:T(128)} %refs_4_.1), custom_call_target="tpu_custom_call" | custom-call | flops 1100000000 | bytes 3600000 | tf_op jit(solution)/shard_map/load/pallas_call | solution.py:296
  1.7 2.4 %collective-permute-start = (f32[8,4,128]{2,1,0:T(4,128)S(1)}, f32[8,4,128]{2,1,0:T(4,128)S(1)}, u32[]{:S(2)}, u32[]{:S(2)}) collective-permute-start(f32[8,4,128]{2,1,0:T(4,128)S(1)} %get-tuple-element.27.refs_3_.refs_0_), channel_id=1, source_target_pairs={{0,12},{4,8},{8,4},{12,0},{16,28},{20,24},{24,20},{28,16},{1,13},{... | collective-permute-start | bytes 49160 | tf_op jit(solution)/shard_map/ppermute | solution.py:316
  4.2 0.4 gram.1.refs_3_
  4.6 3.7 %collective-permute-start.5 = (f32[20,4,128]{2,1,0:T(4,128)S(1)}, f32[20,4,128]{2,1,0:T(4,128)S(1)}, u32[]{:S(2)}, u32[]{:S(2)}) collective-permute-start(f32[20,4,128]{2,1,0:T(4,128)S(1)} %gram.1.refs_3_), channel_id=1, source_target_pairs={{0,3},{1,2},{2,1},{3,0},{4,7},{5,6},{6,5},{7,4},{8,11},{9,10},{10,... | collective-permute-start | bytes 122888 | tf_op jit(solution)/shard_map/ppermute | solution.py:316
  8.2 0.8 %collective-permute-start.3 = (f32[20,4,128]{2,1,0:T(4,128)S(1)}, f32[20,4,128]{2,1,0:T(4,128)S(1)}, u32[]{:S(2)}, u32[]{:S(2)}) collective-permute-start(f32[20,4,128]{2,1,0:T(4,128)S(1)} %gram.1.refs_3_), channel_id=1, source_target_pairs={{0,1},{1,0},{2,3},{3,2},{4,5},{5,4},{6,7},{7,6},{8,9},{9,8},{10,11... | collective-permute-start | bytes 122888 | tf_op jit(solution)/shard_map/ppermute | solution.py:316
  9.0 1.2 %collective-permute-start.1 = (f32[16,4,128]{2,1,0:T(4,128)S(1)}, f32[16,4,128]{2,1,0:T(4,128)S(1)}, u32[]{:S(2)}, u32[]{:S(2)}) collective-permute-start(f32[16,4,128]{2,1,0:T(4,128)S(1)} %pad_maximum_fusion.1), channel_id=1, source_target_pairs={{0,20},{4,16},{8,28},{12,24},{16,4},{20,0},{24,12},{28,8},{1,21},{... | collective-permute-start | bytes 98312 | tf_op jit(solution)/shard_map/ppermute | solution.py:316
  10.2 0.5 %collective-permute-done.5.refs_6_ = f32[20,4,128]{2,1,0:T(4,128)S(1)} collective-permute-done((f32[20,4,128]{2,1,0:T(4,128)S(1)}, f32[20,4,128]{2,1,0:T(4,128)S(1)}, u32[]{:S(2)}, u32[]{:S(2)}) %collective-permute-start.5) | collective-permute-done | bytes 40992 | tf_op jit(solution)/shard_map/ppermute | solution.py:316
  10.7 2.5 %collective-permute-done.4.refs_5_ = f32[20,4,128]{2,1,0:T(4,128)S(1)} collective-permute-done((f32[20,4,128]{2,1,0:T(4,128)S(1)}, f32[20,4,128]{2,1,0:T(4,128)S(1)}, u32[]{:S(2)}, u32[]{:S(2)}) %collective-permute-start.4) | collective-permute-done | bytes 40992 | tf_op jit(solution)/shard_map/ppermute | solution.py:316
  13.2 0.3 backward.1
  13.6 0.6 %collective-permute-start.2 = (f32[32,4,128]{2,1,0:T(4,128)S(1)}, f32[32,4,128]{2,1,0:T(4,128)S(1)}, u32[]{:S(2)}, u32[]{:S(2)}) collective-permute-start(f32[32,4,128]{2,1,0:T(4,128)S(1)} %pad_maximum_fusion), channel_id=1, source_target_pairs={{0,4},{4,0},{8,12},{12,8},{16,20},{20,16},{24,28},{28,24},{1,5},{5... | collective-permute-start | bytes 196616 | tf_op jit(solution)/shard_map/ppermute | solution.py:316
  14.1 0.7 %collective-permute-done.6.refs_2_ = f32[44,4,128]{2,1,0:T(4,128)S(1)} collective-permute-done((f32[44,4,128]{2,1,0:T(4,128)S(1)}, f32[44,4,128]{2,1,0:T(4,128)S(1)}, u32[]{:S(2)}, u32[]{:S(2)}) %collective-permute-start.6) | collective-permute-done | bytes 90144 | tf_op jit(solution)/shard_map/ppermute | solution.py:316
  14.8 0.4 %collective-permute-start.7 = (f32[28,4,128]{2,1,0:T(4,128)S(1)}, f32[28,4,128]{2,1,0:T(4,128)S(1)}, u32[]{:S(2)}, u32[]{:S(2)}) collective-permute-start(f32[28,4,128]{2,1,0:T(4,128)S(1)} %get-tuple-element.34.refs_2_), channel_id=1, source_target_pairs={{0,12},{4,8},{8,4},{12,0},{16,28},{20,24},{24,20},{28,16},{1,13},{... | collective-permute-start | bytes 172040 | tf_op jit(solution)/shard_map/ppermute | solution.py:316
  15.2 0.3 forward.1
  15.6 1.1 %collective-permute-start.9 = (f32[16,4,128]{2,1,0:T(4,128)S(1)}, f32[16,4,128]{2,1,0:T(4,128)S(1)}, u32[]{:S(2)}, u32[]{:S(2)}) collective-permute-start(f32[16,4,128]{2,1,0:T(4,128)S(1)} %get-tuple-element.40.refs_1_), channel_id=1, source_target_pairs={{0,1},{1,0},{2,3},{3,2},{4,5},{5,4},{6,7},{7,6},{8,9},{9,8},{10,11... | collective-permute-start | bytes 98312 | tf_op jit(solution)/shard_map/ppermute | solution.py:316
  16.6 2.2 %collective-permute-done.7.refs_3_ = f32[28,4,128]{2,1,0:T(4,128)S(1)} collective-permute-done((f32[28,4,128]{2,1,0:T(4,128)S(1)}, f32[28,4,128]{2,1,0:T(4,128)S(1)}, u32[]{:S(2)}, u32[]{:S(2)}) %collective-permute-start.7) | collective-permute-done | bytes 57376 | tf_op jit(solution)/shard_map/ppermute | solution.py:316
  18.8 1.3 %collective-permute-start.8 = (f32[20,4,128]{2,1,0:T(4,128)S(1)}, f32[20,4,128]{2,1,0:T(4,128)S(1)}, u32[]{:S(2)}, u32[]{:S(2)}) collective-permute-start(f32[20,4,128]{2,1,0:T(4,128)S(1)} %get-tuple-element.35.refs_0_), channel_id=1, source_target_pairs={{0,20},{4,16},{8,28},{12,24},{16,4},{20,0},{24,12},{28,8},{1,21},{... | collective-permute-start | bytes 122888 | tf_op jit(solution)/shard_map/ppermute | solution.py:316
  20.2 2.1 %collective-permute-start.10 = (f32[8,4,128]{2,1,0:T(4,128)S(1)}, f32[8,4,128]{2,1,0:T(4,128)S(1)}, u32[]{:S(2)}, u32[]{:S(2)}) collective-permute-start(f32[8,4,128]{2,1,0:T(4,128)S(1)} %get-tuple-element.42), channel_id=1, source_target_pairs={{0,2},{1,3},{2,0},{3,1},{4,6},{5,7},{6,4},{7,5},{8,10},{9,11},{10,... | collective-permute-start | bytes 49160 | tf_op jit(solution)/shard_map/ppermute | solution.py:316
  22.3 0.1 collective-permute-done.8.refs_1_.refs_4_
  22.4 1.1 %factor.1 = (f32[48,48]{1,0:T(8,128)S(1)}, f32[48,128]{1,0:T(8,128)S(1)}) custom-call(f32[20,4,128]{2,1,0:T(4,128)S(1)} %get-tuple-element.35.refs_0_, f32[20,4,128]{2,1,0:T(4,128)S(1)} %collective-permute-done.8.refs_1_.refs_4_), custom_call_target="tpu_custom_call" | custom-call | flops 1210000000 | bytes 3960000 | tf_op jit(solution)/shard_map/factor/pallas_call | solution.py:296
  23.5 0.6 %basis.1 = (f32[48,1024]{1,0:T(8,128)S(1)}, f32[48,1024]{1,0:T(8,128)S(1)}, f32[48,48]{1,0:T(8,128)S(1)}) custom-call(f32[48,48]{1,0:T(8,128)S(1)} %get-tuple-element.36.refs_0_, f32[48,128]{1,0:T(8,128)S(1)} %get-tuple-element.37.refs_1_, f32[48,1024]{1,0:T(8,128)S(1)} %get-tuple-element.29.refs_1_.refs_2_, f32[44,1024]{1,0:T(8,128)S(1)} %get-tuple-element.30.refs_2_.refs_3_), custom_call_target="tpu_custom_call" | custom-call | tf_op jit(solution)/shard_map/basis/pallas_call | solution.py:296
  24.1 0.8 %collective-permute-done.10.refs_2_ = f32[8,4,128]{2,1,0:T(4,128)S(1)} collective-permute-done((f32[8,4,128]{2,1,0:T(4,128)S(1)}, f32[8,4,128]{2,1,0:T(4,128)S(1)}, u32[]{:S(2)}, u32[]{:S(2)}) %collective-permute-start.10) | collective-permute-done | bytes 16416 | tf_op jit(solution)/shard_map/ppermute | solution.py:316
  24.9 0.2 image.1
  25.1 11.0 %all_to_all.5.refs_5_ = f32[32,4,128]{2,1,0:T(4,128)S(1)} all-to-all(f32[32,4,128]{2,1,0:T(4,128)S(1)} %get-tuple-element.46), channel_id=1, replica_groups=mesh['row'=8,'col'=4] {'row','col'}, dimensions={0} | all-to-all | bytes 131072 | tf_op jit(solution)/shard_map/all_to_all | solution.py:444
  36.1 0.9 %finish.1 = (f32[48,48]{1,0:T(8,128)}, f32[48,1024]{1,0:T(8,128)}, f32[48,1024]{1,0:T(8,128)}) custom-call(f32[48,48]{1,0:T(8,128)S(1)} %get-tuple-element.36.refs_0_, f32[48,1024]{1,0:T(8,128)S(1)} %get-tuple-element.38.refs_0_.refs_1_, f32[48,1024]{1,0:T(8,128)S(1)} %get-tuple-element.39.refs_2_, f32[4,1024]{1,0:T(4,128)S(1)} %get-tuple-element.44.refs_3_, ...), custom_call_target="tpu_custom_call" | custom-call | tf_op jit(solution)/shard_map/finish/pallas_call | solution.py:296
  (14 shorter events, 0.2 us)
Async XLA Ops:
  1.7 7.3 %collective-permute-start = (f32[8,4,128]{2,1,0:T(4,128)S(1)}, f32[8,4,128]{2,1,0:T(4,128)S(1)}, u32[]{:S(2)}, u32[]{:S(2)}) collective-permute-start(f32[8,4,128]{2,1,0:T(4,128)S(1)} %get-tuple-element.27.refs_3_.refs_0_), channel_id=1, source_target_pairs={{0,12},{4,8},{8,4},{12,0},{16,28},{20,24},{24,20},{28,16},{1,13},{... | collective-permute-start | bytes 49160 | tf_op jit(solution)/shard_map/ppermute | solution.py:316
  4.2 9.0 %copy-start = (bf16[24,128,128]{2,1,0:T(8,128)(2,1)S(1)}, bf16[24,128,128]{2,1,0:T(8,128)(2,1)}, u32[]{:S(2)}) copy-start(bf16[24,128,128]{2,1,0:T(8,128)(2,1)} %refs_2_.5) | copy-start | bytes 2359300
  4.6 6.1 %collective-permute-start.5 = (f32[20,4,128]{2,1,0:T(4,128)S(1)}, f32[20,4,128]{2,1,0:T(4,128)S(1)}, u32[]{:S(2)}, u32[]{:S(2)}) collective-permute-start(f32[20,4,128]{2,1,0:T(4,128)S(1)} %gram.1.refs_3_), channel_id=1, source_target_pairs={{0,3},{1,2},{2,1},{3,0},{4,7},{5,6},{6,5},{7,4},{8,11},{9,10},{10,... | collective-permute-start | bytes 122888 | tf_op jit(solution)/shard_map/ppermute | solution.py:316
  8.2 4.9 %collective-permute-start.4 = (f32[20,4,128]{2,1,0:T(4,128)S(1)}, f32[20,4,128]{2,1,0:T(4,128)S(1)}, u32[]{:S(2)}, u32[]{:S(2)}) collective-permute-start(f32[20,4,128]{2,1,0:T(4,128)S(1)} %gram.1.refs_3_), channel_id=1, source_target_pairs={{0,2},{1,3},{2,0},{3,1},{4,6},{5,7},{6,4},{7,5},{8,10},{9,11},{10,... | collective-permute-start | bytes 122888 | tf_op jit(solution)/shard_map/ppermute | solution.py:316
  8.2 4.9 %collective-permute-start.3 = (f32[20,4,128]{2,1,0:T(4,128)S(1)}, f32[20,4,128]{2,1,0:T(4,128)S(1)}, u32[]{:S(2)}, u32[]{:S(2)}) collective-permute-start(f32[20,4,128]{2,1,0:T(4,128)S(1)} %gram.1.refs_3_), channel_id=1, source_target_pairs={{0,1},{1,0},{2,3},{3,2},{4,5},{5,4},{6,7},{7,6},{8,9},{9,8},{10,11... | collective-permute-start | bytes 122888 | tf_op jit(solution)/shard_map/ppermute | solution.py:316
  9.0 4.5 %collective-permute-start.1 = (f32[16,4,128]{2,1,0:T(4,128)S(1)}, f32[16,4,128]{2,1,0:T(4,128)S(1)}, u32[]{:S(2)}, u32[]{:S(2)}) collective-permute-start(f32[16,4,128]{2,1,0:T(4,128)S(1)} %pad_maximum_fusion.1), channel_id=1, source_target_pairs={{0,20},{4,16},{8,28},{12,24},{16,4},{20,0},{24,12},{28,8},{1,21},{... | collective-permute-start | bytes 98312 | tf_op jit(solution)/shard_map/ppermute | solution.py:316
  13.5 1.4 %collective-permute-start.6 = (f32[44,4,128]{2,1,0:T(4,128)S(1)}, f32[44,4,128]{2,1,0:T(4,128)S(1)}, u32[]{:S(2)}, u32[]{:S(2)}) collective-permute-start(f32[44,4,128]{2,1,0:T(4,128)S(1)} %get-tuple-element.32.refs_1_), channel_id=1, source_target_pairs={{0,4},{4,0},{8,12},{12,8},{16,20},{20,16},{24,28},{28,24},{1,5},{5... | collective-permute-start | bytes 270344 | tf_op jit(solution)/shard_map/ppermute | solution.py:316
  13.6 1.6 %collective-permute-start.2 = (f32[32,4,128]{2,1,0:T(4,128)S(1)}, f32[32,4,128]{2,1,0:T(4,128)S(1)}, u32[]{:S(2)}, u32[]{:S(2)}) collective-permute-start(f32[32,4,128]{2,1,0:T(4,128)S(1)} %pad_maximum_fusion), channel_id=1, source_target_pairs={{0,4},{4,0},{8,12},{12,8},{16,20},{20,16},{24,28},{28,24},{1,5},{5... | collective-permute-start | bytes 196616 | tf_op jit(solution)/shard_map/ppermute | solution.py:316
  14.8 3.9 %collective-permute-start.7 = (f32[28,4,128]{2,1,0:T(4,128)S(1)}, f32[28,4,128]{2,1,0:T(4,128)S(1)}, u32[]{:S(2)}, u32[]{:S(2)}) collective-permute-start(f32[28,4,128]{2,1,0:T(4,128)S(1)} %get-tuple-element.34.refs_2_), channel_id=1, source_target_pairs={{0,12},{4,8},{8,4},{12,0},{16,28},{20,24},{24,20},{28,16},{1,13},{... | collective-permute-start | bytes 172040 | tf_op jit(solution)/shard_map/ppermute | solution.py:316
  15.6 4.6 %collective-permute-start.9 = (f32[16,4,128]{2,1,0:T(4,128)S(1)}, f32[16,4,128]{2,1,0:T(4,128)S(1)}, u32[]{:S(2)}, u32[]{:S(2)}) collective-permute-start(f32[16,4,128]{2,1,0:T(4,128)S(1)} %get-tuple-element.40.refs_1_), channel_id=1, source_target_pairs={{0,1},{1,0},{2,3},{3,2},{4,5},{5,4},{6,7},{7,6},{8,9},{9,8},{10,11... | collective-permute-start | bytes 98312 | tf_op jit(solution)/shard_map/ppermute | solution.py:316
  18.8 3.6 %collective-permute-start.8 = (f32[20,4,128]{2,1,0:T(4,128)S(1)}, f32[20,4,128]{2,1,0:T(4,128)S(1)}, u32[]{:S(2)}, u32[]{:S(2)}) collective-permute-start(f32[20,4,128]{2,1,0:T(4,128)S(1)} %get-tuple-element.35.refs_0_), channel_id=1, source_target_pairs={{0,20},{4,16},{8,28},{12,24},{16,4},{20,0},{24,12},{28,8},{1,21},{... | collective-permute-start | bytes 122888 | tf_op jit(solution)/shard_map/ppermute | solution.py:316
  20.2 4.7 %collective-permute-start.10 = (f32[8,4,128]{2,1,0:T(4,128)S(1)}, f32[8,4,128]{2,1,0:T(4,128)S(1)}, u32[]{:S(2)}, u32[]{:S(2)}) collective-permute-start(f32[8,4,128]{2,1,0:T(4,128)S(1)} %get-tuple-element.42), channel_id=1, source_target_pairs={{0,2},{1,3},{2,0},{3,1},{4,6},{5,7},{6,4},{7,5},{8,10},{9,11},{10,... | collective-permute-start | bytes 49160 | tf_op jit(solution)/shard_map/ppermute | solution.py:316

commit v6 on v5

--- a/solution.py
+++ b/solution.py
@@ -66,7 +66,7 @@
 
 def load_kernel(
     trial_hbm, basis_hbm, image_hbm, rows_hbm, cols_hbm,
-    wide_ref, basis_ref, image_ref, rows_ref, cols_ref, trial_vmem, basis_vmem, sems,
+    wide_ref, narrow_ref, basis_ref, image_ref, rows_ref, cols_ref, trial_vmem, basis_vmem, sems,
 ):
     copies = [
         pltpu.make_async_copy(source, target, sems.at[i])
@@ -86,22 +86,45 @@
     trial = trial_vmem[...].astype(jnp.float32)
     for b in range(wide_ref.shape[0]):
         wide_ref[b] = trial[:, b * LANES : (b + 1) * LANES]
+    by_blocks = [trial[:, b * LANES : (b + 1) * LANES] for b in range(wide_ref.shape[0])]
+    narrow_ref[...] = jnp.concatenate(by_blocks, axis=0).astype(narrow_ref.dtype)
     copies[1].wait()
     basis_ref[...] = jnp.concatenate([basis_vmem[...], trial], axis=0)
     for copy in copies[2:]:
         copy.wait()
 
 
-def gram_kernel(scale, wide_ref, basis_ref, image_ref, sent_ref):
+def gram_kernel(scale, wide_ref, narrow_ref, basis_ref, image_ref, sent_ref, again_ref):
     blocks, vecs = wide_ref.shape[:2]
     basis_all = basis_ref[...]
     images = image_ref[...]
-    unused = LANES - basis_all.shape[0] - images.shape[0]
-    filler = jnp.zeros((unused, images.shape[1]), jnp.float32)
+    count = basis_all.shape[0]
+    used = count + images.shape[0]
+    filler = jnp.zeros((LANES - used, images.shape[1]), jnp.float32)
     gram = contract_last(basis_all, jnp.concatenate([basis_all, images, filler], axis=0)) * scale
+    third, top = count // 3, count - count // 3
+    middle = (top + used) // 2
+    folded = jnp.concatenate([gram[top:, top:middle], gram[top:, middle:used]], axis=0)
+    unused = jnp.zeros((top, LANES - used - (middle - top)), jnp.float32)
+    packed = jnp.concatenate([gram[:top, :used], folded, unused], axis=1)
+    again_ref[...] = narrow_ref[...]
     sent_ref[:blocks] = wide_ref[...]
-    for i in range(sent_ref.shape[0] - blocks):
-        sent_ref[blocks + i] = gram[i * vecs : (i + 1) * vecs]
+    for i in range(top // vecs):
+        sent_ref[blocks + i] = packed[i * vecs : (i + 1) * vecs]
+
+
+def unpack(packed, count, old):
+    third, top = count // 3, count - count // 3
+    used = count + old
+    middle = (top + used) // 2
+    width = middle - top
+    parts = [
+        packed[:, top:count].T,
+        packed[:third, used : used + width],
+        packed[third:, used : used + width],
+        jnp.zeros((third, LANES - used), jnp.float32),
+    ]
+    return jnp.concatenate([packed, jnp.concatenate(parts, axis=1)], axis=0)
 
 
 def split(index, size):
@@ -165,9 +188,12 @@
     got_refs = refs[3 : 3 + n_got]
     *piece_refs, vecs_ref, sums_ref = refs[3 + n_got :]
     at = 0
+    vecs = vecs_ref.shape[1]
     for ref in got_refs:
-        vecs_ref[at : at + ref.shape[0]] = ref[...]
-        at += ref.shape[0]
+        got = ref[...].astype(jnp.float32)
+        for b in range(got.shape[0] // vecs):
+            vecs_ref[at + b] = got[b * vecs : (b + 1) * vecs]
+        at += got.shape[0] // vecs
     tiles_product(1, by_rows, by_cols, n_row, blocks, scalars, tiles_ref, vecs_ref, sums_ref)
     at = 0
     for ref in piece_refs:
@@ -183,9 +209,10 @@
         sent_next_ref[half:] = sent_ref[size:] + got_ref[size:]
 
 
-def factor_kernel(count, blocks, sent_ref, got_ref, inverse_ref, gram_ref):
+def factor_kernel(count, old, blocks, sent_ref, got_ref, inverse_ref, gram_ref):
     summed = sent_ref[blocks:] + got_ref[blocks:]
-    gram = jnp.concatenate([summed[i] for i in range(summed.shape[0])], axis=0)
+    packed = jnp.concatenate([summed[i] for i in range(summed.shape[0])], axis=0)
+    gram = unpack(packed, count, old)
     gram_ref[...] = gram
     row_id = lax.broadcasted_iota(jnp.int32, (count, LANES), 0)
     lane_id = lax.broadcasted_iota(jnp.int32, (count, LANES), 1)
@@ -245,7 +272,8 @@
     image_ref[...] = image
     vecs, count = image.shape[0], basis_new_ref.shape[0]
     part = contract_last(image, basis_new_ref[...]) * scale
-    part = jnp.concatenate([part, jnp.zeros((vecs, LANES - count), jnp.float32)], axis=1)
+    part = jnp.concatenate([part, jnp.zeros((vecs, LANES // 2 - count), jnp.float32)], axis=1)
+    part = jnp.concatenate([part[: vecs // 2], part[vecs // 2 :]], axis=1)
     part_ref[...] = jnp.broadcast_to(part[None], part_ref.shape)
 
 
@@ -265,6 +293,7 @@
     image_copy = pltpu.make_async_copy(image_new_vmem, image_new_hbm, sems.at[1])
     image_copy.start()
     total = jnp.sum(parts_ref[...], axis=0)
+    total = jnp.concatenate([total[:, : LANES // 2], total[:, LANES // 2 :]], axis=0)
     new = lax.dot_general(
         total[:, :count],
         last,
@@ -286,7 +315,7 @@
     scalars = pl.BlockSpec(memory_space=pltpu.SMEM)
     if from_hbm:
         args = [pltpu.with_memory_space_constraint(arg, pltpu.HBM) for arg in args]
-    result_specs = [scalars if hasattr(o, "dtype") else result for o in outs]
+    result_specs = [scalars if getattr(o, "dtype", None) == jnp.int32 else result for o in outs]
     outs = [o if hasattr(o, "dtype") else jax.ShapeDtypeStruct(o, jnp.float32) for o in outs]
     n_after = len(after)
 
@@ -327,13 +356,14 @@
     row_bits, col_bits = [m | 1 for m in bits_of(n_row)], bits_of(n_col)
     gather_row = row_bits[1:] + row_bits[:1]
     scatter_row, scatter_col = row_bits, col_bits
-    grams = count // vecs
+    grams = (count - count // 3) // vecs
     tile = (vecs, tile_size)
 
+    narrow_shape = jax.ShapeDtypeStruct((blocks * vecs, tile_size), trial_vectors.dtype)
     places = pltpu.SMEM(tile_rows.shape, tile_rows.dtype)
-    wide, basis_all, image_kept, rows_kept, cols_kept = call(
+    wide, narrow, basis_all, image_kept, rows_kept, cols_kept = call(
         load_kernel,
-        [(blocks, *tile), (count, width), (old, width), places, places],
+        [(blocks, *tile), narrow_shape, (count, width), (old, width), places, places],
         trial_vectors,
         basis_old,
         image_old,
@@ -347,16 +377,17 @@
             pltpu.SemaphoreType.DMA((5,)),
         ],
     )
-    (own,) = call(
+    own, again = call(
         functools.partial(gram_kernel, scale),
-        [(blocks + grams, *tile)],
+        [(blocks + grams, *tile), narrow_shape],
         wide,
+        narrow,
         basis_all,
         image_kept,
         time=0.5,
     )
     row_got = [swap(own, "col", m) for m in range(1, n_col)]
-    col_got = [wide]
+    col_got = [again]
     for m in gather_row:
         col_got.append(swap(jnp.concatenate(col_got, axis=0), "row", m))
 
@@ -420,7 +451,7 @@
     row_parts = [row_kept, swap(row_sent, "col", scatter_col[-1])]
 
     inverse, gram = call(
-        functools.partial(factor_kernel, count, blocks),
+        functools.partial(factor_kernel, count, old, blocks),
         [(count, count), (count, LANES)],
         col_sent,
         col_parts[1],
@@ -436,7 +467,7 @@
     )
     image, part = call(
         functools.partial(image_kernel, scale),
-        [(vecs, width), (n_row * n_col, vecs, LANES)],
+        [(vecs, width), (n_row * n_col, vecs // 2, LANES)],
         basis_new,
         *row_parts,
         *col_parts,

time: 37.2 us -> 37 us (level)
  starting transfers between devices: 13.6 us -> 12.8 us
  waiting for transfers between devices: 6.74 us -> 7.16 us
    ppermute x11, starting transfers between devices: 13.6 us -> 12.8 us  [swap(): return lax.ppermute(array, axis, [(i, i ^ mask) for i in range(size)])]
    ppermute x11, waiting for transfers between devices: 6.74 us -> 7.16 us  [swap(): return lax.ppermute(array, axis, [(i, i ^ mask) for i in range(size)])]
  transfers between devices with their start and end apart: 11 -> 11, of which waited for: 6 -> 5; matrix products, arithmetic and copies ran while one was open for 0% -> 0% of each run, Pallas kernels for 7% -> 7%
where the time goes in v6:
time: 37 us; the launch traced here: 36.8 us
  starting transfers between devices  12.8 us (35%)
  blocking collectives  10.8 us (29%)
  waiting for transfers between devices  7.16 us (19%)
  Pallas kernels  5.27 us (14%)
  between operations  0.77 us (2%)
    ppermute x11, starting transfers between devices, swap(): return lax.ppermute(array, axis, [(i, i ^ mask) for i in range(size)])  12.8 us
    all_to_all x1, blocking collectives, local(): lax.all_to_all(part, ('row', 'col'), split_axis=0, concat_axis=0, tiled=T...  10.8 us
    ppermute x11, waiting for transfers between devices, swap(): return lax.ppermute(array, axis, [(i, i ^ mask) for i in range(size)])  7.16 us
    pallas_call x11, Pallas kernels, call(): pl.pallas_call(body, out_shape=outs, in_specs=[operand] * n_after + [scal...  5.27 us
  transfers between devices with their start and end apart: 11, of which 5 were waited for; matrix products, arithmetic and copies ran while one was open for 0% of the time, Pallas kernels for 7%

profile of v6, /device:TPU:0, one launch (start us, length us, event | category | flops | bytes accessed | tf_op | source)
XLA Modules:
  0.0 36.8 jit_solution(17409149856951466628)
XLA Ops:
  0.6 1.1 %load.1 = (f32[8,4,128]{2,1,0:T(4,128)S(1)}, bf16[32,128]{1,0:T(8,128)(2,1)S(1)}, f32[48,1024]{1,0:T(8,128)S(1)}, f32[44,1024]{1,0:T(8,128)S(1)}, s32[24]{0:T(128)S(4)}, /*index=5*/s32[24]{0:T(128)S(4)}) custom-call(bf16[4,1024]{1,0:T(4,128)(2,1)} %refs_0_.1, f32[44,1024]{1,0:T(8,128)} %refs_1_.1, f32[44,1024]{1,0:T(8,128)} %refs_2_.3, s32[24]{0:T(128)} %refs_3_.1, ...), custom_call_target="tpu_custom_call" | custom-call | flops 1100000000 | bytes 3600000 | tf_op jit(solution)/shard_map/load/pallas_call | solution.py:325
  1.8 0.5 %gram.1 = (f32[16,4,128]{2,1,0:T(4,128)S(1)}, bf16[32,128]{1,0:T(8,128)(2,1)S(1)}) custom-call(f32[8,4,128]{2,1,0:T(4,128)S(1)} %get-tuple-element.30.refs_0_, bf16[32,128]{1,0:T(8,128)(2,1)S(1)} %get-tuple-element.31.refs_1_, f32[48,1024]{1,0:T(8,128)S(1)} %get-tuple-element.32.refs_2_, f32[44,1024]{1,0:T(8,128)S(1)} %get-tuple-element.33.refs_3_), custom_call_target="tpu_custom_call" | custom-call | flops 550000000 | bytes 1800000 | tf_op jit(solution)/shard_map/gram/pallas_call | solution.py:325
  2.2 2.4 %collective-permute-start = (bf16[32,128]{1,0:T(8,128)(2,1)S(1)}, bf16[32,128]{1,0:T(8,128)(2,1)S(1)}, u32[]{:S(2)}, u32[]{:S(2)}) collective-permute-start(bf16[32,128]{1,0:T(8,128)(2,1)S(1)} %get-tuple-element.34.refs_3_), channel_id=1, source_target_pairs={{0,12},{4,8},{8,4},{12,0},{16,28},{20,24},{24,20},{28,16},{1,13},{... | collective-permute-start | bytes 24584 | tf_op jit(solution)/shard_map/ppermute | solution.py:345
  4.6 3.6 %collective-permute-start.5 = (f32[16,4,128]{2,1,0:T(4,128)S(1)}, f32[16,4,128]{2,1,0:T(4,128)S(1)}, u32[]{:S(2)}, u32[]{:S(2)}) collective-permute-start(f32[16,4,128]{2,1,0:T(4,128)S(1)} %get-tuple-element.36.refs_3_), channel_id=1, source_target_pairs={{0,3},{1,2},{2,1},{3,0},{4,7},{5,6},{6,5},{7,4},{8,11},{9,10},{10,... | collective-permute-start | bytes 98312 | tf_op jit(solution)/shard_map/ppermute | solution.py:345
  8.2 0.8 %collective-permute-start.3 = (f32[16,4,128]{2,1,0:T(4,128)S(1)}, f32[16,4,128]{2,1,0:T(4,128)S(1)}, u32[]{:S(2)}, u32[]{:S(2)}) collective-permute-start(f32[16,4,128]{2,1,0:T(4,128)S(1)} %get-tuple-element.36.refs_3_), channel_id=1, source_target_pairs={{0,1},{1,0},{2,3},{3,2},{4,5},{5,4},{6,7},{7,6},{8,9},{9,8},{10,11... | collective-permute-start | bytes 98312 | tf_op jit(solution)/shard_map/ppermute | solution.py:345
  9.0 1.0 %collective-permute-start.1 = (bf16[64,128]{1,0:T(8,128)(2,1)S(1)}, bf16[64,128]{1,0:T(8,128)(2,1)S(1)}, u32[]{:S(2)}, u32[]{:S(2)}) collective-permute-start(bf16[64,128]{1,0:T(8,128)(2,1)S(1)} %pad_maximum_fusion.1), channel_id=1, source_target_pairs={{0,20},{4,16},{8,28},{12,24},{16,4},{20,0},{24,12},{28,8},{1,21},{... | collective-permute-start | bytes 49160 | tf_op jit(solution)/shard_map/ppermute | solution.py:345
  10.1 0.4 %collective-permute-done.5.refs_6_ = f32[16,4,128]{2,1,0:T(4,128)S(1)} collective-permute-done((f32[16,4,128]{2,1,0:T(4,128)S(1)}, f32[16,4,128]{2,1,0:T(4,128)S(1)}, u32[]{:S(2)}, u32[]{:S(2)}) %collective-permute-start.5) | collective-permute-done | bytes 32800 | tf_op jit(solution)/shard_map/ppermute | solution.py:345
  10.5 2.6 %collective-permute-done.4.refs_5_ = f32[16,4,128]{2,1,0:T(4,128)S(1)} collective-permute-done((f32[16,4,128]{2,1,0:T(4,128)S(1)}, f32[16,4,128]{2,1,0:T(4,128)S(1)}, u32[]{:S(2)}, u32[]{:S(2)}) %collective-permute-start.4) | collective-permute-done | bytes 32800 | tf_op jit(solution)/shard_map/ppermute | solution.py:345
  13.1 0.3 backward.1
  13.3 0.1 collective-permute-start.6
  13.5 0.5 %collective-permute-start.2 = (bf16[128,128]{1,0:T(8,128)(2,1)S(1)}, bf16[128,128]{1,0:T(8,128)(2,1)S(1)}, u32[]{:S(2)}, u32[]{:S(2)}) collective-permute-start(bf16[128,128]{1,0:T(8,128)(2,1)S(1)} %pad_maximum_fusion), channel_id=1, source_target_pairs={{0,4},{4,0},{8,12},{12,8},{16,20},{20,16},{24,28},{28,24},{1,5},{5... | collective-permute-start | bytes 98312 | tf_op jit(solution)/shard_map/ppermute | solution.py:345
  13.9 0.8 %collective-permute-done.6.refs_2_ = f32[40,4,128]{2,1,0:T(4,128)S(1)} collective-permute-done((f32[40,4,128]{2,1,0:T(4,128)S(1)}, f32[40,4,128]{2,1,0:T(4,128)S(1)}, u32[]{:S(2)}, u32[]{:S(2)}) %collective-permute-start.6) | collective-permute-done | bytes 81952 | tf_op jit(solution)/shard_map/ppermute | solution.py:345
  14.7 0.4 %collective-permute-start.7 = (f32[24,4,128]{2,1,0:T(4,128)S(1)}, f32[24,4,128]{2,1,0:T(4,128)S(1)}, u32[]{:S(2)}, u32[]{:S(2)}) collective-permute-start(f32[24,4,128]{2,1,0:T(4,128)S(1)} %get-tuple-element.40.refs_2_), channel_id=1, source_target_pairs={{0,12},{4,8},{8,4},{12,0},{16,28},{20,24},{24,20},{28,16},{1,13},{... | collective-permute-start | bytes 147464 | tf_op jit(solution)/shard_map/ppermute | solution.py:345
  15.2 0.3 forward.1
  15.5 0.6 %collective-permute-start.9 = (f32[16,4,128]{2,1,0:T(4,128)S(1)}, f32[16,4,128]{2,1,0:T(4,128)S(1)}, u32[]{:S(2)}, u32[]{:S(2)}) collective-permute-start(f32[16,4,128]{2,1,0:T(4,128)S(1)} %get-tuple-element.46.refs_1_), channel_id=1, source_target_pairs={{0,1},{1,0},{2,3},{3,2},{4,5},{5,4},{6,7},{7,6},{8,9},{9,8},{10,11... | collective-permute-start | bytes 98312 | tf_op jit(solution)/shard_map/ppermute | solution.py:345
  16.1 2.4 %collective-permute-done.7.refs_3_ = f32[24,4,128]{2,1,0:T(4,128)S(1)} collective-permute-done((f32[24,4,128]{2,1,0:T(4,128)S(1)}, f32[24,4,128]{2,1,0:T(4,128)S(1)}, u32[]{:S(2)}, u32[]{:S(2)}) %collective-permute-start.7) | collective-permute-done | bytes 49184 | tf_op jit(solution)/shard_map/ppermute | solution.py:345
  18.5 1.4 %collective-permute-start.8 = (f32[16,4,128]{2,1,0:T(4,128)S(1)}, f32[16,4,128]{2,1,0:T(4,128)S(1)}, u32[]{:S(2)}, u32[]{:S(2)}) collective-permute-start(f32[16,4,128]{2,1,0:T(4,128)S(1)} %get-tuple-element.41.refs_0_), channel_id=1, source_target_pairs={{0,20},{4,16},{8,28},{12,24},{16,4},{20,0},{24,12},{28,8},{1,21},{... | collective-permute-start | bytes 98312 | tf_op jit(solution)/shard_map/ppermute | solution.py:345
  19.9 2.1 %collective-permute-start.10 = (f32[8,4,128]{2,1,0:T(4,128)S(1)}, f32[8,4,128]{2,1,0:T(4,128)S(1)}, u32[]{:S(2)}, u32[]{:S(2)}) collective-permute-start(f32[8,4,128]{2,1,0:T(4,128)S(1)} %get-tuple-element.48), channel_id=1, source_target_pairs={{0,2},{1,3},{2,0},{3,1},{4,6},{5,7},{6,4},{7,5},{8,10},{9,11},{10,... | collective-permute-start | bytes 49160 | tf_op jit(solution)/shard_map/ppermute | solution.py:345
  22.0 1.2 %factor.1 = (f32[48,48]{1,0:T(8,128)S(1)}, f32[48,128]{1,0:T(8,128)S(1)}) custom-call(f32[16,4,128]{2,1,0:T(4,128)S(1)} %get-tuple-element.41.refs_0_, f32[16,4,128]{2,1,0:T(4,128)S(1)} %collective-permute-done.8.refs_1_.refs_4_), custom_call_target="tpu_custom_call" | custom-call | flops 1210000000 | bytes 3960000 | tf_op jit(solution)/shard_map/factor/pallas_call | solution.py:325
  23.1 0.6 %basis.1 = (f32[48,1024]{1,0:T(8,128)S(1)}, f32[48,1024]{1,0:T(8,128)S(1)}, f32[48,48]{1,0:T(8,128)S(1)}) custom-call(f32[48,48]{1,0:T(8,128)S(1)} %get-tuple-element.42.refs_0_, f32[48,128]{1,0:T(8,128)S(1)} %get-tuple-element.43.refs_1_, f32[48,1024]{1,0:T(8,128)S(1)} %get-tuple-element.32.refs_2_, f32[44,1024]{1,0:T(8,128)S(1)} %get-tuple-element.33.refs_3_), custom_call_target="tpu_custom_call" | custom-call | tf_op jit(solution)/shard_map/basis/pallas_call | solution.py:325
  23.8 1.0 %collective-permute-done.10.refs_2_ = f32[8,4,128]{2,1,0:T(4,128)S(1)} collective-permute-done((f32[8,4,128]{2,1,0:T(4,128)S(1)}, f32[8,4,128]{2,1,0:T(4,128)S(1)}, u32[]{:S(2)}, u32[]{:S(2)}) %collective-permute-start.10) | collective-permute-done | bytes 16416 | tf_op jit(solution)/shard_map/ppermute | solution.py:345
  24.7 0.3 image.1
  25.1 10.8 %all_to_all.5.refs_5_ = f32[32,2,128]{2,1,0:T(2,128)S(1)} all-to-all(f32[32,2,128]{2,1,0:T(2,128)S(1)} %get-tuple-element.52), channel_id=1, replica_groups=mesh['row'=8,'col'=4] {'row','col'}, dimensions={0} | all-to-all | bytes 65536 | tf_op jit(solution)/shard_map/all_to_all | solution.py:475
  35.8 1.0 %finish.1 = (f32[48,48]{1,0:T(8,128)}, f32[48,1024]{1,0:T(8,128)}, f32[48,1024]{1,0:T(8,128)}) custom-call(f32[48,48]{1,0:T(8,128)S(1)} %get-tuple-element.42.refs_0_, f32[48,1024]{1,0:T(8,128)S(1)} %get-tuple-element.44.refs_0_.refs_1_, f32[48,1024]{1,0:T(8,128)S(1)} %get-tuple-element.45.refs_2_, f32[4,1024]{1,0:T(4,128)S(1)} %get-tuple-element.50.refs_3_, ...), custom_call_target="tpu_custom_call" | custom-call | tf_op jit(solution)/shard_map/finish/pallas_call | solution.py:325
  (14 shorter events, 0.1 us)
Async XLA Ops:
  1.7 11.3 %copy-start = (bf16[24,128,128]{2,1,0:T(8,128)(2,1)S(1)}, bf16[24,128,128]{2,1,0:T(8,128)(2,1)}, u32[]{:S(2)}) copy-start(bf16[24,128,128]{2,1,0:T(8,128)(2,1)} %refs_2_.5) | copy-start | bytes 2359300
  2.2 6.8 %collective-permute-start = (bf16[32,128]{1,0:T(8,128)(2,1)S(1)}, bf16[32,128]{1,0:T(8,128)(2,1)S(1)}, u32[]{:S(2)}, u32[]{:S(2)}) collective-permute-start(bf16[32,128]{1,0:T(8,128)(2,1)S(1)} %get-tuple-element.34.refs_3_), channel_id=1, source_target_pairs={{0,12},{4,8},{8,4},{12,0},{16,28},{20,24},{24,20},{28,16},{1,13},{... | collective-permute-start | bytes 24584 | tf_op jit(solution)/shard_map/ppermute | solution.py:345
  4.6 5.8 %collective-permute-start.5 = (f32[16,4,128]{2,1,0:T(4,128)S(1)}, f32[16,4,128]{2,1,0:T(4,128)S(1)}, u32[]{:S(2)}, u32[]{:S(2)}) collective-permute-start(f32[16,4,128]{2,1,0:T(4,128)S(1)} %get-tuple-element.36.refs_3_), channel_id=1, source_target_pairs={{0,3},{1,2},{2,1},{3,0},{4,7},{5,6},{6,5},{7,4},{8,11},{9,10},{10,... | collective-permute-start | bytes 98312 | tf_op jit(solution)/shard_map/ppermute | solution.py:345
  8.2 4.8 %collective-permute-start.4 = (f32[16,4,128]{2,1,0:T(4,128)S(1)}, f32[16,4,128]{2,1,0:T(4,128)S(1)}, u32[]{:S(2)}, u32[]{:S(2)}) collective-permute-start(f32[16,4,128]{2,1,0:T(4,128)S(1)} %get-tuple-element.36.refs_3_), channel_id=1, source_target_pairs={{0,2},{1,3},{2,0},{3,1},{4,6},{5,7},{6,4},{7,5},{8,10},{9,11},{10,... | collective-permute-start | bytes 98312 | tf_op jit(solution)/shard_map/ppermute | solution.py:345
  8.2 4.8 %collective-permute-start.3 = (f32[16,4,128]{2,1,0:T(4,128)S(1)}, f32[16,4,128]{2,1,0:T(4,128)S(1)}, u32[]{:S(2)}, u32[]{:S(2)}) collective-permute-start(f32[16,4,128]{2,1,0:T(4,128)S(1)} %get-tuple-element.36.refs_3_), channel_id=1, source_target_pairs={{0,1},{1,0},{2,3},{3,2},{4,5},{5,4},{6,7},{7,6},{8,9},{9,8},{10,11... | collective-permute-start | bytes 98312 | tf_op jit(solution)/shard_map/ppermute | solution.py:345
  9.0 4.4 %collective-permute-start.1 = (bf16[64,128]{1,0:T(8,128)(2,1)S(1)}, bf16[64,128]{1,0:T(8,128)(2,1)S(1)}, u32[]{:S(2)}, u32[]{:S(2)}) collective-permute-start(bf16[64,128]{1,0:T(8,128)(2,1)S(1)} %pad_maximum_fusion.1), channel_id=1, source_target_pairs={{0,20},{4,16},{8,28},{12,24},{16,4},{20,0},{24,12},{28,8},{1,21},{... | collective-permute-start | bytes 49160 | tf_op jit(solution)/shard_map/ppermute | solution.py:345
  13.3 1.3 %collective-permute-start.6 = (f32[40,4,128]{2,1,0:T(4,128)S(1)}, f32[40,4,128]{2,1,0:T(4,128)S(1)}, u32[]{:S(2)}, u32[]{:S(2)}) collective-permute-start(f32[40,4,128]{2,1,0:T(4,128)S(1)} %get-tuple-element.38.refs_1_), channel_id=1, source_target_pairs={{0,4},{4,0},{8,12},{12,8},{16,20},{20,16},{24,28},{28,24},{1,5},{5... | collective-permute-start | bytes 245768 | tf_op jit(solution)/shard_map/ppermute | solution.py:345
  13.5 1.7 %collective-permute-start.2 = (bf16[128,128]{1,0:T(8,128)(2,1)S(1)}, bf16[128,128]{1,0:T(8,128)(2,1)S(1)}, u32[]{:S(2)}, u32[]{:S(2)}) collective-permute-start(bf16[128,128]{1,0:T(8,128)(2,1)S(1)} %pad_maximum_fusion), channel_id=1, source_target_pairs={{0,4},{4,0},{8,12},{12,8},{16,20},{20,16},{24,28},{28,24},{1,5},{5... | collective-permute-start | bytes 98312 | tf_op jit(solution)/shard_map/ppermute | solution.py:345
  14.7 3.8 %collective-permute-start.7 = (f32[24,4,128]{2,1,0:T(4,128)S(1)}, f32[24,4,128]{2,1,0:T(4,128)S(1)}, u32[]{:S(2)}, u32[]{:S(2)}) collective-permute-start(f32[24,4,128]{2,1,0:T(4,128)S(1)} %get-tuple-element.40.refs_2_), channel_id=1, source_target_pairs={{0,12},{4,8},{8,4},{12,0},{16,28},{20,24},{24,20},{28,16},{1,13},{... | collective-permute-start | bytes 147464 | tf_op jit(solution)/shard_map/ppermute | solution.py:345
  15.5 4.4 %collective-permute-start.9 = (f32[16,4,128]{2,1,0:T(4,128)S(1)}, f32[16,4,128]{2,1,0:T(4,128)S(1)}, u32[]{:S(2)}, u32[]{:S(2)}) collective-permute-start(f32[16,4,128]{2,1,0:T(4,128)S(1)} %get-tuple-element.46.refs_1_), channel_id=1, source_target_pairs={{0,1},{1,0},{2,3},{3,2},{4,5},{5,4},{6,7},{7,6},{8,9},{9,8},{10,11... | collective-permute-start | bytes 98312 | tf_op jit(solution)/shard_map/ppermute | solution.py:345
  18.5 3.5 %collective-permute-start.8 = (f32[16,4,128]{2,1,0:T(4,128)S(1)}, f32[16,4,128]{2,1,0:T(4,128)S(1)}, u32[]{:S(2)}, u32[]{:S(2)}) collective-permute-start(f32[16,4,128]{2,1,0:T(4,128)S(1)} %get-tuple-element.41.refs_0_), channel_id=1, source_target_pairs={{0,20},{4,16},{8,28},{12,24},{16,4},{20,0},{24,12},{28,8},{1,21},{... | collective-permute-start | bytes 98312 | tf_op jit(solution)/shard_map/ppermute | solution.py:345
  19.9 4.8 %collective-permute-start.10 = (f32[8,4,128]{2,1,0:T(4,128)S(1)}, f32[8,4,128]{2,1,0:T(4,128)S(1)}, u32[]{:S(2)}, u32[]{:S(2)}) collective-permute-start(f32[8,4,128]{2,1,0:T(4,128)S(1)} %get-tuple-element.48), channel_id=1, source_target_pairs={{0,2},{1,3},{2,0},{3,1},{4,6},{5,7},{6,4},{7,5},{8,10},{9,11},{10,... | collective-permute-start | bytes 49160 | tf_op jit(solution)/shard_map/ppermute | solution.py:345

commit v7 on v6

--- a/solution.py
+++ b/solution.py
@@ -236,11 +236,16 @@
             }
             for j in range(start, stop)
         }
+        ahead = spread(columns[start][first], start % SUBLANES)
         for j in range(start, stop):
             i, own = j % SUBLANES, j // SUBLANES
-            pivot = spread(columns[j][own], i)
+            pivot = ahead
             diagonal[own] = jnp.where(sublane == i, pivot, diagonal[own])
             reciprocal = 1.0 / pivot
+            if j + 1 < stop:
+                row_next, own_next = (j + 1) % SUBLANES, (j + 1) // SUBLANES
+                taken = spread(columns[j][own_next], row_next) * spread(columns[j + 1][own], i)
+                ahead = spread(columns[j + 1][own_next], row_next) - taken * reciprocal
             row = spread(work[own], i)
             entries = {k: spread(columns[k][own], i) for k in range(j + 1, stop)}
             for g in range(own, tiles):
@@ -355,7 +360,7 @@
     scale = 1.0 / float(width * n_row * n_col)
     row_bits, col_bits = [m | 1 for m in bits_of(n_row)], bits_of(n_col)
     gather_row = row_bits[1:] + row_bits[:1]
-    scatter_row, scatter_col = row_bits, col_bits
+    scatter_row, scatter_col = row_bits[:1] + row_bits[:0:-1], col_bits
     grams = (count - count // 3) // vecs
     tile = (vecs, tile_size)
 

time: 37 us -> 36.5 us (0.986)
  blocking collectives: 10.8 us -> 9.71 us
  waiting for transfers between devices: 7.16 us -> 7.83 us
    all_to_all x1, blocking collectives: 10.8 us -> 9.71 us  [local(): lax.all_to_all(part, ('row', 'col'), split_axis=0, concat_axis=0, tiled=T...]
    ppermute x11, waiting for transfers between devices: 7.16 us -> 7.83 us  [swap(): return lax.ppermute(array, axis, [(i, i ^ mask) for i in range(size)])]
  transfers between devices with their start and end apart: 11 -> 11, of which waited for: 5 -> 6; matrix products, arithmetic and copies ran while one was open for 0% -> 0% of each run, Pallas kernels for 7% -> 6%
where the time goes in v7:
time: 36.5 us; the launch traced here: 36.3 us
  starting transfers between devices  12.9 us (35%)
  blocking collectives  9.71 us (27%)
  waiting for transfers between devices  7.83 us (21%)
  Pallas kernels  5.08 us (14%)
  between operations  0.76 us (2%)
    ppermute x11, starting transfers between devices, swap(): return lax.ppermute(array, axis, [(i, i ^ mask) for i in range(size)])  12.9 us
    all_to_all x1, blocking collectives, local(): lax.all_to_all(part, ('row', 'col'), split_axis=0, concat_axis=0, tiled=T...  9.71 us
    ppermute x11, waiting for transfers between devices, swap(): return lax.ppermute(array, axis, [(i, i ^ mask) for i in range(size)])  7.83 us
    pallas_call x11, Pallas kernels, call(): pl.pallas_call(body, out_shape=outs, in_specs=[operand] * n_after + [scal...  5.08 us
  transfers between devices with their start and end apart: 11, of which 6 were waited for; matrix products, arithmetic and copies ran while one was open for 0% of the time, Pallas kernels for 6%

profile of v7, /device:TPU:0, one launch (start us, length us, event | category | flops | bytes accessed | tf_op | source)
XLA Modules:
  0.0 36.3 jit_solution(13112414794952307536)
XLA Ops:
  0.6 1.1 %load.1 = (f32[8,4,128]{2,1,0:T(4,128)S(1)}, bf16[32,128]{1,0:T(8,128)(2,1)S(1)}, f32[48,1024]{1,0:T(8,128)S(1)}, f32[44,1024]{1,0:T(8,128)S(1)}, s32[24]{0:T(128)S(4)}, /*index=5*/s32[24]{0:T(128)S(4)}) custom-call(bf16[4,1024]{1,0:T(4,128)(2,1)} %refs_0_.1, f32[44,1024]{1,0:T(8,128)} %refs_1_.1, f32[44,1024]{1,0:T(8,128)} %refs_2_.3, s32[24]{0:T(128)} %refs_3_.1, ...), custom_call_target="tpu_custom_call" | custom-call | flops 1100000000 | bytes 3600000 | tf_op jit(solution)/shard_map/load/pallas_call | solution.py:330
  1.8 0.5 %gram.1 = (f32[16,4,128]{2,1,0:T(4,128)S(1)}, bf16[32,128]{1,0:T(8,128)(2,1)S(1)}) custom-call(f32[8,4,128]{2,1,0:T(4,128)S(1)} %get-tuple-element.30.refs_0_, bf16[32,128]{1,0:T(8,128)(2,1)S(1)} %get-tuple-element.31.refs_1_, f32[48,1024]{1,0:T(8,128)S(1)} %get-tuple-element.32.refs_2_, f32[44,1024]{1,0:T(8,128)S(1)} %get-tuple-element.33.refs_3_), custom_call_target="tpu_custom_call" | custom-call | flops 550000000 | bytes 1800000 | tf_op jit(solution)/shard_map/gram/pallas_call | solution.py:330
  2.2 2.4 %collective-permute-start = (bf16[32,128]{1,0:T(8,128)(2,1)S(1)}, bf16[32,128]{1,0:T(8,128)(2,1)S(1)}, u32[]{:S(2)}, u32[]{:S(2)}) collective-permute-start(bf16[32,128]{1,0:T(8,128)(2,1)S(1)} %get-tuple-element.34.refs_3_), channel_id=1, source_target_pairs={{0,12},{4,8},{8,4},{12,0},{16,28},{20,24},{24,20},{28,16},{1,13},{... | collective-permute-start | bytes 24584 | tf_op jit(solution)/shard_map/ppermute | solution.py:350
  4.6 3.6 %collective-permute-start.5 = (f32[16,4,128]{2,1,0:T(4,128)S(1)}, f32[16,4,128]{2,1,0:T(4,128)S(1)}, u32[]{:S(2)}, u32[]{:S(2)}) collective-permute-start(f32[16,4,128]{2,1,0:T(4,128)S(1)} %get-tuple-element.36.refs_3_), channel_id=1, source_target_pairs={{0,3},{1,2},{2,1},{3,0},{4,7},{5,6},{6,5},{7,4},{8,11},{9,10},{10,... | collective-permute-start | bytes 98312 | tf_op jit(solution)/shard_map/ppermute | solution.py:350
  8.2 0.8 %collective-permute-start.3 = (f32[16,4,128]{2,1,0:T(4,128)S(1)}, f32[16,4,128]{2,1,0:T(4,128)S(1)}, u32[]{:S(2)}, u32[]{:S(2)}) collective-permute-start(f32[16,4,128]{2,1,0:T(4,128)S(1)} %get-tuple-element.36.refs_3_), channel_id=1, source_target_pairs={{0,1},{1,0},{2,3},{3,2},{4,5},{5,4},{6,7},{7,6},{8,9},{9,8},{10,11... | collective-permute-start | bytes 98312 | tf_op jit(solution)/shard_map/ppermute | solution.py:350
  9.0 1.0 %collective-permute-start.1 = (bf16[64,128]{1,0:T(8,128)(2,1)S(1)}, bf16[64,128]{1,0:T(8,128)(2,1)S(1)}, u32[]{:S(2)}, u32[]{:S(2)}) collective-permute-start(bf16[64,128]{1,0:T(8,128)(2,1)S(1)} %pad_maximum_fusion.1), channel_id=1, source_target_pairs={{0,20},{4,16},{8,28},{12,24},{16,4},{20,0},{24,12},{28,8},{1,21},{... | collective-permute-start | bytes 49160 | tf_op jit(solution)/shard_map/ppermute | solution.py:350
  10.1 0.4 %collective-permute-done.5.refs_6_ = f32[16,4,128]{2,1,0:T(4,128)S(1)} collective-permute-done((f32[16,4,128]{2,1,0:T(4,128)S(1)}, f32[16,4,128]{2,1,0:T(4,128)S(1)}, u32[]{:S(2)}, u32[]{:S(2)}) %collective-permute-start.5) | collective-permute-done | bytes 32800 | tf_op jit(solution)/shard_map/ppermute | solution.py:350
  10.5 2.6 %collective-permute-done.4.refs_5_ = f32[16,4,128]{2,1,0:T(4,128)S(1)} collective-permute-done((f32[16,4,128]{2,1,0:T(4,128)S(1)}, f32[16,4,128]{2,1,0:T(4,128)S(1)}, u32[]{:S(2)}, u32[]{:S(2)}) %collective-permute-start.4) | collective-permute-done | bytes 32800 | tf_op jit(solution)/shard_map/ppermute | solution.py:350
  13.1 0.3 backward.1
  13.5 0.5 %collective-permute-start.2 = (bf16[128,128]{1,0:T(8,128)(2,1)S(1)}, bf16[128,128]{1,0:T(8,128)(2,1)S(1)}, u32[]{:S(2)}, u32[]{:S(2)}) collective-permute-start(bf16[128,128]{1,0:T(8,128)(2,1)S(1)} %pad_maximum_fusion), channel_id=1, source_target_pairs={{0,4},{4,0},{8,12},{12,8},{16,20},{20,16},{24,28},{28,24},{1,5},{5... | collective-permute-start | bytes 98312 | tf_op jit(solution)/shard_map/ppermute | solution.py:350
  13.9 0.8 %collective-permute-done.6.refs_2_ = f32[40,4,128]{2,1,0:T(4,128)S(1)} collective-permute-done((f32[40,4,128]{2,1,0:T(4,128)S(1)}, f32[40,4,128]{2,1,0:T(4,128)S(1)}, u32[]{:S(2)}, u32[]{:S(2)}) %collective-permute-start.6) | collective-permute-done | bytes 81952 | tf_op jit(solution)/shard_map/ppermute | solution.py:350
  14.7 1.4 %collective-permute-start.7 = (f32[24,4,128]{2,1,0:T(4,128)S(1)}, f32[24,4,128]{2,1,0:T(4,128)S(1)}, u32[]{:S(2)}, u32[]{:S(2)}) collective-permute-start(f32[24,4,128]{2,1,0:T(4,128)S(1)} %get-tuple-element.40.refs_2_), channel_id=1, source_target_pairs={{0,20},{4,16},{8,28},{12,24},{16,4},{20,0},{24,12},{28,8},{1,21},{... | collective-permute-start | bytes 147464 | tf_op jit(solution)/shard_map/ppermute | solution.py:350
  16.1 0.3 forward.1
  16.4 0.6 %collective-permute-start.9 = (f32[16,4,128]{2,1,0:T(4,128)S(1)}, f32[16,4,128]{2,1,0:T(4,128)S(1)}, u32[]{:S(2)}, u32[]{:S(2)}) collective-permute-start(f32[16,4,128]{2,1,0:T(4,128)S(1)} %get-tuple-element.46.refs_1_), channel_id=1, source_target_pairs={{0,1},{1,0},{2,3},{3,2},{4,5},{5,4},{6,7},{7,6},{8,9},{9,8},{10,11... | collective-permute-start | bytes 98312 | tf_op jit(solution)/shard_map/ppermute | solution.py:350
  17.0 1.4 %collective-permute-done.7.refs_3_ = f32[24,4,128]{2,1,0:T(4,128)S(1)} collective-permute-done((f32[24,4,128]{2,1,0:T(4,128)S(1)}, f32[24,4,128]{2,1,0:T(4,128)S(1)}, u32[]{:S(2)}, u32[]{:S(2)}) %collective-permute-start.7) | collective-permute-done | bytes 49184 | tf_op jit(solution)/shard_map/ppermute | solution.py:350
  18.5 0.4 %collective-permute-start.8 = (f32[16,4,128]{2,1,0:T(4,128)S(1)}, f32[16,4,128]{2,1,0:T(4,128)S(1)}, u32[]{:S(2)}, u32[]{:S(2)}) collective-permute-start(f32[16,4,128]{2,1,0:T(4,128)S(1)} %get-tuple-element.41.refs_0_), channel_id=1, source_target_pairs={{0,12},{4,8},{8,4},{12,0},{16,28},{20,24},{24,20},{28,16},{1,13},{... | collective-permute-start | bytes 98312 | tf_op jit(solution)/shard_map/ppermute | solution.py:350
  18.9 1.5 %collective-permute-done.9.refs_2_ = f32[16,4,128]{2,1,0:T(4,128)S(1)} collective-permute-done((f32[16,4,128]{2,1,0:T(4,128)S(1)}, f32[16,4,128]{2,1,0:T(4,128)S(1)}, u32[]{:S(2)}, u32[]{:S(2)}) %collective-permute-start.9) | collective-permute-done | bytes 32800 | tf_op jit(solution)/shard_map/ppermute | solution.py:350
  20.4 2.1 %collective-permute-start.10 = (f32[8,4,128]{2,1,0:T(4,128)S(1)}, f32[8,4,128]{2,1,0:T(4,128)S(1)}, u32[]{:S(2)}, u32[]{:S(2)}) collective-permute-start(f32[8,4,128]{2,1,0:T(4,128)S(1)} %get-tuple-element.48), channel_id=1, source_target_pairs={{0,2},{1,3},{2,0},{3,1},{4,6},{5,7},{6,4},{7,5},{8,10},{9,11},{10,... | collective-permute-start | bytes 49160 | tf_op jit(solution)/shard_map/ppermute | solution.py:350
  22.5 1.0 %factor.1 = (f32[48,48]{1,0:T(8,128)S(1)}, f32[48,128]{1,0:T(8,128)S(1)}) custom-call(f32[16,4,128]{2,1,0:T(4,128)S(1)} %get-tuple-element.41.refs_0_, f32[16,4,128]{2,1,0:T(4,128)S(1)} %collective-permute-done.8.refs_1_.refs_4_), custom_call_target="tpu_custom_call" | custom-call | flops 1210000000 | bytes 3960000 | tf_op jit(solution)/shard_map/factor/pallas_call | solution.py:330
  23.5 0.6 %basis.1 = (f32[48,1024]{1,0:T(8,128)S(1)}, f32[48,1024]{1,0:T(8,128)S(1)}, f32[48,48]{1,0:T(8,128)S(1)}) custom-call(f32[48,48]{1,0:T(8,128)S(1)} %get-tuple-element.42.refs_0_, f32[48,128]{1,0:T(8,128)S(1)} %get-tuple-element.43.refs_1_, f32[48,1024]{1,0:T(8,128)S(1)} %get-tuple-element.32.refs_2_, f32[44,1024]{1,0:T(8,128)S(1)} %get-tuple-element.33.refs_3_), custom_call_target="tpu_custom_call" | custom-call | tf_op jit(solution)/shard_map/basis/pallas_call | solution.py:330
  24.1 1.1 %collective-permute-done.10.refs_2_ = f32[8,4,128]{2,1,0:T(4,128)S(1)} collective-permute-done((f32[8,4,128]{2,1,0:T(4,128)S(1)}, f32[8,4,128]{2,1,0:T(4,128)S(1)}, u32[]{:S(2)}, u32[]{:S(2)}) %collective-permute-start.10) | collective-permute-done | bytes 16416 | tf_op jit(solution)/shard_map/ppermute | solution.py:350
  25.3 0.3 image.1
  25.6 9.7 %all_to_all.5.refs_5_ = f32[32,2,128]{2,1,0:T(2,128)S(1)} all-to-all(f32[32,2,128]{2,1,0:T(2,128)S(1)} %get-tuple-element.52), channel_id=1, replica_groups=mesh['row'=8,'col'=4] {'row','col'}, dimensions={0} | all-to-all | bytes 65536 | tf_op jit(solution)/shard_map/all_to_all | solution.py:480
  35.3 1.0 %finish.1 = (f32[48,48]{1,0:T(8,128)}, f32[48,1024]{1,0:T(8,128)}, f32[48,1024]{1,0:T(8,128)}) custom-call(f32[48,48]{1,0:T(8,128)S(1)} %get-tuple-element.42.refs_0_, f32[48,1024]{1,0:T(8,128)S(1)} %get-tuple-element.44.refs_0_.refs_1_, f32[48,1024]{1,0:T(8,128)S(1)} %get-tuple-element.45.refs_2_, f32[4,1024]{1,0:T(4,128)S(1)} %get-tuple-element.50.refs_3_, ...), custom_call_target="tpu_custom_call" | custom-call | tf_op jit(solution)/shard_map/finish/pallas_call | solution.py:330
  (14 shorter events, 0.1 us)
Async XLA Ops:
  1.7 11.3 %copy-start = (bf16[24,128,128]{2,1,0:T(8,128)(2,1)S(1)}, bf16[24,128,128]{2,1,0:T(8,128)(2,1)}, u32[]{:S(2)}) copy-start(bf16[24,128,128]{2,1,0:T(8,128)(2,1)} %refs_2_.5) | copy-start | bytes 2359300
  2.2 6.8 %collective-permute-start = (bf16[32,128]{1,0:T(8,128)(2,1)S(1)}, bf16[32,128]{1,0:T(8,128)(2,1)S(1)}, u32[]{:S(2)}, u32[]{:S(2)}) collective-permute-start(bf16[32,128]{1,0:T(8,128)(2,1)S(1)} %get-tuple-element.34.refs_3_), channel_id=1, source_target_pairs={{0,12},{4,8},{8,4},{12,0},{16,28},{20,24},{24,20},{28,16},{1,13},{... | collective-permute-start | bytes 24584 | tf_op jit(solution)/shard_map/ppermute | solution.py:350
  4.6 5.8 %collective-permute-start.5 = (f32[16,4,128]{2,1,0:T(4,128)S(1)}, f32[16,4,128]{2,1,0:T(4,128)S(1)}, u32[]{:S(2)}, u32[]{:S(2)}) collective-permute-start(f32[16,4,128]{2,1,0:T(4,128)S(1)} %get-tuple-element.36.refs_3_), channel_id=1, source_target_pairs={{0,3},{1,2},{2,1},{3,0},{4,7},{5,6},{6,5},{7,4},{8,11},{9,10},{10,... | collective-permute-start | bytes 98312 | tf_op jit(solution)/shard_map/ppermute | solution.py:350
  8.2 4.8 %collective-permute-start.4 = (f32[16,4,128]{2,1,0:T(4,128)S(1)}, f32[16,4,128]{2,1,0:T(4,128)S(1)}, u32[]{:S(2)}, u32[]{:S(2)}) collective-permute-start(f32[16,4,128]{2,1,0:T(4,128)S(1)} %get-tuple-element.36.refs_3_), channel_id=1, source_target_pairs={{0,2},{1,3},{2,0},{3,1},{4,6},{5,7},{6,4},{7,5},{8,10},{9,11},{10,... | collective-permute-start | bytes 98312 | tf_op jit(solution)/shard_map/ppermute | solution.py:350
  8.2 4.8 %collective-permute-start.3 = (f32[16,4,128]{2,1,0:T(4,128)S(1)}, f32[16,4,128]{2,1,0:T(4,128)S(1)}, u32[]{:S(2)}, u32[]{:S(2)}) collective-permute-start(f32[16,4,128]{2,1,0:T(4,128)S(1)} %get-tuple-element.36.refs_3_), channel_id=1, source_target_pairs={{0,1},{1,0},{2,3},{3,2},{4,5},{5,4},{6,7},{7,6},{8,9},{9,8},{10,11... | collective-permute-start | bytes 98312 | tf_op jit(solution)/shard_map/ppermute | solution.py:350
  9.0 4.4 %collective-permute-start.1 = (bf16[64,128]{1,0:T(8,128)(2,1)S(1)}, bf16[64,128]{1,0:T(8,128)(2,1)S(1)}, u32[]{:S(2)}, u32[]{:S(2)}) collective-permute-start(bf16[64,128]{1,0:T(8,128)(2,1)S(1)} %pad_maximum_fusion.1), channel_id=1, source_target_pairs={{0,20},{4,16},{8,28},{12,24},{16,4},{20,0},{24,12},{28,8},{1,21},{... | collective-permute-start | bytes 49160 | tf_op jit(solution)/shard_map/ppermute | solution.py:350
  13.3 1.3 %collective-permute-start.6 = (f32[40,4,128]{2,1,0:T(4,128)S(1)}, f32[40,4,128]{2,1,0:T(4,128)S(1)}, u32[]{:S(2)}, u32[]{:S(2)}) collective-permute-start(f32[40,4,128]{2,1,0:T(4,128)S(1)} %get-tuple-element.38.refs_1_), channel_id=1, source_target_pairs={{0,4},{4,0},{8,12},{12,8},{16,20},{20,16},{24,28},{28,24},{1,5},{5... | collective-permute-start | bytes 245768 | tf_op jit(solution)/shard_map/ppermute | solution.py:350
  13.5 2.6 %collective-permute-start.2 = (bf16[128,128]{1,0:T(8,128)(2,1)S(1)}, bf16[128,128]{1,0:T(8,128)(2,1)S(1)}, u32[]{:S(2)}, u32[]{:S(2)}) collective-permute-start(bf16[128,128]{1,0:T(8,128)(2,1)S(1)} %pad_maximum_fusion), channel_id=1, source_target_pairs={{0,4},{4,0},{8,12},{12,8},{16,20},{20,16},{24,28},{28,24},{1,5},{5... | collective-permute-start | bytes 98312 | tf_op jit(solution)/shard_map/ppermute | solution.py:350
  14.7 3.8 %collective-permute-start.7 = (f32[24,4,128]{2,1,0:T(4,128)S(1)}, f32[24,4,128]{2,1,0:T(4,128)S(1)}, u32[]{:S(2)}, u32[]{:S(2)}) collective-permute-start(f32[24,4,128]{2,1,0:T(4,128)S(1)} %get-tuple-element.40.refs_2_), channel_id=1, source_target_pairs={{0,20},{4,16},{8,28},{12,24},{16,4},{20,0},{24,12},{28,8},{1,21},{... | collective-permute-start | bytes 147464 | tf_op jit(solution)/shard_map/ppermute | solution.py:350
  16.4 4.0 %collective-permute-start.9 = (f32[16,4,128]{2,1,0:T(4,128)S(1)}, f32[16,4,128]{2,1,0:T(4,128)S(1)}, u32[]{:S(2)}, u32[]{:S(2)}) collective-permute-start(f32[16,4,128]{2,1,0:T(4,128)S(1)} %get-tuple-element.46.refs_1_), channel_id=1, source_target_pairs={{0,1},{1,0},{2,3},{3,2},{4,5},{5,4},{6,7},{7,6},{8,9},{9,8},{10,11... | collective-permute-start | bytes 98312 | tf_op jit(solution)/shard_map/ppermute | solution.py:350
  18.5 4.0 %collective-permute-start.8 = (f32[16,4,128]{2,1,0:T(4,128)S(1)}, f32[16,4,128]{2,1,0:T(4,128)S(1)}, u32[]{:S(2)}, u32[]{:S(2)}) collective-permute-start(f32[16,4,128]{2,1,0:T(4,128)S(1)} %get-tuple-element.41.refs_0_), channel_id=1, source_target_pairs={{0,12},{4,8},{8,4},{12,0},{16,28},{20,24},{24,20},{28,16},{1,13},{... | collective-permute-start | bytes 98312 | tf_op jit(solution)/shard_map/ppermute | solution.py:350
  20.4 4.9 %collective-permute-start.10 = (f32[8,4,128]{2,1,0:T(4,128)S(1)}, f32[8,4,128]{2,1,0:T(4,128)S(1)}, u32[]{:S(2)}, u32[]{:S(2)}) collective-permute-start(f32[8,4,128]{2,1,0:T(4,128)S(1)} %get-tuple-element.48), channel_id=1, source_target_pairs={{0,2},{1,3},{2,0},{3,1},{4,6},{5,7},{6,4},{7,5},{8,10},{9,11},{10,... | collective-permute-start | bytes 49160 | tf_op jit(solution)/shard_map/ppermute | solution.py:350
